TPU v7x, 512 devices: a whole 4x4x16 slice. The times are simulated.
512 devices in a mesh: dp: 4 (over y_hi, core), rep: 4 (over x), blk: 32 (over z, y_lo).
Axes of the slice: x: 4, y: 4 (y_hi: 2, y_lo: 2; y = y_hi * 2 + y_lo), z: 16, core: 2. Of those that a mesh axis runs over, the one named last changes fastest.
Arguments:
- features: bfloat16 [32768, 512], P(('dp', 'blk')), parts along dimension 0, may hold values from -6 to 6
- pre_act: bfloat16 [32768, 512], P(('dp', 'blk')), parts along dimension 0, may hold values from -6 to 6
- upstream: bfloat16 [32768, 512], P(('dp', 'blk')), parts along dimension 0, may hold values from -6 to 6
- weight: bfloat16 [512, 512], replicated, may hold values from -0.25 to 0.25
- tile_values: bfloat16 [128, 32, 6, 128, 128], P(('dp', 'blk'), 'rep'), parts along dimension 0, may hold values from -0.09375 to 0.09375
- tile_rows: int32 [128, 32, 6], P(('dp', 'blk'), 'rep'), parts along dimension 0, may hold values from 0 to 1
- tile_cols: int32 [128, 32, 6], P(('dp', 'blk'), 'rep'), parts along dimension 0, may hold values from 0 to 1
- tile_count: int32 [128, 32], P(('dp', 'blk'), 'rep'), parts along dimension 0, may hold values from 0 to 6, as said below
Outputs:
- grad_feat: bfloat16 [32768, 512], P(('dp', 'blk')), parts along dimension 0
- grad_weight: float32 [2048, 512], P(('dp', 'blk')), parts along dimension 0
There are 4 independent parts, one for each index of `dp`. A program takes and returns all parts, laid end to end along the dimension named above; an argument that names none is the same for every part. Nothing has to cross between parts.
Inputs may be any that keep to these rules, and one draw needn't show every extreme that they name: `tile_rows`: local tile row block of the cycle position. `tile_cols`: local tile column block of the column owner. The first tile_count[b,k] slots of step k are live and the rest are ignored; every cycle position has a step with all 6 slots live.
All inputs are finite; a program needn't handle non-finite values.
Results may differ from a plain program's by a relative error of at most 0.0049.
Values may be sent and summed in bfloat16 or wider, within the bound.
No kernel may reach another device: no remote copies, remote signals or barrier semaphores. Data moves between devices by JAX's collectives and lax.ppermute only.
A program may use at most 64 MiB of HBM per device.

v0:
```python
import jax
import jax.numpy as jnp
from jax import lax
from jax.sharding import PartitionSpec as P


def passed_along(value, axis, steps):
    count = lax.axis_size(axis)
    pairs = [(source, (source + steps) % count) for source in range(count)]
    return lax.ppermute(value, axis, pairs)


def place_tiles(tile_vals, take_index, put_index, live_count, source, flipped):
    blocks = source.shape[0]
    tile_size = source.shape[1]
    feat_width = source.shape[2]
    slot_ids = lax.iota(jnp.int32, tile_vals.shape[0])
    live_mask = (slot_ids < live_count).astype(jnp.float32)
    block_ids = lax.iota(jnp.int32, blocks)
    if flipped:
        first_index, second_index = (take_index, put_index)
    else:
        first_index, second_index = (put_index, take_index)
    first_hot = (first_index[None, :] == block_ids[:, None]).astype(jnp.float32) * live_mask[
        None, :
    ]
    second_hot = (second_index[None, :] == block_ids[:, None]).astype(jnp.float32)
    operator = jnp.einsum(
        "iq,jq,qab->iajb",
        first_hot,
        second_hot,
        tile_vals.astype(jnp.float32),
        precision=lax.Precision.HIGHEST,
    )
    operator = operator.reshape(blocks * tile_size, blocks * tile_size)
    flat_source = source.reshape(blocks * tile_size, feat_width).astype(jnp.float32)
    contract = 0 if flipped else 1
    result = lax.dot_general(
        operator,
        flat_source,
        (((contract,), (0,)), ((), ())),
        precision=lax.Precision.HIGHEST,
        preferred_element_type=jnp.float32,
    )
    return result.reshape(blocks, tile_size, feat_width)


def shards(features, pre_act, upstream, weight, tile_values, tile_rows, tile_cols, tile_count):
    cycle_size = lax.axis_size("blk")
    rep_count = lax.axis_size("rep")
    rep_id = lax.axis_index("rep")
    step_count = tile_values.shape[1]
    tile_size = tile_values.shape[3]
    row_count, feat_width = features.shape
    blocks = row_count // tile_size
    loss_scale = (row_count * cycle_size) ** (-0.5)
    grad_out = jnp.where(pre_act > 0, upstream, jnp.zeros_like(upstream))
    back_grad = jnp.dot(grad_out, weight, preferred_element_type=jnp.float32).astype(jnp.bfloat16)
    back_blocks = back_grad.reshape(blocks, tile_size, feat_width)
    current = features
    for bit_index in range((rep_count - 1).bit_length()):
        offset = (step_count << bit_index) % cycle_size
        shifted = passed_along(current, "blk", offset)
        current = jnp.where((rep_id >> bit_index) % 2 == 1, shifted, current)
    aggregate = jnp.zeros((blocks, tile_size, feat_width), jnp.float32)
    carried = jnp.zeros((blocks, tile_size, feat_width), jnp.float32)
    for turn_index in range(step_count):
        aggregate = aggregate + place_tiles(
            tile_values[0, turn_index],
            tile_cols[0, turn_index],
            tile_rows[0, turn_index],
            tile_count[0, turn_index],
            current.reshape(blocks, tile_size, feat_width),
            False,
        )
        carried = carried + place_tiles(
            tile_values[0, turn_index],
            tile_rows[0, turn_index],
            tile_cols[0, turn_index],
            tile_count[0, turn_index],
            back_blocks,
            True,
        )
        if turn_index + 1 < step_count:
            current = passed_along(current, "blk", 1)
            carried = passed_along(carried, "blk", 1)
    tail_offset = (1 - step_count) % cycle_size
    carried = passed_along(carried, "blk", tail_offset)
    for bit_index in range((rep_count - 1).bit_length()):
        offset = -(step_count << bit_index) % cycle_size
        shifted = passed_along(carried, "blk", offset)
        carried = jnp.where((rep_id >> bit_index) % 2 == 1, shifted, carried)
    feat_grad = lax.psum(carried.reshape(row_count, feat_width), "rep").astype(jnp.bfloat16)
    aggregate_rows = aggregate.reshape(row_count, feat_width)
    own_aggregate = lax.psum(aggregate_rows, "rep").astype(jnp.bfloat16)
    grad_weight = lax.psum_scatter(
        lax.dot_general(
            grad_out, own_aggregate, (((0,), (0,)), ((), ())), preferred_element_type=jnp.float32
        ),
        "blk",
        scatter_dimension=0,
        tiled=True,
    )
    return (feat_grad, grad_weight * loss_scale)


def solution(mesh):
    return jax.shard_map(
        shards,
        mesh=mesh,
        in_specs=(
            P(("dp", "blk"), None),
            P(("dp", "blk"), None),
            P(("dp", "blk"), None),
            P(),
            P(("dp", "blk"), "rep", None, None, None),
            P(("dp", "blk"), "rep", None),
            P(("dp", "blk"), "rep", None),
            P(("dp", "blk"), "rep"),
        ),
        out_specs=(P(("dp", "blk"), None), P(("dp", "blk"), None)),
        check_vma=False,
    )
```

profile of v0, /device:TPU:24, one launch (start us, length us, event | category | flops | bytes accessed | tf_op | source)
XLA Modules:
  0.0 510.3 jit_solution(12940350921053950105)
XLA Ops:
  7.3 2.3 fusion.62
  11.0 1.0 slice_reduce_fusion
  12.6 1.0 slice_reduce_fusion.1
  14.8 1.2 fusion.64
  16.0 4.0 collective-permute-start
  20.0 9.1 %collective-permute-start.10 = (bf16[256,512]{1,0:T(8,128)(2,1)}, bf16[256,512]{1,0:T(8,128)(2,1)}, u32[]{:S(2)}, u32[]{:S(2)}) collective-permute-start(bf16[256,512]{1,0:T(8,128)(2,1)} %param.8), channel_id=1, source_target_pairs={{0,8},{1,9},{2,10},{3,11},{4,12},{5,13},{6,14},{7,15},{8,16},{9,17... | collective-permute-start | bytes 786440 | tf_op jit(solution)/shard_map/ppermute | solution.py:10
  33.5 2.2 convolution_add_fusion.7
  35.8 4.4 collective-permute-start.1
  41.9 24.4 %collective-permute-done.1 = f32[2,128,512]{2,1,0:T(8,128)} collective-permute-done((f32[2,128,512]{2,1,0:T(8,128)}, f32[2,128,512]{2,1,0:T(8,128)}, u32[]{:S(2)}, u32[]{:S(2)}) %collective-permute-start.1) | collective-permute-done | bytes 524320 | tf_op jit(solution)/shard_map/ppermute | solution.py:10
  66.3 1.9 add.60
  68.2 5.3 %collective-permute-start.2 = (f32[2,128,512]{2,1,0:T(8,128)}, f32[2,128,512]{2,1,0:T(8,128)}, u32[]{:S(2)}, u32[]{:S(2)}) collective-permute-start(f32[2,128,512]{2,1,0:T(8,128)} %add.60), channel_id=1, source_target_pairs={{0,1},{1,2},{2,3},{3,4},{4,5},{5,6},{6,7},{7,8},{8,9},{9,10},{10,1... | collective-permute-start | bytes 1572872 | tf_op jit(solution)/shard_map/ppermute | solution.py:10
  75.3 1.2 fusion.67
  76.4 13.8 %collective-permute-done.2 = f32[2,128,512]{2,1,0:T(8,128)} collective-permute-done((f32[2,128,512]{2,1,0:T(8,128)}, f32[2,128,512]{2,1,0:T(8,128)}, u32[]{:S(2)}, u32[]{:S(2)}) %collective-permute-start.2) | collective-permute-done | bytes 524320 | tf_op jit(solution)/shard_map/ppermute | solution.py:10
  90.3 1.9 add.61
  92.2 1.9 collective-permute-start.3
  95.0 0.8 copy.79
  95.9 1.4 fusion.68
  97.3 11.4 %collective-permute-done.3 = f32[2,128,512]{2,1,0:T(8,128)} collective-permute-done((f32[2,128,512]{2,1,0:T(8,128)}, f32[2,128,512]{2,1,0:T(8,128)}, u32[]{:S(2)}, u32[]{:S(2)}) %collective-permute-start.3) | collective-permute-done | bytes 524320 | tf_op jit(solution)/shard_map/ppermute | solution.py:10
  108.7 2.1 add.62
  110.8 1.9 collective-permute-start.4
  112.7 0.7 broadcast_select_fusion
  113.5 9.3 %collective-permute-start.11 = (bf16[256,512]{1,0:T(8,128)(2,1)}, bf16[256,512]{1,0:T(8,128)(2,1)}, u32[]{:S(2)}, u32[]{:S(2)}) collective-permute-start(bf16[256,512]{1,0:T(8,128)(2,1)} %broadcast_select_fusion), channel_id=1, source_target_pairs={{0,16},{1,17},{2,18},{3,19},{4,20},{5,21},{6,22},{7,23},{8,24},{9,... | collective-permute-start | bytes 786440 | tf_op jit(solution)/shard_map/ppermute | solution.py:10
  123.6 0.8 copy.80
  124.4 6.4 %collective-permute-done.4 = f32[2,128,512]{2,1,0:T(8,128)} collective-permute-done((f32[2,128,512]{2,1,0:T(8,128)}, f32[2,128,512]{2,1,0:T(8,128)}, u32[]{:S(2)}, u32[]{:S(2)}) %collective-permute-start.4) | collective-permute-done | bytes 524320 | tf_op jit(solution)/shard_map/ppermute | solution.py:10
  130.8 1.9 add.63
  132.7 5.8 %collective-permute-start.5 = (f32[2,128,512]{2,1,0:T(8,128)}, f32[2,128,512]{2,1,0:T(8,128)}, u32[]{:S(2)}, u32[]{:S(2)}) collective-permute-start(f32[2,128,512]{2,1,0:T(8,128)} %add.63), channel_id=1, source_target_pairs={{0,1},{1,2},{2,3},{3,4},{4,5},{5,6},{6,7},{7,8},{8,9},{9,10},{10,1... | collective-permute-start | bytes 1572872 | tf_op jit(solution)/shard_map/ppermute | solution.py:10
  138.9 16.8 %collective-permute-done.11 = bf16[256,512]{1,0:T(8,128)(2,1)} collective-permute-done((bf16[256,512]{1,0:T(8,128)(2,1)}, bf16[256,512]{1,0:T(8,128)(2,1)}, u32[]{:S(2)}, u32[]{:S(2)}) %collective-permute-start.11) | collective-permute-done | bytes 262176 | tf_op jit(solution)/shard_map/ppermute | solution.py:10
  155.8 1.7 broadcast_select_fusion.1
  157.5 2.1 collective-permute-start.12
  159.5 1.4 convolution_bitcast_fusion
  161.2 0.7 copy.122
  161.9 1.8 copy.81
  163.7 2.0 add.64
  165.6 1.9 collective-permute-start.6
  168.1 0.8 copy.42
  168.9 0.9 copy.46
  169.8 0.8 copy.48
  170.7 0.9 copy.50
  171.5 0.9 copy.52
  172.4 0.8 copy.54
  173.4 1.9 collective-permute-start.13
  175.3 1.4 fusion.7
  176.7 1.4 convolution_add_fusion.6
  178.1 5.2 %collective-permute-done.13 = bf16[256,512]{1,0:T(8,128)(2,1)S(1)} collective-permute-done((bf16[256,512]{1,0:T(8,128)(2,1)}, bf16[256,512]{1,0:T(8,128)(2,1)S(1)}, u32[]{:S(2)}, u32[]{:S(2)}) %collective-permute-start.13) | collective-permute-done | bytes 262176 | tf_op jit(solution)/shard_map/ppermute | solution.py:10
  183.4 4.3 collective-permute-start.14
  187.7 1.1 add.65
  188.9 2.3 collective-permute-start.7
  191.6 5.4 %collective-permute-done.14 = bf16[256,512]{1,0:T(8,128)(2,1)S(1)} collective-permute-done((bf16[256,512]{1,0:T(8,128)(2,1)S(1)}, bf16[256,512]{1,0:T(8,128)(2,1)S(1)}, u32[]{:S(2)}, u32[]{:S(2)}) %collective-permute-start.14) | collective-permute-done | bytes 262176 | tf_op jit(solution)/shard_map/ppermute | solution.py:10
  197.0 7.0 %collective-permute-start.15 = (bf16[256,512]{1,0:T(8,128)(2,1)S(1)}, bf16[256,512]{1,0:T(8,128)(2,1)S(1)}, u32[]{:S(2)}, u32[]{:S(2)}) collective-permute-start(bf16[256,512]{1,0:T(8,128)(2,1)S(1)} %collective-permute-done.14), channel_id=1, source_target_pairs={{0,1},{1,2},{2,3},{3,4},{4,5},{5,6},{6,7},{7,8},{8,9},{9,10},{10,1... | collective-permute-start | bytes 786440 | tf_op jit(solution)/shard_map/ppermute | solution.py:10
  204.5 7.9 %collective-permute-done.15 = bf16[256,512]{1,0:T(8,128)(2,1)S(1)} collective-permute-done((bf16[256,512]{1,0:T(8,128)(2,1)S(1)}, bf16[256,512]{1,0:T(8,128)(2,1)S(1)}, u32[]{:S(2)}, u32[]{:S(2)}) %collective-permute-start.15) | collective-permute-done | bytes 262176 | tf_op jit(solution)/shard_map/ppermute | solution.py:10
  212.4 5.7 %collective-permute-start.16 = (bf16[256,512]{1,0:T(8,128)(2,1)S(1)}, bf16[256,512]{1,0:T(8,128)(2,1)S(1)}, u32[]{:S(2)}, u32[]{:S(2)}) collective-permute-start(bf16[256,512]{1,0:T(8,128)(2,1)S(1)} %collective-permute-done.15), channel_id=1, source_target_pairs={{0,1},{1,2},{2,3},{3,4},{4,5},{5,6},{6,7},{7,8},{8,9},{9,10},{10,1... | collective-permute-start | bytes 786440 | tf_op jit(solution)/shard_map/ppermute | solution.py:10
  218.0 6.4 %collective-permute-done.7 = f32[2,128,512]{2,1,0:T(8,128)S(1)} collective-permute-done((f32[2,128,512]{2,1,0:T(8,128)S(1)}, f32[2,128,512]{2,1,0:T(8,128)S(1)}, u32[]{:S(2)}, u32[]{:S(2)}) %collective-permute-start.7) | collective-permute-done | bytes 524320 | tf_op jit(solution)/shard_map/ppermute | solution.py:10
  224.5 1.9 collective-permute-start.8
  226.8 3.4 collective-permute-start.17
  230.7 5.5 %collective-permute-done.17 = bf16[256,512]{1,0:T(8,128)(2,1)S(1)} collective-permute-done((bf16[256,512]{1,0:T(8,128)(2,1)S(1)}, bf16[256,512]{1,0:T(8,128)(2,1)S(1)}, u32[]{:S(2)}, u32[]{:S(2)}) %collective-permute-start.17) | collective-permute-done | bytes 262176 | tf_op jit(solution)/shard_map/ppermute | solution.py:10
  236.2 3.2 collective-permute-start.18
  239.4 6.9 %collective-permute-done.8 = f32[2,128,512]{2,1,0:T(8,128)S(1)} collective-permute-done((f32[2,128,512]{2,1,0:T(8,128)S(1)}, f32[2,128,512]{2,1,0:T(8,128)S(1)}, u32[]{:S(2)}, u32[]{:S(2)}) %collective-permute-start.8) | collective-permute-done | bytes 524320 | tf_op jit(solution)/shard_map/ppermute | solution.py:10
  246.3 8.8 %collective-permute-start.9 = (f32[2,128,512]{2,1,0:T(8,128)S(1)}, f32[2,128,512]{2,1,0:T(8,128)S(1)}, u32[]{:S(2)}, u32[]{:S(2)}) collective-permute-start(f32[2,128,512]{2,1,0:T(8,128)S(1)} %broadcast_select_fusion.2), channel_id=1, source_target_pairs={{0,16},{1,17},{2,18},{3,19},{4,20},{5,21},{6,22},{7,23},{8,24},{9,... | collective-permute-start | bytes 1572872 | tf_op jit(solution)/shard_map/ppermute | solution.py:10
  255.6 7.2 %collective-permute-done.18 = bf16[256,512]{1,0:T(8,128)(2,1)S(1)} collective-permute-done((bf16[256,512]{1,0:T(8,128)(2,1)S(1)}, bf16[256,512]{1,0:T(8,128)(2,1)S(1)}, u32[]{:S(2)}, u32[]{:S(2)}) %collective-permute-start.18) | collective-permute-done | bytes 262176 | tf_op jit(solution)/shard_map/ppermute | solution.py:10
  263.2 19.0 %collective-permute-done.9 = f32[2,128,512]{2,1,0:T(8,128)S(1)} collective-permute-done((f32[2,128,512]{2,1,0:T(8,128)S(1)}, f32[2,128,512]{2,1,0:T(8,128)S(1)}, u32[]{:S(2)}, u32[]{:S(2)}) %collective-permute-start.9) | collective-permute-done | bytes 524320 | tf_op jit(solution)/shard_map/ppermute | solution.py:10
  282.3 45.0 %all-reduce.2 = (bf16[256,512]{1,0:T(8,128)(2,1)}, bf16[256,512]{1,0:T(8,128)(2,1)S(1)}) all-reduce(f32[256,512]{1,0:T(8,128)S(1)} %bitcast.287, f32[256,512]{1,0:T(8,128)S(1)} %bitcast.286), channel_id=1, replica_groups=mesh['dp'=4,'rep'=4,'blk'=32] {'rep'}, use_global_device_ids=true, to_apply=%region_0.1 | all-reduce | flops 262144 | bytes 1572864 | tf_op jit(solution)/shard_map/psum | solution.py:93
  327.3 1.3 fusion.10
  328.7 173.4 %reduce-scatter.2.cloned.1.call-done = f32[16,512]{1,0:T(8,128)} async-done(((f32[512,512]{1,0:T(8,128)}), f32[16,512]{1,0:T(8,128)}) %reduce-scatter.2.cloned.1.call-update) | async-done | bytes 32784 | tf_op jit(solution)/shard_map/reduce_scatter | solution.py:96
  502.1 1.4 broadcast_multiply_fusion
  (101 shorter events, 16.4 us)
Async XLA Ops:
  7.2 7.3 %copy-start = (bf16[512,512]{1,0:T(8,128)(2,1)S(1)}, bf16[512,512]{1,0:T(8,128)(2,1)}, u32[]{:S(2)}) copy-start(bf16[512,512]{1,0:T(8,128)(2,1)} %param.11) | copy-start | bytes 1572868
  7.2 2.4 copy-start.16
  7.2 3.8 copy-start.14
  7.2 5.4 %copy-start.15 = (s32[1,8,6]{1,0,2:T(1,128)S(1)}, s32[1,8,6]{1,0,2:T(1,128)}, u32[]{:S(2)}) copy-start(s32[1,8,6]{1,0,2:T(1,128)} %param.14) | copy-start | bytes 580
  7.2 494.9 %reduce-scatter.2.cloned.1.call-start = ((), (), s32[]{:S(2)}) async-start(), calls=%async_computation.1 | async-start | bytes 1081344 | tf_op jit(solution)/shard_map/reduce_scatter | solution.py:96
  9.6 4.9 copy-start.1
  9.6 4.9 copy-start.3
  16.0 17.5 %collective-permute-start = (f32[2,128,512]{2,1,0:T(8,128)}, f32[2,128,512]{2,1,0:T(8,128)}, u32[]{:S(2)}, u32[]{:S(2)}) collective-permute-start(f32[2,128,512]{2,1,0:T(8,128)} %fusion.64), channel_id=1, source_target_pairs={{0,1},{1,2},{2,3},{3,4},{4,5},{5,6},{6,7},{7,8},{8,9},{9,10},{10,1... | collective-permute-start | bytes 1572872 | tf_op jit(solution)/shard_map/ppermute | solution.py:10
  20.0 92.7 %collective-permute-start.10 = (bf16[256,512]{1,0:T(8,128)(2,1)}, bf16[256,512]{1,0:T(8,128)(2,1)}, u32[]{:S(2)}, u32[]{:S(2)}) collective-permute-start(bf16[256,512]{1,0:T(8,128)(2,1)} %param.8), channel_id=1, source_target_pairs={{0,8},{1,9},{2,10},{3,11},{4,12},{5,13},{6,14},{7,15},{8,16},{9,17... | collective-permute-start | bytes 786440 | tf_op jit(solution)/shard_map/ppermute | solution.py:10
  35.8 30.5 %collective-permute-start.1 = (f32[2,128,512]{2,1,0:T(8,128)}, f32[2,128,512]{2,1,0:T(8,128)}, u32[]{:S(2)}, u32[]{:S(2)}) collective-permute-start(f32[2,128,512]{2,1,0:T(8,128)} %convolution_add_fusion.7), channel_id=1, source_target_pairs={{0,1},{1,2},{2,3},{3,4},{4,5},{5,6},{6,7},{7,8},{8,9},{9,10},{10,1... | collective-permute-start | bytes 1572872 | tf_op jit(solution)/shard_map/ppermute | solution.py:10
  68.2 22.1 %collective-permute-start.2 = (f32[2,128,512]{2,1,0:T(8,128)}, f32[2,128,512]{2,1,0:T(8,128)}, u32[]{:S(2)}, u32[]{:S(2)}) collective-permute-start(f32[2,128,512]{2,1,0:T(8,128)} %add.60), channel_id=1, source_target_pairs={{0,1},{1,2},{2,3},{3,4},{4,5},{5,6},{6,7},{7,8},{8,9},{9,10},{10,1... | collective-permute-start | bytes 1572872 | tf_op jit(solution)/shard_map/ppermute | solution.py:10
  92.2 16.5 %collective-permute-start.3 = (f32[2,128,512]{2,1,0:T(8,128)}, f32[2,128,512]{2,1,0:T(8,128)}, u32[]{:S(2)}, u32[]{:S(2)}) collective-permute-start(f32[2,128,512]{2,1,0:T(8,128)} %add.61), channel_id=1, source_target_pairs={{0,1},{1,2},{2,3},{3,4},{4,5},{5,6},{6,7},{7,8},{8,9},{9,10},{10,1... | collective-permute-start | bytes 1572872 | tf_op jit(solution)/shard_map/ppermute | solution.py:10
  95.9 16.9 %copy-start.13 = (bf16[256,512]{1,0:T(8,128)(2,1)S(1)}, bf16[256,512]{1,0:T(8,128)(2,1)}, u32[]{:S(2)}) copy-start(bf16[256,512]{1,0:T(8,128)(2,1)} %param.8) | copy-start | bytes 786436
  110.8 20.0 %collective-permute-start.4 = (f32[2,128,512]{2,1,0:T(8,128)}, f32[2,128,512]{2,1,0:T(8,128)}, u32[]{:S(2)}, u32[]{:S(2)}) collective-permute-start(f32[2,128,512]{2,1,0:T(8,128)} %add.62), channel_id=1, source_target_pairs={{0,1},{1,2},{2,3},{3,4},{4,5},{5,6},{6,7},{7,8},{8,9},{9,10},{10,1... | collective-permute-start | bytes 1572872 | tf_op jit(solution)/shard_map/ppermute | solution.py:10
  113.5 42.3 %collective-permute-start.11 = (bf16[256,512]{1,0:T(8,128)(2,1)}, bf16[256,512]{1,0:T(8,128)(2,1)}, u32[]{:S(2)}, u32[]{:S(2)}) collective-permute-start(bf16[256,512]{1,0:T(8,128)(2,1)} %broadcast_select_fusion), channel_id=1, source_target_pairs={{0,16},{1,17},{2,18},{3,19},{4,20},{5,21},{6,22},{7,23},{8,24},{9,... | collective-permute-start | bytes 786440 | tf_op jit(solution)/shard_map/ppermute | solution.py:10
  124.4 14.1 %copy-start.12 = (f32[256,256]{1,0:T(8,128)S(1)}, f32[256,256]{1,0:T(8,128)}, u32[]{:S(2)}) copy-start(f32[256,256]{1,0:T(8,128)} %copy.80) | copy-start | bytes 786436
  132.7 30.9 %collective-permute-start.5 = (f32[2,128,512]{2,1,0:T(8,128)}, f32[2,128,512]{2,1,0:T(8,128)}, u32[]{:S(2)}, u32[]{:S(2)}) collective-permute-start(f32[2,128,512]{2,1,0:T(8,128)} %add.63), channel_id=1, source_target_pairs={{0,1},{1,2},{2,3},{3,4},{4,5},{5,6},{6,7},{7,8},{8,9},{9,10},{10,1... | collective-permute-start | bytes 1572872 | tf_op jit(solution)/shard_map/ppermute | solution.py:10
  157.5 15.9 %collective-permute-start.12 = (bf16[256,512]{1,0:T(8,128)(2,1)}, bf16[256,512]{1,0:T(8,128)(2,1)}, u32[]{:S(2)}, u32[]{:S(2)}) collective-permute-start(bf16[256,512]{1,0:T(8,128)(2,1)} %broadcast_select_fusion.1), channel_id=1, source_target_pairs={{0,1},{1,2},{2,3},{3,4},{4,5},{5,6},{6,7},{7,8},{8,9},{9,10},{10,1... | collective-permute-start | bytes 786440 | tf_op jit(solution)/shard_map/ppermute | solution.py:10
  163.7 3.9 copy-start.11
  165.6 22.1 %collective-permute-start.6 = (f32[2,128,512]{2,1,0:T(8,128)}, f32[2,128,512]{2,1,0:T(8,128)}, u32[]{:S(2)}, u32[]{:S(2)}) collective-permute-start(f32[2,128,512]{2,1,0:T(8,128)} %add.64), channel_id=1, source_target_pairs={{0,1},{1,2},{2,3},{3,4},{4,5},{5,6},{6,7},{7,8},{8,9},{9,10},{10,1... | collective-permute-start | bytes 1572872 | tf_op jit(solution)/shard_map/ppermute | solution.py:10
  170.6 6.0 %copy-start.10 = (f32[2,128,2,128]{1,3,2,0:T(8,128)S(1)}, f32[2,128,2,128]{1,3,2,0:T(8,128)}, u32[]{:S(2)}) copy-start(f32[2,128,2,128]{1,3,2,0:T(8,128)} %copy.42) | copy-start | bytes 786436
  173.4 10.0 %collective-permute-start.13 = (bf16[256,512]{1,0:T(8,128)(2,1)}, bf16[256,512]{1,0:T(8,128)(2,1)S(1)}, u32[]{:S(2)}, u32[]{:S(2)}) collective-permute-start(bf16[256,512]{1,0:T(8,128)(2,1)} %collective-permute-done.12), channel_id=1, source_target_pairs={{0,1},{1,2},{2,3},{3,4},{4,5},{5,6},{6,7},{7,8},{8,9},{9,10},{10,1... | collective-permute-start | bytes 786440 | tf_op jit(solution)/shard_map/ppermute | solution.py:10
  176.7 14.5 %copy-start.9 = (f32[2,128,2,128]{1,3,2,0:T(8,128)S(1)}, f32[2,128,2,128]{1,3,2,0:T(8,128)}, u32[]{:S(2)}) copy-start(f32[2,128,2,128]{1,3,2,0:T(8,128)} %copy.46) | copy-start | bytes 786436
  178.1 25.9 %copy-start.8 = (f32[2,128,2,128]{1,3,2,0:T(8,128)S(1)}, f32[2,128,2,128]{1,3,2,0:T(8,128)}, u32[]{:S(2)}) copy-start(f32[2,128,2,128]{1,3,2,0:T(8,128)} %copy.48) | copy-start | bytes 786436
  183.4 13.6 %collective-permute-start.14 = (bf16[256,512]{1,0:T(8,128)(2,1)S(1)}, bf16[256,512]{1,0:T(8,128)(2,1)S(1)}, u32[]{:S(2)}, u32[]{:S(2)}) collective-permute-start(bf16[256,512]{1,0:T(8,128)(2,1)S(1)} %collective-permute-done.13), channel_id=1, source_target_pairs={{0,1},{1,2},{2,3},{3,4},{4,5},{5,6},{6,7},{7,8},{8,9},{9,10},{10,1... | collective-permute-start | bytes 786440 | tf_op jit(solution)/shard_map/ppermute | solution.py:10
  188.9 35.6 %collective-permute-start.7 = (f32[2,128,512]{2,1,0:T(8,128)S(1)}, f32[2,128,512]{2,1,0:T(8,128)S(1)}, u32[]{:S(2)}, u32[]{:S(2)}) collective-permute-start(f32[2,128,512]{2,1,0:T(8,128)S(1)} %add.65), channel_id=1, source_target_pairs={{0,25},{1,26},{2,27},{3,28},{4,29},{5,30},{6,31},{7,0},{8,1},{9,2}... | collective-permute-start | bytes 1572872 | tf_op jit(solution)/shard_map/ppermute | solution.py:10
  191.2 35.2 %copy-start.7 = (f32[2,128,2,128]{1,3,2,0:T(8,128)S(1)}, f32[2,128,2,128]{1,3,2,0:T(8,128)}, u32[]{:S(2)}) copy-start(f32[2,128,2,128]{1,3,2,0:T(8,128)} %copy.50) | copy-start | bytes 786436
  197.0 15.4 %collective-permute-start.15 = (bf16[256,512]{1,0:T(8,128)(2,1)S(1)}, bf16[256,512]{1,0:T(8,128)(2,1)S(1)}, u32[]{:S(2)}, u32[]{:S(2)}) collective-permute-start(bf16[256,512]{1,0:T(8,128)(2,1)S(1)} %collective-permute-done.14), channel_id=1, source_target_pairs={{0,1},{1,2},{2,3},{3,4},{4,5},{5,6},{6,7},{7,8},{8,9},{9,10},{10,1... | collective-permute-start | bytes 786440 | tf_op jit(solution)/shard_map/ppermute | solution.py:10
  204.0 26.2 %copy-start.6 = (f32[2,128,2,128]{1,3,2,0:T(8,128)S(1)}, f32[2,128,2,128]{1,3,2,0:T(8,128)}, u32[]{:S(2)}) copy-start(f32[2,128,2,128]{1,3,2,0:T(8,128)} %copy.52) | copy-start | bytes 786436
  212.4 14.5 %collective-permute-start.16 = (bf16[256,512]{1,0:T(8,128)(2,1)S(1)}, bf16[256,512]{1,0:T(8,128)(2,1)S(1)}, u32[]{:S(2)}, u32[]{:S(2)}) collective-permute-start(bf16[256,512]{1,0:T(8,128)(2,1)S(1)} %collective-permute-done.15), channel_id=1, source_target_pairs={{0,1},{1,2},{2,3},{3,4},{4,5},{5,6},{6,7},{7,8},{8,9},{9,10},{10,1... | collective-permute-start | bytes 786440 | tf_op jit(solution)/shard_map/ppermute | solution.py:10
  224.5 21.8 %collective-permute-start.8 = (f32[2,128,512]{2,1,0:T(8,128)S(1)}, f32[2,128,512]{2,1,0:T(8,128)S(1)}, u32[]{:S(2)}, u32[]{:S(2)}) collective-permute-start(f32[2,128,512]{2,1,0:T(8,128)S(1)} %collective-permute-done.7), channel_id=1, source_target_pairs={{0,24},{1,25},{2,26},{3,27},{4,28},{5,29},{6,30},{7,31},{8,0},{9,1... | collective-permute-start | bytes 1572872 | tf_op jit(solution)/shard_map/ppermute | solution.py:10
  226.8 9.3 %collective-permute-start.17 = (bf16[256,512]{1,0:T(8,128)(2,1)S(1)}, bf16[256,512]{1,0:T(8,128)(2,1)S(1)}, u32[]{:S(2)}, u32[]{:S(2)}) collective-permute-start(bf16[256,512]{1,0:T(8,128)(2,1)S(1)} %collective-permute-done.16), channel_id=1, source_target_pairs={{0,1},{1,2},{2,3},{3,4},{4,5},{5,6},{6,7},{7,8},{8,9},{9,10},{10,1... | collective-permute-start | bytes 786440 | tf_op jit(solution)/shard_map/ppermute | solution.py:10
  230.2 24.9 %copy-start.5 = (f32[2,128,2,128]{1,3,2,0:T(8,128)S(1)}, f32[2,128,2,128]{1,3,2,0:T(8,128)}, u32[]{:S(2)}) copy-start(f32[2,128,2,128]{1,3,2,0:T(8,128)} %copy.54) | copy-start | bytes 786436
  236.2 26.6 %collective-permute-start.18 = (bf16[256,512]{1,0:T(8,128)(2,1)S(1)}, bf16[256,512]{1,0:T(8,128)(2,1)S(1)}, u32[]{:S(2)}, u32[]{:S(2)}) collective-permute-start(bf16[256,512]{1,0:T(8,128)(2,1)S(1)} %collective-permute-done.17), channel_id=1, source_target_pairs={{0,1},{1,2},{2,3},{3,4},{4,5},{5,6},{6,7},{7,8},{8,9},{9,10},{10,1... | collective-permute-start | bytes 786440 | tf_op jit(solution)/shard_map/ppermute | solution.py:10
  246.3 35.9 %collective-permute-start.9 = (f32[2,128,512]{2,1,0:T(8,128)S(1)}, f32[2,128,512]{2,1,0:T(8,128)S(1)}, u32[]{:S(2)}, u32[]{:S(2)}) collective-permute-start(f32[2,128,512]{2,1,0:T(8,128)S(1)} %broadcast_select_fusion.2), channel_id=1, source_target_pairs={{0,16},{1,17},{2,18},{3,19},{4,20},{5,21},{6,22},{7,23},{8,24},{9,... | collective-permute-start | bytes 1572872 | tf_op jit(solution)/shard_map/ppermute | solution.py:10
  263.2 64.1 %copy-start.2 = (bf16[256,512]{1,0:T(8,128)(2,1)S(1)}, bf16[256,512]{1,0:T(8,128)(2,1)}, u32[]{:S(2)}) copy-start(bf16[256,512]{1,0:T(8,128)(2,1)} %param.10) | copy-start | bytes 786436
  263.2 64.1 %copy-start.4 = (bf16[256,512]{1,0:T(8,128)(2,1)S(1)}, bf16[256,512]{1,0:T(8,128)(2,1)}, u32[]{:S(2)}) copy-start(bf16[256,512]{1,0:T(8,128)(2,1)} %param.9) | copy-start | bytes 786436
Sparse Core Ops, SparseCore 0:
  328.8 173.2 reduce-scatter.1
where the time goes:
time: 515 us; the launch traced here: 510 us
  waiting for transfers between devices  310 us (60%)
  starting transfers between devices  84.3 us (16%)
  blocking collectives  45 us (9%)
  other arithmetic  20 us (4%)
  matrix products  19.1 us (4%)
  local copies, waits for them, and re-layouts  17.1 us (3%)
  between operations  14.9 us (3%)
    reduce_scatter x1, waiting for transfers between devices, shards(): lax.psum_scatter(lax.dot_general(grad_out, own_aggregate, (((0,), (0,)),...  173 us
    ppermute x19, waiting for transfers between devices, passed_along(): return lax.ppermute(value, axis, pairs)  136 us
    ppermute x19, starting transfers between devices, passed_along(): return lax.ppermute(value, axis, pairs)  84.3 us
    psum x1, blocking collectives, shards(): lax.psum(carried.reshape(row_count, feat_width), 'rep').astype(jnp.bfloat16)  45 us
    dot_general x16, matrix products, place_tiles(): lax.dot_general(operator, flat_source, (((contract,), (0,)), ((), ())), p...  12.8 us
    add x6, other arithmetic, shards(): carried + place_tiles(tile_values[0, turn_index], tile_rows[0, turn_index...  10.9 us
  transfers between devices with their start and end apart: 20, of which 14 were waited for; matrix products, arithmetic and copies ran while one was open for 9% of the time, Pallas kernels for 0%

commit v1 on v0

v1 whole, which is shorter than its diff:
```python
import functools

import jax
import jax.numpy as jnp
import numpy as np
from jax import lax
from jax.experimental import pallas as pl
from jax.experimental.pallas import tpu as pltpu
from jax.sharding import Mesh, PartitionSpec as P

ZH, ZL, YL, REP = 4, 4, 2, 4
BLK = ("zh", "zl", "yl")
BF16, F32 = jnp.bfloat16, jnp.float32
VMEM_LIMIT = 48 * 1024 * 1024


def contract_rows(left, right):
    return lax.dot_general(left, right, (((0,), (0,)), ((), ())), preferred_element_type=F32)


def hidden_order(width):
    rows = width // (ZH * ZL * YL)
    units = np.arange(width).reshape(ZH, ZL, YL, REP, rows // REP)
    return units.transpose(3, 1, 2, 0, 4).reshape(-1)


def dense_kernel(rows_ref, cols_ref, count_ref, tiles_ref, out_ref, acc_ref, *, odd):
    step = 2 * pl.program_id(0) + odd
    slots, tile = tiles_ref.shape[2], tiles_ref.shape[3]
    acc_ref[...] = jnp.zeros_like(acc_ref)
    live = count_ref[step]
    for q in range(slots):

        @pl.when(q < live)
        def _():
            row, col = rows_ref[step * slots + q], cols_ref[step * slots + q]
            acc_ref[row, col] += tiles_ref[0, 0, q].astype(F32)

    for row in range(2):
        for col in range(2):
            out_ref[row * tile : (row + 1) * tile, col * tile : (col + 1) * tile] = acc_ref[
                row, col
            ].astype(BF16)


def dense_steps(tiles, rows, cols, count, odd):
    pairs, _, slots, tile, _ = tiles.shape
    return pl.pallas_call(
        functools.partial(dense_kernel, odd=odd),
        grid_spec=pltpu.PrefetchScalarGridSpec(
            num_scalar_prefetch=3,
            grid=(pairs,),
            in_specs=[pl.BlockSpec((1, 1, slots, tile, tile), lambda i, *_: (i, odd, 0, 0, 0))],
            out_specs=pl.BlockSpec((2 * tile, 2 * tile), lambda i, *_: (0, i)),
            scratch_shapes=[pltpu.VMEM((2, 2, tile, tile), F32)],
        ),
        out_shape=jax.ShapeDtypeStruct((2 * tile, pairs * 2 * tile), BF16),
        cost_estimate=pl.CostEstimate(flops=0, bytes_accessed=2 * tiles.size, transcendentals=0),
    )(rows, cols, count, tiles)


def partial_kernel(zl_ref, even_ref, odd_ref, own_ref, next_ref, out_ref):
    rows, wide = even_ref.shape
    quarter = out_ref.shape[3]
    for m in range(wide // rows):
        span = slice(m * rows, (m + 1) * rows)
        block = contract_rows(even_ref[:, span], own_ref[...])
        block += contract_rows(odd_ref[:, span], next_ref[...])
        block = block.astype(BF16)
        slot = lax.rem(zl_ref[0] + ZL - m, ZL)
        for q in range(REP):
            out_ref[q, slot] = block[:, q * quarter : (q + 1) * quarter]


def gather_kernel(zh_ref, zl_ref, in_ref, out_ref):
    zh, zl = zh_ref[0], zl_ref[0]
    for d in range(ZH):
        total = jnp.zeros(out_ref.shape[1:], F32)
        for s in range(ZL):
            borrow = (s < zl).astype(jnp.int32)
            total += in_ref[lax.rem(zh - d - borrow + 2 * ZH, ZH), s].astype(F32)
        out_ref[d] = total.astype(BF16)


def weight_kernel(in_ref, feat_ref, p_ref, gw_ref, *, scale):
    total = in_ref[0].astype(F32)
    for d in range(1, in_ref.shape[0]):
        total += in_ref[d].astype(F32)
    p_ref[...] = total.astype(BF16)
    gw_ref[...] = (contract_rows(p_ref[...], feat_ref[...]) * scale).astype(BF16)


def feature_kernel(p_ref, weight_ref, out_ref):
    quarter = p_ref.shape[2]
    rows = out_ref.shape[0]
    total = jnp.zeros(out_ref.shape, F32)
    for q in range(p_ref.shape[0]):
        total += jnp.dot(
            p_ref[q, :rows, :],
            weight_ref[q * quarter : (q + 1) * quarter, :],
            preferred_element_type=F32,
        )
    out_ref[...] = total.astype(BF16)


def whole(kernel, outs, scalars, arrays):
    return pl.pallas_call(
        kernel,
        in_specs=[pl.BlockSpec(memory_space=pltpu.SMEM)] * len(scalars)
        + [pl.BlockSpec(memory_space=pltpu.VMEM)] * len(arrays),
        out_specs=jax.tree.map(lambda _: pl.BlockSpec(memory_space=pltpu.VMEM), outs),
        out_shape=outs,
        compiler_params=pltpu.CompilerParams(vmem_limit_bytes=VMEM_LIMIT),
    )(*scalars, *arrays)


def exchange(value, axes):
    return lax.all_to_all(value, axes, 0, 0)


def to_previous(value):
    count = ZH * ZL * YL
    return lax.ppermute(value, BLK, [(b, (b - 1) % count) for b in range(count)])


def shards(features, pre_act, upstream, weight, tile_values, tile_rows, tile_cols, tile_count):
    _, steps, slots, tile, _ = tile_values.shape
    nodes, width = features.shape
    hidden = upstream.shape[1]
    quarter = hidden // REP
    scale = float(nodes * ZH * ZL * YL) ** -0.5
    zh = lax.axis_index("zh").reshape(1)
    zl = lax.axis_index("zl").reshape(1)
    shape = jax.ShapeDtypeStruct

    spread = np.zeros((hidden, hidden), np.float32)
    spread[hidden_order(hidden), np.arange(hidden)] = 1.0
    spread = jnp.asarray(spread, BF16)
    grad_out = jnp.where(pre_act > 0, upstream, jnp.zeros_like(upstream))
    own = jnp.dot(grad_out, spread, preferred_element_type=F32).astype(BF16)
    weight = contract_rows(spread, weight).astype(BF16)

    tiles = tile_values.reshape(steps // 2, 2, slots, tile, tile)
    places = (tile_rows.reshape(-1), tile_cols.reshape(-1), tile_count.reshape(-1))
    following = to_previous(own)
    odd = to_previous(dense_steps(tiles, *places, 1))
    even = dense_steps(tiles, *places, 0)

    parts = whole(
        partial_kernel, shape((REP, ZL, nodes, quarter), BF16), (zl,), (even, odd, own, following)
    )
    parts = exchange(parts.reshape(REP * ZL, nodes, quarter), ("rep", "zl"))
    parts = whole(
        gather_kernel,
        shape((ZH, nodes, quarter), BF16),
        (zh, zl),
        (parts.reshape(REP, ZL, nodes, quarter),),
    )
    parts = exchange(parts, "zh")
    p_quarter, gw = whole(
        functools.partial(weight_kernel, scale=scale),
        (shape((nodes, quarter), BF16), shape((quarter, width), BF16)),
        (),
        (parts, features),
    )
    lanes = ZL * YL
    gw = exchange(gw.reshape(lanes, quarter // lanes, width), ("zl", "yl"))
    gw = jnp.sum(gw.astype(F32), axis=0).astype(BF16)
    gw = exchange(gw.reshape(ZH, quarter // (lanes * ZH), width), "zh")
    gw = jnp.sum(gw.astype(F32), axis=0)
    high = lax.reduce_precision(gw, 8, 7)
    gw_rows = gw.size // quarter
    packed = jnp.concatenate(
        [
            p_quarter,
            high.astype(BF16).reshape(gw_rows, quarter),
            (gw - high).astype(BF16).reshape(gw_rows, quarter),
        ]
    )
    packed = exchange(jnp.broadcast_to(packed[None], (REP,) + packed.shape), "rep")
    grad_feat = whole(feature_kernel, shape((nodes, width), BF16), (), (packed, weight))
    high = packed[:, nodes : nodes + gw_rows].astype(F32)
    low = packed[:, nodes + gw_rows :].astype(F32)
    return grad_feat, (high + low).reshape(-1, width)


def solution(mesh):
    dp = mesh.shape["dp"]
    fine = Mesh(mesh.devices.reshape(dp, REP, ZH, ZL, YL), ("dp", "rep") + BLK)
    rows = ("dp",) + BLK
    return jax.shard_map(
        shards,
        mesh=fine,
        in_specs=(
            P(rows, None),
            P(rows, None),
            P(rows, None),
            P(),
            P(rows, "rep", None, None, None),
            P(rows, "rep", None),
            P(rows, "rep", None),
            P(rows, "rep"),
        ),
        out_specs=(P(rows, None), P(rows, None)),
        check_vma=False,
    )
```

time: 515 us -> 140 us (0.27)
  waiting for transfers between devices: 310 us -> 36.3 us
  starting transfers between devices: 84.3 us -> 28.9 us
  other arithmetic: 20 us -> 0.06 us
  matrix products: 19.1 us -> 0.77 us
  between operations: 14.9 us -> 0.77 us
  local copies, waits for them, and re-layouts: 17.1 us -> 5.29 us
  Pallas kernels: 0 us -> 11.3 us
  blocking collectives: 45 us -> 55 us
    reduce_scatter x1 -> x0, waiting for transfers between devices: 173 us -> none  [shards(): lax.psum_scatter(lax.dot_general(grad_out, own_aggregate, (((0,), (0,)),...]
    ppermute x19 -> x2, waiting for transfers between devices: 136 us -> 3.08 us  [to_previous(): lax.ppermute(value, BLK, [(b, (b - 1) % count) for b in range(count)])]
    ppermute x19 -> x2, starting transfers between devices: 84.3 us -> 14.8 us  [to_previous(): lax.ppermute(value, BLK, [(b, (b - 1) % count) for b in range(count)])]
    all_to_all x0 -> x3, blocking collectives: none -> 55 us  [exchange(): return lax.all_to_all(value, axes, 0, 0)]
    psum x1 -> x0, blocking collectives: 45 us -> none  [shards(): lax.psum(carried.reshape(row_count, feat_width), 'rep').astype(jnp.bfloat16)]
    all_to_all x0 -> x2, waiting for transfers between devices: none -> 33.2 us  [exchange(): return lax.all_to_all(value, axes, 0, 0)]
    dot_general x26 -> x2, matrix products: 19.1 us -> 0.77 us  [the longest x1 0.46 us: contract_rows(): lax.dot_general(left, right, (((0,), (0,)), ((), ())), preferred_element_...]
    all_to_all x0 -> x2, starting transfers between devices: none -> 14.1 us  [exchange(): return lax.all_to_all(value, axes, 0, 0)]
  transfers between devices with their start and end apart: 20 -> 4, of which waited for: 14 -> 3; matrix products, arithmetic and copies ran while one was open for 9% -> 1% of each run, Pallas kernels for 0% -> 3%
where the time goes in v1:
time: 140 us; the launch traced here: 138 us
  blocking collectives  55 us (39%)
  waiting for transfers between devices  36.3 us (26%)
  starting transfers between devices  28.9 us (21%)
  Pallas kernels  11.3 us (8%)
  local copies, waits for them, and re-layouts  5.29 us (4%)
    all_to_all x3, blocking collectives, exchange(): return lax.all_to_all(value, axes, 0, 0)  55 us
    all_to_all x2, waiting for transfers between devices, exchange(): return lax.all_to_all(value, axes, 0, 0)  33.2 us
    ppermute x2, starting transfers between devices, to_previous(): lax.ppermute(value, BLK, [(b, (b - 1) % count) for b in range(count)])  14.8 us
    all_to_all x2, starting transfers between devices, exchange(): return lax.all_to_all(value, axes, 0, 0)  14.1 us
    pallas_call x2, Pallas kernels, dense_steps(): pl.pallas_call(functools.partial(dense_kernel, odd=odd), grid_spec=pltpu....  8.07 us
    pallas_call x4, Pallas kernels, whole(): pl.pallas_call(kernel, in_specs=[pl.BlockSpec(memory_space=pltpu.SMEM)] *...  3.2 us
    ppermute x2, waiting for transfers between devices, to_previous(): lax.ppermute(value, BLK, [(b, (b - 1) % count) for b in range(count)])  3.08 us
  transfers between devices with their start and end apart: 4, of which 3 were waited for; matrix products, arithmetic and copies ran while one was open for 1% of the time, Pallas kernels for 3%

profile of v1, /device:TPU:24, one launch (start us, length us, event | category | flops | bytes accessed | tf_op | source)
XLA Modules:
  0.0 138.4 jit_solution(9566770119307344808)
XLA Ops:
  0.6 0.0 copy-start
  0.6 0.0 copy-start.5
  0.7 0.0 copy-start.4
  0.7 0.0 copy-start.3
  0.7 0.9 copy.15
  1.6 0.6 reshape.44.rows_ref
  2.1 0.8 copy.16
  2.9 0.6 reshape.45.cols_ref
  3.5 4.0 %shard_map.105 = bf16[256,1024]{1,0:T(8,128)(2,1)} custom-call(s32[48]{0:T(128)} %reshape.44.rows_ref, s32[48]{0:T(128)} %reshape.45.cols_ref, s32[8]{0:T(128)} %bitcast.14, bf16[4,2,6,128,128]{4,3,2,1,0:T(8,128)(2,1)} %bitcast.12), custom_call_target="tpu_custom_call" | custom-call | bytes 1572864 | tf_op jit(solution)/shard_map/pallas_call | solution.py:48
  7.5 2.7 %collective-permute-start = (bf16[256,1024]{1,0:T(8,128)(2,1)}, bf16[256,1024]{1,0:T(8,128)(2,1)S(1)}, u32[]{:S(2)}, u32[]{:S(2)}) collective-permute-start(bf16[256,1024]{1,0:T(8,128)(2,1)} %shard_map.105), channel_id=1, source_target_pairs={{0,31},{1,0},{2,1},{3,2},{4,3},{5,4},{6,5},{7,6},{8,7},{9,8},{10,9... | collective-permute-start | bytes 1572872 | tf_op jit(solution)/shard_map/ppermute | solution.py:123
  10.2 0.0 copy-done.5
  10.2 0.0 copy-done.4
  10.2 0.0 copy-done.3
  10.2 0.3 convolution_convert_fusion.1.own_ref
  10.5 12.1 %collective-permute-start.1 = (bf16[256,512]{1,0:T(8,128)(2,1)S(1)}, bf16[256,512]{1,0:T(8,128)(2,1)S(1)}, u32[]{:S(2)}, u32[]{:S(2)}) collective-permute-start(bf16[256,512]{1,0:T(8,128)(2,1)S(1)} %convolution_convert_fusion.1.own_ref), channel_id=1, source_target_pairs={{0,31},{1,0},{2,1},{3,2},{4,3},{5,4},{6,5},{7,6},{8,7},{9,8},{10,9... | collective-permute-start | bytes 786440 | tf_op jit(solution)/shard_map/ppermute | solution.py:123
  22.6 4.1 %shard_map.104.even_ref = bf16[256,1024]{1,0:T(8,128)(2,1)} custom-call(s32[48]{0:T(128)} %reshape.44.rows_ref, s32[48]{0:T(128)} %reshape.45.cols_ref, s32[8]{0:T(128)} %bitcast.15, bf16[4,2,6,128,128]{4,3,2,1,0:T(8,128)(2,1)} %bitcast.13), custom_call_target="tpu_custom_call" | custom-call | bytes 1572864 | tf_op jit(solution)/shard_map/pallas_call | solution.py:48
  26.7 3.1 %collective-permute-done.1.next_ref = bf16[256,512]{1,0:T(8,128)(2,1)S(1)} collective-permute-done((bf16[256,512]{1,0:T(8,128)(2,1)S(1)}, bf16[256,512]{1,0:T(8,128)(2,1)S(1)}, u32[]{:S(2)}, u32[]{:S(2)}) %collective-permute-start.1) | collective-permute-done | bytes 262176 | tf_op jit(solution)/shard_map/ppermute | solution.py:123
  29.8 0.0 collective-permute-done.odd_ref
  29.8 0.0 copy-start.1
  29.8 1.0 copy-done.1
  30.8 1.7 %shard_map.106 = bf16[4,4,256,128]{3,2,1,0:T(8,128)(2,1)} custom-call(s32[1]{0:T(128)} %bitcast.1.zl_ref, bf16[256,1024]{1,0:T(8,128)(2,1)S(1)} %copy-done.1, bf16[256,1024]{1,0:T(8,128)(2,1)S(1)} %collective-permute-done.odd_ref, bf16[256,512]{1,0:T(8,128)(2,1)S(1)} %convolution_convert_fusion.1.own_ref, bf16[256,512]{1,0:T(8,128)(2,1)S(1)} %collective-permute-done.1.next_ref), custom_call_target="tpu_custom_call" | custom-call | tf_op jit(solution)/shard_map/pallas_call | solution.py:107
  32.5 0.0 copy-start.2
  32.5 9.8 %all-to-all-start = ((bf16[16,256,128]{2,1,0:T(8,128)(2,1)}), bf16[16,256,128]{2,1,0:T(8,128)(2,1)S(1)}, u32[]{:S(2)}, u32[]{:S(2)}) async-start(bf16[16,256,128]{2,1,0:T(8,128)(2,1)} %bitcast.4), calls=%async_computation | async-start | bytes 2097152 | tf_op jit(solution)/shard_map/all_to_all | solution.py:118
  42.4 26.9 %all-to-all-done = bf16[16,256,128]{2,1,0:T(8,128)(2,1)S(1)} async-done(((bf16[16,256,128]{2,1,0:T(8,128)(2,1)}), bf16[16,256,128]{2,1,0:T(8,128)(2,1)S(1)}, u32[]{:S(2)}, u32[]{:S(2)}) %all-to-all-start) | async-done | bytes 1048608 | tf_op jit(solution)/shard_map/all_to_all | solution.py:118
  69.2 0.1 shard_map.107
  69.4 29.8 %all_to_all.25.in_ref = bf16[4,256,128]{2,1,0:T(8,128)(2,1)S(1)} all-to-all(bf16[4,256,128]{2,1,0:T(8,128)(2,1)S(1)} %shard_map.107), channel_id=1, replica_groups=mesh['dp'=4,'rep'=4,'zh'=4,'zl'=4,'yl'=2] {'zh'}, dimensions={0} | all-to-all | bytes 524288 | tf_op jit(solution)/shard_map/all_to_all | solution.py:118
  99.1 0.0 copy-done.2
  99.1 0.2 shard_map.108
  99.4 9.5 %all_to_all.26 = bf16[8,16,512]{2,1,0:T(8,128)(2,1)S(1)} all-to-all(bf16[8,16,512]{2,1,0:T(8,128)(2,1)S(1)} %bitcast.11), channel_id=1, replica_groups=mesh['dp'=4,'rep'=4,'zh'=4,'zl'=4,'yl'=2] {'zl','yl'}, dimensions={0} | all-to-all | bytes 262144 | tf_op jit(solution)/shard_map/all_to_all | solution.py:118
  108.9 15.8 %all_to_all.27 = bf16[4,4,512]{2,1,0:T(4,128)(2,1)S(1)} all-to-all(bf16[4,4,512]{2,1,0:T(4,128)(2,1)S(1)} %reshape.51), channel_id=1, replica_groups=mesh['dp'=4,'rep'=4,'zh'=4,'zl'=4,'yl'=2] {'zh'}, dimensions={0} | all-to-all | bytes 32768 | tf_op jit(solution)/shard_map/all_to_all | solution.py:118
  124.7 0.8 broadcast_in_dim.2
  125.5 4.3 %all-to-all-start.4 = ((bf16[4,288,128]{2,1,0:T(8,128)(2,1)}), bf16[4,288,128]{2,1,0:T(8,128)(2,1)S(1)}, u32[]{:S(2)}, u32[]{:S(2)}) async-start(bf16[4,288,128]{2,1,0:T(8,128)(2,1)} %broadcast_in_dim.2), calls=%async_computation.4 | async-start | bytes 589824 | tf_op jit(solution)/shard_map/all_to_all | solution.py:118
  129.8 0.0 copy-done
  129.8 0.5 convolution_convert_fusion.weight_ref
  130.2 6.4 %all-to-all-done.4.p_ref = bf16[4,288,128]{2,1,0:T(8,128)(2,1)S(1)} async-done(((bf16[4,288,128]{2,1,0:T(8,128)(2,1)}), bf16[4,288,128]{2,1,0:T(8,128)(2,1)S(1)}, u32[]{:S(2)}, u32[]{:S(2)}) %all-to-all-start.4) | async-done | bytes 294944 | tf_op jit(solution)/shard_map/all_to_all | solution.py:118
  136.6 0.6 reshape.52
  137.2 1.1 shard_map.109
  (7 shorter events, 0.1 us)
Async XLA Ops:
  0.6 129.1 %copy-start = (bf16[512,512]{1,0:T(8,128)(2,1)S(1)}, bf16[512,512]{1,0:T(8,128)(2,1)}, u32[]{:S(2)}) copy-start(bf16[512,512]{1,0:T(8,128)(2,1)} %param.12) | copy-start | bytes 1572868
  0.6 9.5 %copy-start.5 = (bf16[512,512]{1,0:T(8,128)(2,1)S(1)}, bf16[512,512]{1,0:T(8,128)(2,1)}, u32[]{:S(2)}) copy-start(bf16[512,512]{1,0:T(8,128)(2,1)} %constant.16.clone) | copy-start | bytes 1572868
  0.7 9.5 %copy-start.4 = (bf16[256,512]{1,0:T(8,128)(2,1)S(1)}, bf16[256,512]{1,0:T(8,128)(2,1)}, u32[]{:S(2)}) copy-start(bf16[256,512]{1,0:T(8,128)(2,1)} %param.10) | copy-start | bytes 786436
  0.7 9.5 %copy-start.3 = (bf16[256,512]{1,0:T(8,128)(2,1)S(1)}, bf16[256,512]{1,0:T(8,128)(2,1)}, u32[]{:S(2)}) copy-start(bf16[256,512]{1,0:T(8,128)(2,1)} %param.11) | copy-start | bytes 786436
  7.5 22.3 %collective-permute-start = (bf16[256,1024]{1,0:T(8,128)(2,1)}, bf16[256,1024]{1,0:T(8,128)(2,1)S(1)}, u32[]{:S(2)}, u32[]{:S(2)}) collective-permute-start(bf16[256,1024]{1,0:T(8,128)(2,1)} %shard_map.105), channel_id=1, source_target_pairs={{0,31},{1,0},{2,1},{3,2},{4,3},{5,4},{6,5},{7,6},{8,7},{9,8},{10,9... | collective-permute-start | bytes 1572872 | tf_op jit(solution)/shard_map/ppermute | solution.py:123
  10.5 19.2 %collective-permute-start.1 = (bf16[256,512]{1,0:T(8,128)(2,1)S(1)}, bf16[256,512]{1,0:T(8,128)(2,1)S(1)}, u32[]{:S(2)}, u32[]{:S(2)}) collective-permute-start(bf16[256,512]{1,0:T(8,128)(2,1)S(1)} %convolution_convert_fusion.1.own_ref), channel_id=1, source_target_pairs={{0,31},{1,0},{2,1},{3,2},{4,3},{5,4},{6,5},{7,6},{8,7},{9,8},{10,9... | collective-permute-start | bytes 786440 | tf_op jit(solution)/shard_map/ppermute | solution.py:123
  29.8 1.0 copy-start.1
  32.5 66.6 %copy-start.2 = (bf16[256,512]{1,0:T(8,128)(2,1)S(1)}, bf16[256,512]{1,0:T(8,128)(2,1)}, u32[]{:S(2)}) copy-start(bf16[256,512]{1,0:T(8,128)(2,1)} %feat_ref.1) | copy-start | bytes 786436
  32.5 36.7 %all-to-all-start = ((bf16[16,256,128]{2,1,0:T(8,128)(2,1)}), bf16[16,256,128]{2,1,0:T(8,128)(2,1)S(1)}, u32[]{:S(2)}, u32[]{:S(2)}) async-start(bf16[16,256,128]{2,1,0:T(8,128)(2,1)} %bitcast.4), calls=%async_computation | async-start | bytes 2097152 | tf_op jit(solution)/shard_map/all_to_all | solution.py:118
  125.5 11.1 %all-to-all-start.4 = ((bf16[4,288,128]{2,1,0:T(8,128)(2,1)}), bf16[4,288,128]{2,1,0:T(8,128)(2,1)S(1)}, u32[]{:S(2)}, u32[]{:S(2)}) async-start(bf16[4,288,128]{2,1,0:T(8,128)(2,1)} %broadcast_in_dim.2), calls=%async_computation.4 | async-start | bytes 589824 | tf_op jit(solution)/shard_map/all_to_all | solution.py:118

commit v2 on v1

v2 whole, which is shorter than its diff:
```python
import functools

import jax
import jax.numpy as jnp
import numpy as np
from jax import lax
from jax.experimental import pallas as pl
from jax.experimental.pallas import tpu as pltpu
from jax.sharding import Mesh, PartitionSpec as P

ZH, ZL, YL, REP = 4, 4, 2, 4
BLK = ("zh", "zl", "yl")
BF16, F32 = jnp.bfloat16, jnp.float32
VMEM_LIMIT = 48 * 1024 * 1024


def contract_rows(left, right):
    return lax.dot_general(left, right, (((0,), (0,)), ((), ())), preferred_element_type=F32)


def hidden_order(width):
    units = np.arange(width).reshape(ZH * ZL * YL, REP, -1)
    return units.transpose(1, 0, 2).reshape(-1)


def dense_kernel(rows_ref, cols_ref, count_ref, tiles_ref, out_ref, acc_ref, *, places):
    slots, tile = tiles_ref.shape[2], tiles_ref.shape[3]
    for at, step in enumerate(places):
        acc_ref[...] = jnp.zeros_like(acc_ref)
        live = count_ref[0, step]
        for q in range(slots):

            @pl.when(q < live)
            def _():
                row, col = rows_ref[q, 0, step], cols_ref[q, 0, step]
                acc_ref[row, col] += tiles_ref[0, step, q].astype(F32)

        for row in range(2):
            for col in range(2):
                left = (2 * at + col) * tile
                out_ref[row * tile : (row + 1) * tile, left : left + tile] = acc_ref[
                    row, col
                ].astype(BF16)


def partial_kernel(even_ref, odd_ref, own_ref, next_ref, *out_refs, first):
    rows = even_ref.shape[0]
    for m, out_ref in enumerate(out_refs):
        span = slice(m * rows, (m + 1) * rows)
        far = slice((first + m) * rows, (first + m + 1) * rows)
        block = contract_rows(even_ref[:, far], own_ref[...])
        block += contract_rows(odd_ref[:, span], next_ref[...])
        out_ref[...] = block.astype(out_ref.dtype)


def near_kernel(keep_ref, first_ref, second_ref, third_ref, out_ref):
    quarter = out_ref.shape[2]
    for q in range(out_ref.shape[0]):
        span = slice(q * quarter, (q + 1) * quarter)
        total = keep_ref[:, span] + first_ref[:, span].astype(F32)
        total += second_ref[:, span].astype(F32) + third_ref[:, span].astype(F32)
        out_ref[q] = total.astype(BF16)


def weight_kernel(*refs, scale):
    *in_refs, feat_ref, p_ref, gw_ref = refs
    total = in_refs[0][...].astype(F32)
    for in_ref in in_refs[1:]:
        total += in_ref[...].astype(F32)
    p_ref[...] = total.astype(BF16)
    gw_ref[...] = (contract_rows(p_ref[...], feat_ref[...]) * scale).astype(BF16)


def feature_kernel(p_ref, weight_ref, out_ref):
    quarter = p_ref.shape[2]
    rows = out_ref.shape[0]
    total = jnp.zeros(out_ref.shape, F32)
    for q in range(p_ref.shape[0]):
        total += jnp.dot(
            p_ref[q, :rows, :],
            weight_ref[q * quarter : (q + 1) * quarter, :],
            preferred_element_type=F32,
        )
    out_ref[...] = total.astype(BF16)


def whole(kernel, outs, scalars, arrays, scratch=()):
    return pl.pallas_call(
        kernel,
        in_specs=[pl.BlockSpec(memory_space=pltpu.SMEM)] * len(scalars)
        + [pl.BlockSpec(memory_space=pltpu.VMEM)] * len(arrays),
        out_specs=jax.tree.map(lambda _: pl.BlockSpec(memory_space=pltpu.VMEM), outs),
        out_shape=outs,
        scratch_shapes=scratch,
        compiler_params=pltpu.CompilerParams(vmem_limit_bytes=VMEM_LIMIT),
    )(*scalars, *arrays)


def exchange(value, axes):
    return lax.all_to_all(value, axes, 0, 0)


def move(value, axes, count, shift):
    return lax.ppermute(value, axes, [(i, (i + shift) % count) for i in range(count)])


def shards(features, pre_act, upstream, weight, tile_values, tile_rows, tile_cols, tile_count):
    _, steps, slots, tile, _ = tile_values.shape
    nodes, width = features.shape
    hidden = upstream.shape[1]
    quarter = hidden // REP
    scale = float(nodes * ZH * ZL * YL) ** -0.5
    ring = functools.partial(move, axes=BLK, count=ZH * ZL * YL)
    column = functools.partial(move, axes=("zh", "zl"), count=ZH * ZL)
    shape = jax.ShapeDtypeStruct

    spread = np.zeros((hidden, hidden), np.float32)
    spread[hidden_order(hidden), np.arange(hidden)] = 1.0
    spread = jnp.asarray(spread, BF16)
    grad_out = jnp.where(pre_act > 0, upstream, jnp.zeros_like(upstream))
    own = jnp.dot(grad_out, spread, preferred_element_type=F32).astype(BF16)
    weight = contract_rows(spread, weight).astype(BF16)

    def dense(places):
        return whole(
            functools.partial(dense_kernel, places=places),
            shape((2 * tile, len(places) * 2 * tile), BF16),
            (tile_rows.transpose(2, 0, 1), tile_cols.transpose(2, 0, 1), tile_count),
            (tile_values,),
            (pltpu.VMEM((2, 2, tile, tile), F32),),
        )

    following = ring(own, shift=-1)
    odd_high = ring(dense((5, 7)), shift=-1)
    odd_low = ring(dense((1, 3)), shift=-1)
    even = dense((0, 2, 4, 6))
    block = shape((nodes, hidden), BF16)
    second, third = whole(
        functools.partial(partial_kernel, first=2),
        (block, block),
        (),
        (even, odd_high, own, following),
    )
    third = column(third, shift=-2)
    second = column(second, shift=-1)
    zeroth, keep = whole(
        functools.partial(partial_kernel, first=0),
        (block, shape((nodes, hidden), F32)),
        (),
        (even, odd_low, own, following),
    )
    zeroth = column(zeroth, shift=1)
    parts = whole(
        near_kernel,
        shape((REP, nodes, quarter), BF16),
        (),
        (keep, third, second, zeroth),
    )
    parts = exchange(parts, "rep")
    parts = [column(parts[r], shift=-1 - ZL * r) for r in (2, 1, 3, 0)]
    p_quarter, gw = whole(
        functools.partial(weight_kernel, scale=scale),
        (shape((nodes, quarter), BF16), shape((quarter, width), BF16)),
        (),
        (*parts, features),
    )
    gw = exchange(gw.reshape(ZH * ZL * YL, -1, width), BLK)
    gw = jnp.sum(gw.astype(F32), axis=0)
    high = lax.reduce_precision(gw, 8, 7)
    gw_rows = gw.size // quarter
    packed = jnp.concatenate(
        [
            p_quarter,
            high.astype(BF16).reshape(gw_rows, quarter),
            (gw - high).astype(BF16).reshape(gw_rows, quarter),
        ]
    )
    packed = exchange(jnp.broadcast_to(packed[None], (REP,) + packed.shape), "rep")
    grad_feat = whole(feature_kernel, shape((nodes, width), BF16), (), (packed, weight))
    high = packed[:, nodes : nodes + gw_rows].astype(F32)
    low = packed[:, nodes + gw_rows :].astype(F32)
    return grad_feat, (high + low).reshape(-1, width)


def solution(mesh):
    dp = mesh.shape["dp"]
    fine = Mesh(mesh.devices.reshape(dp, REP, ZH, ZL, YL), ("dp", "rep") + BLK)
    rows = ("dp",) + BLK
    return jax.shard_map(
        shards,
        mesh=fine,
        in_specs=(
            P(rows, None),
            P(rows, None),
            P(rows, None),
            P(),
            P(rows, "rep", None, None, None),
            P(rows, "rep", None),
            P(rows, "rep", None),
            P(rows, "rep"),
        ),
        out_specs=(P(rows, None), P(rows, None)),
        check_vma=False,
    )
```

time: 140 us -> 123 us (0.88)
  starting transfers between devices: 28.9 us -> 52.8 us
  blocking collectives: 55 us -> 36.6 us
  waiting for transfers between devices: 36.3 us -> 20.9 us
  Pallas kernels: 11.3 us -> 5.04 us
    ppermute x2 -> x10, starting transfers between devices: 14.8 us -> 49.3 us  [move(): lax.ppermute(value, axes, [(i, (i + shift) % count) for i in range(count)])]
    all_to_all x2 -> x1, waiting for transfers between devices: 33.2 us -> 6.34 us  [exchange(): return lax.all_to_all(value, axes, 0, 0)]
    all_to_all x3 -> x2, blocking collectives: 55 us -> 36.6 us  [exchange(): return lax.all_to_all(value, axes, 0, 0)]
    ppermute x2 -> x10, waiting for transfers between devices: 3.08 us -> 14.5 us  [move(): lax.ppermute(value, axes, [(i, (i + shift) % count) for i in range(count)])]
    all_to_all x2 -> x1, starting transfers between devices: 14.1 us -> 3.45 us  [exchange(): return lax.all_to_all(value, axes, 0, 0)]
    pallas_call x2 -> x0, Pallas kernels: 8.07 us -> none  [dense_steps(): pl.pallas_call(functools.partial(dense_kernel, odd=odd), grid_spec=pltpu....]
    pallas_call x4 -> x8, Pallas kernels: 3.2 us -> 5.04 us  [whole(): pl.pallas_call(kernel, in_specs=[pl.BlockSpec(memory_space=pltpu.SMEM)] *...]
    unnamed x14 -> x18, local copies, waits for them, and re-layouts: 2.7 us -> 3.51 us
  transfers between devices with their start and end apart: 4 -> 11, of which waited for: 3 -> 7; matrix products, arithmetic and copies ran while one was open for 1% -> 1% of each run, Pallas kernels for 3% -> 2%
where the time goes in v2:
time: 123 us; the launch traced here: 122 us
  starting transfers between devices  52.8 us (43%)
  blocking collectives  36.6 us (30%)
  waiting for transfers between devices  20.9 us (17%)
  Pallas kernels  5.04 us (4%)
  local copies, waits for them, and re-layouts  4.95 us (4%)
    ppermute x10, starting transfers between devices, move(): lax.ppermute(value, axes, [(i, (i + shift) % count) for i in range(count)])  49.3 us
    all_to_all x2, blocking collectives, exchange(): return lax.all_to_all(value, axes, 0, 0)  36.6 us
    ppermute x10, waiting for transfers between devices, move(): lax.ppermute(value, axes, [(i, (i + shift) % count) for i in range(count)])  14.5 us
    all_to_all x1, waiting for transfers between devices, exchange(): return lax.all_to_all(value, axes, 0, 0)  6.34 us
    pallas_call x8, Pallas kernels, whole(): pl.pallas_call(kernel, in_specs=[pl.BlockSpec(memory_space=pltpu.SMEM)] *...  5.04 us
    unnamed x18, local copies, waits for them, and re-layouts  3.51 us
    all_to_all x1, starting transfers between devices, exchange(): return lax.all_to_all(value, axes, 0, 0)  3.45 us
  transfers between devices with their start and end apart: 11, of which 7 were waited for; matrix products, arithmetic and copies ran while one was open for 1% of the time, Pallas kernels for 2%

profile of v2, /device:TPU:24, one launch (start us, length us, event | category | flops | bytes accessed | tf_op | source)
XLA Modules:
  0.0 121.9 jit_solution(18238661107257229621)
XLA Ops:
  0.6 0.0 copy-start
  0.6 0.0 copy-start.1
  0.7 1.5 %copy-done.1 = bf16[1,8,6,128,128]{4,3,2,1,0:T(8,128)(2,1)S(1)} copy-done((bf16[1,8,6,128,128]{4,3,2,1,0:T(8,128)(2,1)S(1)}, bf16[1,8,6,128,128]{4,3,2,1,0:T(8,128)(2,1)}, u32[]{:S(2)}) %copy-start.1) | copy-done | bytes 1572888
  2.1 0.0 copy-start.3
  2.1 0.7 copy-done.3
  2.8 0.0 copy-start.4
  2.8 0.7 copy-done.4
  3.5 0.0 copy-start.5
  3.5 0.7 copy-done.5
  4.1 0.0 copy-start.6
  4.1 0.0 copy-start.7
  4.1 0.0 copy-start.8
  4.1 0.8 shard_map.107
  5.0 2.6 %collective-permute-start.2 = (bf16[256,512]{1,0:T(8,128)(2,1)S(1)}, bf16[256,512]{1,0:T(8,128)(2,1)S(1)}, u32[]{:S(2)}, u32[]{:S(2)}) collective-permute-start(bf16[256,512]{1,0:T(8,128)(2,1)S(1)} %shard_map.107), channel_id=1, source_target_pairs={{0,31},{1,0},{2,1},{3,2},{4,3},{5,4},{6,5},{7,6},{8,7},{9,8},{10,9... | collective-permute-start | bytes 786440 | tf_op jit(solution)/shard_map/ppermute | solution.py:104
  7.6 0.0 copy-done.6
  7.6 0.0 copy-done.7
  7.6 0.0 copy-done.8
  7.6 0.3 convolution_convert_fusion.1.own_ref
  7.9 12.1 %collective-permute-start.1 = (bf16[256,512]{1,0:T(8,128)(2,1)S(1)}, bf16[256,512]{1,0:T(8,128)(2,1)S(1)}, u32[]{:S(2)}, u32[]{:S(2)}) collective-permute-start(bf16[256,512]{1,0:T(8,128)(2,1)S(1)} %convolution_convert_fusion.1.own_ref), channel_id=1, source_target_pairs={{0,31},{1,0},{2,1},{3,2},{4,3},{5,4},{6,5},{7,6},{8,7},{9,8},{10,9... | collective-permute-start | bytes 786440 | tf_op jit(solution)/shard_map/ppermute | solution.py:104
  20.1 0.8 shard_map.105
  20.9 2.7 %collective-permute-start = (bf16[256,512]{1,0:T(8,128)(2,1)S(1)}, bf16[256,512]{1,0:T(8,128)(2,1)S(1)}, u32[]{:S(2)}, u32[]{:S(2)}) collective-permute-start(bf16[256,512]{1,0:T(8,128)(2,1)S(1)} %shard_map.105), channel_id=1, source_target_pairs={{0,31},{1,0},{2,1},{3,2},{4,3},{5,4},{6,5},{7,6},{8,7},{9,8},{10,9... | collective-permute-start | bytes 786440 | tf_op jit(solution)/shard_map/ppermute | solution.py:104
  23.5 1.0 shard_map.104.even_ref
  24.6 0.0 collective-permute-done.2.odd_ref
  24.6 2.2 %collective-permute-done.1.next_ref = bf16[256,512]{1,0:T(8,128)(2,1)S(1)} collective-permute-done((bf16[256,512]{1,0:T(8,128)(2,1)S(1)}, bf16[256,512]{1,0:T(8,128)(2,1)S(1)}, u32[]{:S(2)}, u32[]{:S(2)}) %collective-permute-start.1) | collective-permute-done | bytes 262176 | tf_op jit(solution)/shard_map/ppermute | solution.py:104
  26.8 0.5 shard_map.108
  27.2 7.6 %collective-permute-start.3 = (bf16[256,512]{1,0:T(8,128)(2,1)S(1)}, bf16[256,512]{1,0:T(8,128)(2,1)S(1)}, u32[]{:S(2)}, u32[]{:S(2)}) collective-permute-start(bf16[256,512]{1,0:T(8,128)(2,1)S(1)} %get-tuple-element.9), channel_id=1, source_target_pairs={{0,28},{2,30},{4,0},{6,2},{8,4},{10,6},{12,8},{14,10},{16,12},{18,... | collective-permute-start | bytes 786440 | tf_op jit(solution)/shard_map/ppermute | solution.py:104
  34.9 2.9 %collective-permute-start.4 = (bf16[256,512]{1,0:T(8,128)(2,1)S(1)}, bf16[256,512]{1,0:T(8,128)(2,1)S(1)}, u32[]{:S(2)}, u32[]{:S(2)}) collective-permute-start(bf16[256,512]{1,0:T(8,128)(2,1)S(1)} %get-tuple-element.10), channel_id=1, source_target_pairs={{0,30},{2,0},{4,2},{6,4},{8,6},{10,8},{12,10},{14,12},{16,14},{18,... | collective-permute-start | bytes 786440 | tf_op jit(solution)/shard_map/ppermute | solution.py:104
  37.8 0.0 collective-permute-done.odd_ref
  37.8 0.5 shard_map.106
  38.3 0.0 copy-start.2
  38.3 3.3 %collective-permute-start.5 = (bf16[256,512]{1,0:T(8,128)(2,1)S(1)}, bf16[256,512]{1,0:T(8,128)(2,1)S(1)}, u32[]{:S(2)}, u32[]{:S(2)}) collective-permute-start(bf16[256,512]{1,0:T(8,128)(2,1)S(1)} %get-tuple-element.11), channel_id=1, source_target_pairs={{0,2},{2,4},{4,6},{6,8},{8,10},{10,12},{12,14},{14,16},{16,18},{18... | collective-permute-start | bytes 786440 | tf_op jit(solution)/shard_map/ppermute | solution.py:104
  41.5 4.7 %collective-permute-done.3.first_ref = bf16[256,512]{1,0:T(8,128)(2,1)S(1)} collective-permute-done((bf16[256,512]{1,0:T(8,128)(2,1)S(1)}, bf16[256,512]{1,0:T(8,128)(2,1)S(1)}, u32[]{:S(2)}, u32[]{:S(2)}) %collective-permute-start.3) | collective-permute-done | bytes 262176 | tf_op jit(solution)/shard_map/ppermute | solution.py:104
  46.2 3.4 %collective-permute-done.4.second_ref = bf16[256,512]{1,0:T(8,128)(2,1)S(1)} collective-permute-done((bf16[256,512]{1,0:T(8,128)(2,1)S(1)}, bf16[256,512]{1,0:T(8,128)(2,1)S(1)}, u32[]{:S(2)}, u32[]{:S(2)}) %collective-permute-start.4) | collective-permute-done | bytes 262176 | tf_op jit(solution)/shard_map/ppermute | solution.py:104
  49.6 0.0 collective-permute-done.5.third_ref
  49.6 0.1 shard_map.109
  49.8 10.8 %all_to_all.15 = bf16[4,256,128]{2,1,0:T(8,128)(2,1)S(1)} all-to-all(bf16[4,256,128]{2,1,0:T(8,128)(2,1)S(1)} %shard_map.109), channel_id=1, replica_groups=mesh['dp'=4,'rep'=4,'zh'=4,'zl'=4,'yl'=2] {'rep'}, dimensions={0} | all-to-all | bytes 524288 | tf_op jit(solution)/shard_map/all_to_all | solution.py:100
  60.6 7.0 %collective-permute-start.6 = (bf16[256,128]{1,0:T(8,128)(2,1)S(1)}, bf16[256,128]{1,0:T(8,128)(2,1)S(1)}, u32[]{:S(2)}, u32[]{:S(2)}) collective-permute-start(bf16[256,128]{1,0:T(8,128)(2,1)S(1)} %get-tuple-element.17), channel_id=1, source_target_pairs={{0,14},{2,16},{4,18},{6,20},{8,22},{10,24},{12,26},{14,28},{16,30}... | collective-permute-start | bytes 196616 | tf_op jit(solution)/shard_map/ppermute | solution.py:104
  67.6 4.0 %collective-permute-start.7 = (bf16[256,128]{1,0:T(8,128)(2,1)S(1)}, bf16[256,128]{1,0:T(8,128)(2,1)S(1)}, u32[]{:S(2)}, u32[]{:S(2)}) collective-permute-start(bf16[256,128]{1,0:T(8,128)(2,1)S(1)} %get-tuple-element.16), channel_id=1, source_target_pairs={{0,22},{2,24},{4,26},{6,28},{8,30},{10,0},{12,2},{14,4},{16,6},{18... | collective-permute-start | bytes 196616 | tf_op jit(solution)/shard_map/ppermute | solution.py:104
  71.6 3.1 %collective-permute-start.8 = (bf16[256,128]{1,0:T(8,128)(2,1)S(1)}, bf16[256,128]{1,0:T(8,128)(2,1)S(1)}, u32[]{:S(2)}, u32[]{:S(2)}) collective-permute-start(bf16[256,128]{1,0:T(8,128)(2,1)S(1)} %get-tuple-element.15), channel_id=1, source_target_pairs={{0,6},{2,8},{4,10},{6,12},{8,14},{10,16},{12,18},{14,20},{16,22},{... | collective-permute-start | bytes 196616 | tf_op jit(solution)/shard_map/ppermute | solution.py:104
  74.7 4.1 %collective-permute-start.9 = (bf16[256,128]{1,0:T(8,128)(2,1)S(1)}, bf16[256,128]{1,0:T(8,128)(2,1)S(1)}, u32[]{:S(2)}, u32[]{:S(2)}) collective-permute-start(bf16[256,128]{1,0:T(8,128)(2,1)S(1)} %get-tuple-element.14), channel_id=1, source_target_pairs={{0,30},{2,0},{4,2},{6,4},{8,6},{10,8},{12,10},{14,12},{16,14},{18,... | collective-permute-start | bytes 196616 | tf_op jit(solution)/shard_map/ppermute | solution.py:104
  78.7 0.0 collective-permute-done.6.refs_0_
  78.7 0.3 collective-permute-done.7.refs_1_
  79.1 2.7 %collective-permute-done.8.refs_2_ = bf16[256,128]{1,0:T(8,128)(2,1)S(1)} collective-permute-done((bf16[256,128]{1,0:T(8,128)(2,1)S(1)}, bf16[256,128]{1,0:T(8,128)(2,1)S(1)}, u32[]{:S(2)}, u32[]{:S(2)}) %collective-permute-start.8) | collective-permute-done | bytes 65568 | tf_op jit(solution)/shard_map/ppermute | solution.py:104
  81.8 1.2 collective-permute-done.9.refs_3_
  83.0 0.0 copy-done.2
  83.0 0.2 shard_map.110
  83.3 25.8 %all_to_all.16 = bf16[32,4,512]{2,1,0:T(4,128)(2,1)S(1)} all-to-all(bf16[32,4,512]{2,1,0:T(4,128)(2,1)S(1)} %reshape.15), channel_id=1, replica_groups=mesh['dp'=4,'rep'=4,'zh'=4,'zl'=4,'yl'=2] {'zh','zl','yl'}, dimensions={0} | all-to-all | bytes 262144 | tf_op jit(solution)/shard_map/all_to_all | solution.py:100
  109.0 0.1 convert_reduce_fusion
  109.1 0.8 broadcast_in_dim.2
  109.9 3.5 %all-to-all-start.2 = ((bf16[4,288,128]{2,1,0:T(8,128)(2,1)}), bf16[4,288,128]{2,1,0:T(8,128)(2,1)S(1)}, u32[]{:S(2)}, u32[]{:S(2)}) async-start(bf16[4,288,128]{2,1,0:T(8,128)(2,1)} %broadcast_in_dim.2), calls=%async_computation.2 | async-start | bytes 589824 | tf_op jit(solution)/shard_map/all_to_all | solution.py:100
  113.3 0.0 copy-done
  113.3 0.5 convolution_convert_fusion.weight_ref
  113.8 6.3 %all-to-all-done.2.p_ref = bf16[4,288,128]{2,1,0:T(8,128)(2,1)S(1)} async-done(((bf16[4,288,128]{2,1,0:T(8,128)(2,1)}), bf16[4,288,128]{2,1,0:T(8,128)(2,1)S(1)}, u32[]{:S(2)}, u32[]{:S(2)}) %all-to-all-start.2) | async-done | bytes 294944 | tf_op jit(solution)/shard_map/all_to_all | solution.py:100
  120.2 0.6 reshape.16
  120.8 1.1 shard_map.111
  (6 shorter events, 0.1 us)
Async XLA Ops:
  0.6 112.7 %copy-start = (bf16[512,512]{1,0:T(8,128)(2,1)S(1)}, bf16[512,512]{1,0:T(8,128)(2,1)}, u32[]{:S(2)}) copy-start(bf16[512,512]{1,0:T(8,128)(2,1)} %param.12) | copy-start | bytes 1572868
  0.6 1.5 %copy-start.1 = (bf16[1,8,6,128,128]{4,3,2,1,0:T(8,128)(2,1)S(1)}, bf16[1,8,6,128,128]{4,3,2,1,0:T(8,128)(2,1)}, u32[]{:S(2)}) copy-start(bf16[1,8,6,128,128]{4,3,2,1,0:T(8,128)(2,1)} %tiles_ref.5) | copy-start | bytes 4718596
  2.1 0.7 copy-start.3
  2.8 0.7 copy-start.4
  3.5 0.7 copy-start.5
  4.1 3.5 %copy-start.6 = (bf16[256,512]{1,0:T(8,128)(2,1)S(1)}, bf16[256,512]{1,0:T(8,128)(2,1)}, u32[]{:S(2)}) copy-start(bf16[256,512]{1,0:T(8,128)(2,1)} %param.11) | copy-start | bytes 786436
  4.1 3.5 %copy-start.7 = (bf16[256,512]{1,0:T(8,128)(2,1)S(1)}, bf16[256,512]{1,0:T(8,128)(2,1)}, u32[]{:S(2)}) copy-start(bf16[256,512]{1,0:T(8,128)(2,1)} %param.10) | copy-start | bytes 786436
  4.1 3.5 %copy-start.8 = (bf16[512,512]{1,0:T(8,128)(2,1)S(1)}, bf16[512,512]{1,0:T(8,128)(2,1)}, u32[]{:S(2)}) copy-start(bf16[512,512]{1,0:T(8,128)(2,1)} %constant.6.clone) | copy-start | bytes 1572868
  5.0 19.6 %collective-permute-start.2 = (bf16[256,512]{1,0:T(8,128)(2,1)S(1)}, bf16[256,512]{1,0:T(8,128)(2,1)S(1)}, u32[]{:S(2)}, u32[]{:S(2)}) collective-permute-start(bf16[256,512]{1,0:T(8,128)(2,1)S(1)} %shard_map.107), channel_id=1, source_target_pairs={{0,31},{1,0},{2,1},{3,2},{4,3},{5,4},{6,5},{7,6},{8,7},{9,8},{10,9... | collective-permute-start | bytes 786440 | tf_op jit(solution)/shard_map/ppermute | solution.py:104
  7.9 18.9 %collective-permute-start.1 = (bf16[256,512]{1,0:T(8,128)(2,1)S(1)}, bf16[256,512]{1,0:T(8,128)(2,1)S(1)}, u32[]{:S(2)}, u32[]{:S(2)}) collective-permute-start(bf16[256,512]{1,0:T(8,128)(2,1)S(1)} %convolution_convert_fusion.1.own_ref), channel_id=1, source_target_pairs={{0,31},{1,0},{2,1},{3,2},{4,3},{5,4},{6,5},{7,6},{8,7},{9,8},{10,9... | collective-permute-start | bytes 786440 | tf_op jit(solution)/shard_map/ppermute | solution.py:104
  20.9 16.9 %collective-permute-start = (bf16[256,512]{1,0:T(8,128)(2,1)S(1)}, bf16[256,512]{1,0:T(8,128)(2,1)S(1)}, u32[]{:S(2)}, u32[]{:S(2)}) collective-permute-start(bf16[256,512]{1,0:T(8,128)(2,1)S(1)} %shard_map.105), channel_id=1, source_target_pairs={{0,31},{1,0},{2,1},{3,2},{4,3},{5,4},{6,5},{7,6},{8,7},{9,8},{10,9... | collective-permute-start | bytes 786440 | tf_op jit(solution)/shard_map/ppermute | solution.py:104
  27.2 19.0 %collective-permute-start.3 = (bf16[256,512]{1,0:T(8,128)(2,1)S(1)}, bf16[256,512]{1,0:T(8,128)(2,1)S(1)}, u32[]{:S(2)}, u32[]{:S(2)}) collective-permute-start(bf16[256,512]{1,0:T(8,128)(2,1)S(1)} %get-tuple-element.9), channel_id=1, source_target_pairs={{0,28},{2,30},{4,0},{6,2},{8,4},{10,6},{12,8},{14,10},{16,12},{18,... | collective-permute-start | bytes 786440 | tf_op jit(solution)/shard_map/ppermute | solution.py:104
  34.9 14.7 %collective-permute-start.4 = (bf16[256,512]{1,0:T(8,128)(2,1)S(1)}, bf16[256,512]{1,0:T(8,128)(2,1)S(1)}, u32[]{:S(2)}, u32[]{:S(2)}) collective-permute-start(bf16[256,512]{1,0:T(8,128)(2,1)S(1)} %get-tuple-element.10), channel_id=1, source_target_pairs={{0,30},{2,0},{4,2},{6,4},{8,6},{10,8},{12,10},{14,12},{16,14},{18,... | collective-permute-start | bytes 786440 | tf_op jit(solution)/shard_map/ppermute | solution.py:104
  38.3 44.7 %copy-start.2 = (bf16[256,512]{1,0:T(8,128)(2,1)S(1)}, bf16[256,512]{1,0:T(8,128)(2,1)}, u32[]{:S(2)}) copy-start(bf16[256,512]{1,0:T(8,128)(2,1)} %refs_4_.1) | copy-start | bytes 786436
  38.3 11.3 %collective-permute-start.5 = (bf16[256,512]{1,0:T(8,128)(2,1)S(1)}, bf16[256,512]{1,0:T(8,128)(2,1)S(1)}, u32[]{:S(2)}, u32[]{:S(2)}) collective-permute-start(bf16[256,512]{1,0:T(8,128)(2,1)S(1)} %get-tuple-element.11), channel_id=1, source_target_pairs={{0,2},{2,4},{4,6},{6,8},{8,10},{10,12},{12,14},{14,16},{16,18},{18... | collective-permute-start | bytes 786440 | tf_op jit(solution)/shard_map/ppermute | solution.py:104
  60.6 18.1 %collective-permute-start.6 = (bf16[256,128]{1,0:T(8,128)(2,1)S(1)}, bf16[256,128]{1,0:T(8,128)(2,1)S(1)}, u32[]{:S(2)}, u32[]{:S(2)}) collective-permute-start(bf16[256,128]{1,0:T(8,128)(2,1)S(1)} %get-tuple-element.17), channel_id=1, source_target_pairs={{0,14},{2,16},{4,18},{6,20},{8,22},{10,24},{12,26},{14,28},{16,30}... | collective-permute-start | bytes 196616 | tf_op jit(solution)/shard_map/ppermute | solution.py:104
  67.6 11.5 %collective-permute-start.7 = (bf16[256,128]{1,0:T(8,128)(2,1)S(1)}, bf16[256,128]{1,0:T(8,128)(2,1)S(1)}, u32[]{:S(2)}, u32[]{:S(2)}) collective-permute-start(bf16[256,128]{1,0:T(8,128)(2,1)S(1)} %get-tuple-element.16), channel_id=1, source_target_pairs={{0,22},{2,24},{4,26},{6,28},{8,30},{10,0},{12,2},{14,4},{16,6},{18... | collective-permute-start | bytes 196616 | tf_op jit(solution)/shard_map/ppermute | solution.py:104
  71.6 10.2 %collective-permute-start.8 = (bf16[256,128]{1,0:T(8,128)(2,1)S(1)}, bf16[256,128]{1,0:T(8,128)(2,1)S(1)}, u32[]{:S(2)}, u32[]{:S(2)}) collective-permute-start(bf16[256,128]{1,0:T(8,128)(2,1)S(1)} %get-tuple-element.15), channel_id=1, source_target_pairs={{0,6},{2,8},{4,10},{6,12},{8,14},{10,16},{12,18},{14,20},{16,22},{... | collective-permute-start | bytes 196616 | tf_op jit(solution)/shard_map/ppermute | solution.py:104
  74.7 8.3 %collective-permute-start.9 = (bf16[256,128]{1,0:T(8,128)(2,1)S(1)}, bf16[256,128]{1,0:T(8,128)(2,1)S(1)}, u32[]{:S(2)}, u32[]{:S(2)}) collective-permute-start(bf16[256,128]{1,0:T(8,128)(2,1)S(1)} %get-tuple-element.14), channel_id=1, source_target_pairs={{0,30},{2,0},{4,2},{6,4},{8,6},{10,8},{12,10},{14,12},{16,14},{18,... | collective-permute-start | bytes 196616 | tf_op jit(solution)/shard_map/ppermute | solution.py:104
  109.9 10.3 %all-to-all-start.2 = ((bf16[4,288,128]{2,1,0:T(8,128)(2,1)}), bf16[4,288,128]{2,1,0:T(8,128)(2,1)S(1)}, u32[]{:S(2)}, u32[]{:S(2)}) async-start(bf16[4,288,128]{2,1,0:T(8,128)(2,1)} %broadcast_in_dim.2), calls=%async_computation.2 | async-start | bytes 589824 | tf_op jit(solution)/shard_map/all_to_all | solution.py:100

commit v3 on v2

v3 whole, which is shorter than its diff:
```python
import functools

import jax
import jax.numpy as jnp
import numpy as np
from jax import lax
from jax.experimental import pallas as pl
from jax.experimental.pallas import tpu as pltpu
from jax.sharding import Mesh, PartitionSpec as P

ZH, ZL, YL, REP = 4, 4, 2, 4
BLK = ("zh", "zl", "yl")
BF16, F32 = jnp.bfloat16, jnp.float32


def contract_rows(left, right):
    return lax.dot_general(left, right, (((0,), (0,)), ((), ())), preferred_element_type=F32)


def hidden_order(width):
    units = np.arange(width).reshape(ZH * ZL * YL, REP, -1)
    return units.transpose(1, 2, 0).reshape(-1)


def dense_kernel(lane_ref, tiles_ref, *refs, places, masked):
    lists, refs = refs[:3], refs[3:]
    if masked:
        (pre_ref, up_ref, own_ref, *refs) = refs
        (*refs, pre_held, up_held, own_sems) = refs
        inputs = [
            pltpu.make_async_copy(source, held, own_sems.at[at])
            for at, (source, held) in enumerate(((pre_ref, pre_held), (up_ref, up_held)))
        ]
        for copy in inputs:
            copy.start()
    out_ref, rows_ref, cols_ref, count_ref, held_ref, acc_ref, sems, list_sems = refs
    _, slots, tile, _ = held_ref.shape
    fetches = [
        pltpu.make_async_copy(source, held, list_sems.at[at])
        for at, (source, held) in enumerate(zip(lists, (rows_ref, cols_ref, count_ref)))
    ]
    for fetch in fetches:
        fetch.start()
    last = tiles_ref.shape[1] // 2 - 1
    mirrored = lane_ref[0] >= REP // 2
    steps = [2 * jnp.where(mirrored, last - m, m) + odd for m, odd in places]
    copies = [
        pltpu.make_async_copy(tiles_ref.at[0, step], held_ref.at[at], sems.at[at])
        for at, step in enumerate(steps)
    ]
    for copy in copies:
        copy.start()
    if masked:
        for copy in inputs:
            copy.wait()
        own_ref[...] = jnp.where(pre_held[...] > 0, up_held[...], jnp.zeros_like(up_held))
    for fetch in fetches:
        fetch.wait()
    for at, step in enumerate(steps):
        acc_ref[...] = jnp.zeros_like(acc_ref)
        live = count_ref[0, step]
        copies[at].wait()
        for q in range(slots):

            @pl.when(q < live)
            def _():
                row, col = rows_ref[q, 0, step], cols_ref[q, 0, step]
                acc_ref[row, col] += held_ref[at, q].astype(F32)

        for row in range(2):
            for col in range(2):
                left = (2 * at + col) * tile
                out_ref[row * tile : (row + 1) * tile, left : left + tile] = acc_ref[
                    row, col
                ].astype(BF16)


def partial_kernel(even_ref, odd_ref, own_ref, next_ref, *out_refs, first):
    rows = even_ref.shape[0]
    for m, out_ref in enumerate(out_refs):
        span = slice(m * rows, (m + 1) * rows)
        far = slice((first + m) * rows, (first + m + 1) * rows)
        block = contract_rows(even_ref[:, far], own_ref[...])
        block += contract_rows(odd_ref[:, span], next_ref[...])
        out_ref[...] = block.astype(out_ref.dtype)


def near_kernel(keep_ref, first_ref, second_ref, third_ref, spread_ref, out_ref):
    total = keep_ref[...] + first_ref[...].astype(F32)
    total += second_ref[...].astype(F32) + third_ref[...].astype(F32)
    low = total.astype(BF16)
    quarter = out_ref.shape[2]
    for q in range(REP):
        span = slice(q * quarter, (q + 1) * quarter)
        out_ref[q] = jnp.dot(
            low, spread_ref[:, span], preferred_element_type=F32
        ).astype(BF16)


def weight_kernel(*refs, scale):
    *in_refs, feat_ref, p_ref, gw_ref, lines_ref = refs
    total = in_refs[0][...].astype(F32)
    for in_ref in in_refs[1:]:
        total += in_ref[...].astype(F32)
    p_ref[...] = total.astype(BF16)
    gw = contract_rows(p_ref[...], feat_ref[...]) * scale
    quarter = lines_ref.shape[1]
    spots = ZH * ZL * YL
    rows, pieces = gw.shape[0] // spots, gw.shape[1] // quarter
    for i in range(rows):
        for f in range(pieces):
            lines_ref[pl.ds(i * pieces + f, spots, rows * pieces), :] = gw[
                i * spots : (i + 1) * spots, f * quarter : (f + 1) * quarter
            ]
    gw_ref[...] = lines_ref[...].astype(BF16)


def pack_kernel(p_ref, gw_ref, out_ref):
    nodes, rows = p_ref.shape[0], gw_ref.shape[1]
    total = gw_ref[0].astype(F32)
    for d in range(1, gw_ref.shape[0]):
        total += gw_ref[d].astype(F32)
    high = total.astype(BF16)
    low = (total - high.astype(F32)).astype(BF16)
    for r in range(out_ref.shape[0]):
        out_ref[r, :nodes] = p_ref[...]
        out_ref[r, nodes : nodes + rows] = high
        out_ref[r, nodes + rows :] = low


def last_kernel(in_ref, weight_ref, feat_ref, gw_ref):
    nodes, width = feat_ref.shape
    quarter = in_ref.shape[2]
    lines = (in_ref.shape[1] - nodes) // 2
    pieces = width // quarter
    total = jnp.zeros(feat_ref.shape, F32)
    for q in range(REP):
        total += jnp.dot(
            in_ref[q, :nodes],
            weight_ref[q * quarter : (q + 1) * quarter, :],
            preferred_element_type=F32,
        )
        gw = in_ref[q, nodes : nodes + lines].astype(F32) + in_ref[q, nodes + lines :].astype(F32)
        for at in range(lines):
            row = q * (lines // pieces) + at // pieces
            left = at % pieces * quarter
            gw_ref[row : row + 1, left : left + quarter] = gw[at : at + 1, :]
    feat_ref[...] = total.astype(BF16)


def whole(kernel, outs, scalars, arrays, scratch=(), space=pltpu.VMEM, limit=48):
    return pl.pallas_call(
        kernel,
        in_specs=[pl.BlockSpec(memory_space=pltpu.SMEM)] * len(scalars)
        + [pl.BlockSpec(memory_space=space)] * len(arrays),
        out_specs=jax.tree.map(lambda _: pl.BlockSpec(memory_space=pltpu.VMEM), outs),
        out_shape=outs,
        scratch_shapes=scratch,
        compiler_params=pltpu.CompilerParams(vmem_limit_bytes=limit * 1024 * 1024),
    )(*scalars, *arrays)


def nothing(*refs):
    pass


def held_until(value, other):
    return pl.pallas_call(
        nothing,
        in_specs=[pl.BlockSpec(memory_space=pl.ANY), pl.BlockSpec(memory_space=pltpu.VMEM)],
        out_specs=pl.BlockSpec(memory_space=pl.ANY),
        out_shape=jax.ShapeDtypeStruct(value.shape, value.dtype),
        input_output_aliases={0: 0},
    )(value, other)


def exchange(value, axes):
    return lax.all_to_all(value, axes, 0, 0)


def to_previous(value):
    count = ZH * ZL * YL
    return lax.ppermute(value, BLK, [(b, (b - 1) % count) for b in range(count)])


def along_z(value, shifts):
    count = ZH * ZL
    pairs = [
        (r * count + z, r * count + (z + shift) % count)
        for r, shift in enumerate(shifts)
        for z in range(count)
    ]
    return lax.ppermute(value, ("rep", "zh", "zl"), pairs)


def shards(features, pre_act, upstream, weight, tile_values, tile_rows, tile_cols, tile_count):
    _, steps, slots, tile, _ = tile_values.shape
    nodes, width = features.shape
    hidden = upstream.shape[1]
    quarter = width // REP
    scale = float(nodes * ZH * ZL * YL) ** -0.5
    shape = jax.ShapeDtypeStruct
    lane = lax.axis_index("rep").reshape(1)

    lists = (tile_rows.transpose(2, 0, 1), tile_cols.transpose(2, 0, 1), tile_count)
    block = shape((nodes, hidden), BF16)

    def dense(places, masked=()):
        outs = (shape((2 * tile, len(places) * 2 * tile), BF16),)
        held = [pltpu.VMEM(value.shape, value.dtype) for value in masked]
        return whole(
            functools.partial(dense_kernel, places=places, masked=bool(masked)),
            ((block,) + outs) if masked else outs,
            (lane,),
            (tile_values, *lists, *masked),
            (
                *(pltpu.SMEM(listed.shape, listed.dtype) for listed in lists),
                pltpu.VMEM((len(places), slots, tile, tile), BF16),
                pltpu.VMEM((2, 2, tile, tile), F32),
                pltpu.SemaphoreType.DMA((len(places),)),
                pltpu.SemaphoreType.DMA((len(lists),)),
                *held,
                *((pltpu.SemaphoreType.DMA((len(held),)),) if held else ()),
            ),
            pltpu.HBM,
            60 if masked else 48,
        )

    def partial(odd, first, kinds):
        return whole(
            functools.partial(partial_kernel, first=first),
            tuple(shape((nodes, hidden), kind) for kind in kinds),
            (),
            (even, odd, own, following),
        )

    own, third_odd = dense(((3, 1),), (pre_act, upstream))
    even = dense(((0, 0), (1, 0), (2, 0), (3, 0)))[0]
    rest_odd = dense(((0, 1), (1, 1), (2, 1)))[0]
    following = to_previous(own)
    third_odd = to_previous(third_odd)
    third = partial(third_odd, 3, (BF16,))[0]
    rest_odd = to_previous(held_until(rest_odd, third))
    zeroth, keep, second = partial(rest_odd, 0, (BF16, F32, BF16))
    third = along_z(third, (-2, -2, 2, 2))
    second = along_z(second, (-1, -1, 1, 1))
    zeroth = along_z(zeroth, (1, 1, -1, -1))

    spread = np.zeros((hidden, hidden), np.float32)
    spread[hidden_order(hidden), np.arange(hidden)] = 1.0
    spread = jnp.asarray(spread, BF16)
    weight = contract_rows(spread, weight).astype(BF16)
    parts = whole(
        near_kernel,
        (shape((REP, nodes, quarter), BF16),),
        (),
        (keep, third, second, zeroth, spread),
    )[0]
    parts = exchange(parts, "rep")
    hops = (-1, -5, 6, 2)
    parts = [along_z(parts[r], (hops[r],) * REP) for r in (2, 1, 3, 0)]
    p_quarter, gw = whole(
        functools.partial(weight_kernel, scale=scale),
        (shape((nodes, quarter), BF16), shape((hidden, quarter), BF16)),
        (),
        (*parts, features),
        (pltpu.VMEM((hidden, quarter), F32),),
    )
    gw = exchange(gw.reshape(ZH * ZL * YL, -1, quarter), BLK)
    packed = whole(
        pack_kernel,
        (shape((REP, nodes + 2 * gw.shape[1], quarter), BF16),),
        (),
        (p_quarter, gw),
    )[0]
    packed = exchange(packed, "rep")
    return whole(
        last_kernel,
        (shape((nodes, width), BF16), shape((hidden // (ZH * ZL * YL), width), F32)),
        (),
        (packed, weight),
    )


def solution(mesh):
    dp = mesh.shape["dp"]
    fine = Mesh(mesh.devices.reshape(dp, REP, ZH, ZL, YL), ("dp", "rep") + BLK)
    rows = ("dp",) + BLK
    return jax.shard_map(
        shards,
        mesh=fine,
        in_specs=(
            P(rows, None),
            P(rows, None),
            P(rows, None),
            P(),
            P(rows, "rep", None, None, None),
            P(rows, "rep", None),
            P(rows, "rep", None),
            P(rows, "rep"),
        ),
        out_specs=(P(rows, None), P(rows, None)),
        check_vma=False,
    )
```

time: 123 us -> 133 us (1.081)
  waiting for transfers between devices: 20.9 us -> 30 us
  starting transfers between devices: 52.8 us -> 59.6 us
  blocking collectives: 36.6 us -> 30.8 us
  Pallas kernels: 5.04 us -> 9.11 us
  local copies, waits for them, and re-layouts: 4.95 us -> 1.49 us
    ppermute x10, waiting for transfers between devices: 14.5 us -> 23.7 us  [the longest x7 17.4 us: along_z(): return lax.ppermute(value, ('rep', 'zh', 'zl'), pairs)]
    ppermute x10, starting transfers between devices: 49.3 us -> 56.2 us  [the longest x7 36 us: along_z(): return lax.ppermute(value, ('rep', 'zh', 'zl'), pairs)]
    all_to_all x2, blocking collectives: 36.6 us -> 30.8 us  [exchange(): return lax.all_to_all(value, axes, 0, 0)]
    pallas_call x8 -> x9, Pallas kernels: 5.04 us -> 8.1 us  [whole(): pl.pallas_call(kernel, in_specs=[pl.BlockSpec(memory_space=pltpu.SMEM)] *...]
    unnamed x18 -> x20, local copies, waits for them, and re-layouts: 3.51 us -> 1.47 us
  transfers between devices with their start and end apart: 11 -> 11, of which waited for: 7 -> 5; matrix products, arithmetic and copies ran while one was open for 1% -> 0% of each run, Pallas kernels for 2% -> 2%
where the time goes in v3:
time: 133 us; the launch traced here: 132 us
  starting transfers between devices  59.6 us (45%)
  blocking collectives  30.8 us (23%)
  waiting for transfers between devices  30 us (23%)
  Pallas kernels  9.11 us (7%)
  local copies, waits for them, and re-layouts  1.49 us (1%)
    ppermute x7, starting transfers between devices, along_z(): return lax.ppermute(value, ('rep', 'zh', 'zl'), pairs)  36 us
    all_to_all x2, blocking collectives, exchange(): return lax.all_to_all(value, axes, 0, 0)  30.8 us
    ppermute x3, starting transfers between devices, to_previous(): lax.ppermute(value, BLK, [(b, (b - 1) % count) for b in range(count)])  20.1 us
    ppermute x7, waiting for transfers between devices, along_z(): return lax.ppermute(value, ('rep', 'zh', 'zl'), pairs)  17.4 us
    pallas_call x9, Pallas kernels, whole(): pl.pallas_call(kernel, in_specs=[pl.BlockSpec(memory_space=pltpu.SMEM)] *...  8.1 us
    all_to_all x1, waiting for transfers between devices, exchange(): return lax.all_to_all(value, axes, 0, 0)  6.34 us
    ppermute x3, waiting for transfers between devices, to_previous(): lax.ppermute(value, BLK, [(b, (b - 1) % count) for b in range(count)])  6.23 us
    all_to_all x1, starting transfers between devices, exchange(): return lax.all_to_all(value, axes, 0, 0)  3.45 us
  transfers between devices with their start and end apart: 11, of which 5 were waited for; matrix products, arithmetic and copies ran while one was open for 0% of the time, Pallas kernels for 2%

profile of v3, /device:TPU:24, one launch (start us, length us, event | category | flops | bytes accessed | tf_op | source)
XLA Modules:
  0.0 132.4 jit_solution(10025837141377817279)
XLA Ops:
  0.6 0.0 copy-start
  0.6 0.0 copy-start.9
  0.7 0.0 copy-start.1
  0.7 0.0 copy-start.8
  0.7 0.0 copy-start.7
  0.7 2.1 %shard_map.106 = (bf16[256,512]{1,0:T(8,128)(2,1)}, bf16[256,256]{1,0:T(8,128)(2,1)}) custom-call(s32[1]{0:T(128)} %bitcast.lane_ref, bf16[1,8,6,128,128]{4,3,2,1,0:T(8,128)(2,1)} %tiles_ref.5, s32[6,1,8]{2,1,0:T(1,128)} %bitcast.15, s32[6,1,8]{2,1,0:T(1,128)} %bitcast.18, s32[1,8]{1,0:T(1,128)} %refs_2_.5, bf16[256,512]{1,0:T(8,128)(2,1)} %refs_3_.1, ...), custom_call_target="tpu_custom_call" | custom-call | tf_op jit(solution)/shard_map/pallas_call | solution.py:152
  2.8 2.6 %collective-permute-start.1 = (bf16[256,512]{1,0:T(8,128)(2,1)}, bf16[256,512]{1,0:T(8,128)(2,1)S(1)}, u32[]{:S(2)}, u32[]{:S(2)}) collective-permute-start(bf16[256,512]{1,0:T(8,128)(2,1)} %get-tuple-element.10.own_ref), channel_id=1, source_target_pairs={{0,31},{1,0},{2,1},{3,2},{4,3},{5,4},{6,5},{7,6},{8,7},{9,8},{10,9... | collective-permute-start | bytes 786440 | tf_op jit(solution)/shard_map/ppermute | solution.py:183
  5.4 0.0 copy-start.3
  5.4 12.3 %collective-permute-start = (bf16[256,256]{1,0:T(8,128)(2,1)}, bf16[256,256]{1,0:T(8,128)(2,1)S(1)}, u32[]{:S(2)}, u32[]{:S(2)}) collective-permute-start(bf16[256,256]{1,0:T(8,128)(2,1)} %get-tuple-element.9), channel_id=1, source_target_pairs={{0,31},{1,0},{2,1},{3,2},{4,3},{5,4},{6,5},{7,6},{8,7},{9,8},{10,9... | collective-permute-start | bytes 393224 | tf_op jit(solution)/shard_map/ppermute | solution.py:183
  17.7 0.0 copy-done.9
  17.7 0.0 copy-done.1
  17.7 0.0 copy-done.8
  17.7 0.0 copy-done.7
  17.7 1.1 shard_map.105.refs_0_
  18.8 0.0 copy-start.2
  18.8 0.7 copy-done.2
  19.6 1.4 %shard_map.104.even_ref = bf16[256,1024]{1,0:T(8,128)(2,1)S(1)} custom-call(s32[1]{0:T(128)} %bitcast.lane_ref, bf16[1,8,6,128,128]{4,3,2,1,0:T(8,128)(2,1)S(1)} %copy-done.1, s32[6,1,8]{2,1,0:T(1,128)S(1)} %bitcast.17, s32[6,1,8]{2,1,0:T(1,128)S(1)} %bitcast.20, s32[1,8]{1,0:T(1,128)S(1)} %copy-done.9), custom_call_target="tpu_custom_call" | custom-call | tf_op jit(solution)/shard_map/pallas_call | solution.py:152
  21.0 0.0 collective-permute-done.odd_ref
  21.0 0.0 collective-permute-done.1.next_ref
  21.0 0.0 copy-done.3
  21.0 0.3 shard_map.107.refs_1_
  21.3 0.0 copy-start.4
  21.3 0.7 copy-done.4
  22.0 0.0 copy-start.5
  22.0 1.0 shard_map.108
  23.0 5.2 %collective-permute-start.2 = (bf16[256,768]{1,0:T(8,128)(2,1)}, bf16[256,768]{1,0:T(8,128)(2,1)S(1)}, u32[]{:S(2)}, u32[]{:S(2)}) collective-permute-start(bf16[256,768]{1,0:T(8,128)(2,1)} %shard_map.108), channel_id=1, source_target_pairs={{0,31},{1,0},{2,1},{3,2},{4,3},{5,4},{6,5},{7,6},{8,7},{9,8},{10,9... | collective-permute-start | bytes 1179656 | tf_op jit(solution)/shard_map/ppermute | solution.py:183
  28.3 4.2 %collective-permute-start.3 = (bf16[256,512]{1,0:T(8,128)(2,1)}, bf16[256,512]{1,0:T(8,128)(2,1)S(1)}, u32[]{:S(2)}, u32[]{:S(2)}) collective-permute-start(bf16[256,512]{1,0:T(8,128)(2,1)} %copy-done.4), channel_id=1, source_target_pairs={{0,28},{2,30},{4,0},{6,2},{8,4},{10,6},{12,8},{14,10},{16,12},{18,... | collective-permute-start | bytes 786440 | tf_op jit(solution)/shard_map/ppermute | solution.py:193
  32.5 6.2 %collective-permute-done.2.odd_ref = bf16[256,768]{1,0:T(8,128)(2,1)S(1)} collective-permute-done((bf16[256,768]{1,0:T(8,128)(2,1)}, bf16[256,768]{1,0:T(8,128)(2,1)S(1)}, u32[]{:S(2)}, u32[]{:S(2)}) %collective-permute-start.2) | collective-permute-done | bytes 393248 | tf_op jit(solution)/shard_map/ppermute | solution.py:183
  38.7 0.6 shard_map.109
  39.3 14.0 %collective-permute-start.4 = (bf16[256,512]{1,0:T(8,128)(2,1)S(1)}, bf16[256,512]{1,0:T(8,128)(2,1)S(1)}, u32[]{:S(2)}, u32[]{:S(2)}) collective-permute-start(bf16[256,512]{1,0:T(8,128)(2,1)S(1)} %get-tuple-element.12), channel_id=1, source_target_pairs={{0,30},{2,0},{4,2},{6,4},{8,6},{10,8},{12,10},{14,12},{16,14},{18,... | collective-permute-start | bytes 786440 | tf_op jit(solution)/shard_map/ppermute | solution.py:193
  53.3 1.9 %collective-permute-start.5 = (bf16[256,512]{1,0:T(8,128)(2,1)S(1)}, bf16[256,512]{1,0:T(8,128)(2,1)S(1)}, u32[]{:S(2)}, u32[]{:S(2)}) collective-permute-start(bf16[256,512]{1,0:T(8,128)(2,1)S(1)} %get-tuple-element.13), channel_id=1, source_target_pairs={{0,2},{2,4},{4,6},{6,8},{8,10},{10,12},{12,14},{14,16},{16,18},{18... | collective-permute-start | bytes 786440 | tf_op jit(solution)/shard_map/ppermute | solution.py:193
  55.2 0.0 collective-permute-done.3.first_ref
  55.2 1.9 %collective-permute-done.4.second_ref = bf16[256,512]{1,0:T(8,128)(2,1)S(1)} collective-permute-done((bf16[256,512]{1,0:T(8,128)(2,1)S(1)}, bf16[256,512]{1,0:T(8,128)(2,1)S(1)}, u32[]{:S(2)}, u32[]{:S(2)}) %collective-permute-start.4) | collective-permute-done | bytes 262176 | tf_op jit(solution)/shard_map/ppermute | solution.py:193
  57.1 5.6 %collective-permute-done.5.third_ref = bf16[256,512]{1,0:T(8,128)(2,1)S(1)} collective-permute-done((bf16[256,512]{1,0:T(8,128)(2,1)S(1)}, bf16[256,512]{1,0:T(8,128)(2,1)S(1)}, u32[]{:S(2)}, u32[]{:S(2)}) %collective-permute-start.5) | collective-permute-done | bytes 262176 | tf_op jit(solution)/shard_map/ppermute | solution.py:193
  62.8 0.0 copy-done.5
  62.8 0.0 copy-start.6
  62.8 0.5 shard_map.110
  63.2 9.2 %all_to_all.15 = bf16[4,256,128]{2,1,0:T(8,128)(2,1)S(1)} all-to-all(bf16[4,256,128]{2,1,0:T(8,128)(2,1)S(1)} %shard_map.110), channel_id=1, replica_groups=mesh['dp'=4,'rep'=4,'zh'=4,'zl'=4,'yl'=2] {'rep'}, dimensions={0} | all-to-all | bytes 524288 | tf_op jit(solution)/shard_map/all_to_all | solution.py:178
  72.5 1.9 %collective-permute-start.9 = (bf16[256,128]{1,0:T(8,128)(2,1)S(1)}, bf16[256,128]{1,0:T(8,128)(2,1)S(1)}, u32[]{:S(2)}, u32[]{:S(2)}) collective-permute-start(bf16[256,128]{1,0:T(8,128)(2,1)S(1)} %get-tuple-element.16), channel_id=1, source_target_pairs={{0,30},{2,0},{4,2},{6,4},{8,6},{10,8},{12,10},{14,12},{16,14},{18,... | collective-permute-start | bytes 196616 | tf_op jit(solution)/shard_map/ppermute | solution.py:193
  74.4 2.2 %collective-permute-start.8 = (bf16[256,128]{1,0:T(8,128)(2,1)S(1)}, bf16[256,128]{1,0:T(8,128)(2,1)S(1)}, u32[]{:S(2)}, u32[]{:S(2)}) collective-permute-start(bf16[256,128]{1,0:T(8,128)(2,1)S(1)} %get-tuple-element.17), channel_id=1, source_target_pairs={{0,4},{2,6},{4,8},{6,10},{8,12},{10,14},{12,16},{14,18},{16,20},{1... | collective-permute-start | bytes 196616 | tf_op jit(solution)/shard_map/ppermute | solution.py:193
  76.6 8.7 %collective-permute-start.7 = (bf16[256,128]{1,0:T(8,128)(2,1)S(1)}, bf16[256,128]{1,0:T(8,128)(2,1)S(1)}, u32[]{:S(2)}, u32[]{:S(2)}) collective-permute-start(bf16[256,128]{1,0:T(8,128)(2,1)S(1)} %get-tuple-element.18), channel_id=1, source_target_pairs={{0,22},{2,24},{4,26},{6,28},{8,30},{10,0},{12,2},{14,4},{16,6},{18... | collective-permute-start | bytes 196616 | tf_op jit(solution)/shard_map/ppermute | solution.py:193
  85.3 3.2 %collective-permute-start.6 = (bf16[256,128]{1,0:T(8,128)(2,1)S(1)}, bf16[256,128]{1,0:T(8,128)(2,1)S(1)}, u32[]{:S(2)}, u32[]{:S(2)}) collective-permute-start(bf16[256,128]{1,0:T(8,128)(2,1)S(1)} %get-tuple-element.19), channel_id=1, source_target_pairs={{0,12},{2,14},{4,16},{6,18},{8,20},{10,22},{12,24},{14,26},{16,28}... | collective-permute-start | bytes 196616 | tf_op jit(solution)/shard_map/ppermute | solution.py:193
  88.5 0.0 collective-permute-done.9.refs_3_
  88.5 0.0 collective-permute-done.8.refs_2_
  88.5 0.0 collective-permute-done.7.refs_1_
  88.5 9.9 %collective-permute-done.6.refs_0_ = bf16[256,128]{1,0:T(8,128)(2,1)S(1)} collective-permute-done((bf16[256,128]{1,0:T(8,128)(2,1)S(1)}, bf16[256,128]{1,0:T(8,128)(2,1)S(1)}, u32[]{:S(2)}, u32[]{:S(2)}) %collective-permute-start.6) | collective-permute-done | bytes 65568 | tf_op jit(solution)/shard_map/ppermute | solution.py:193
  98.4 0.0 copy-done.6
  98.4 0.3 shard_map.111
  98.7 21.5 %all_to_all.16.gw_ref = bf16[32,16,128]{2,1,0:T(8,128)(2,1)S(1)} all-to-all(bf16[32,16,128]{2,1,0:T(8,128)(2,1)S(1)} %bitcast.14), channel_id=1, replica_groups=mesh['dp'=4,'rep'=4,'zh'=4,'zl'=4,'yl'=2] {'zh','zl','yl'}, dimensions={0} | all-to-all | bytes 262144 | tf_op jit(solution)/shard_map/all_to_all | solution.py:178
  120.2 0.8 shard_map.112
  121.0 3.5 %all-to-all-start.2 = ((bf16[4,288,128]{2,1,0:T(8,128)(2,1)}), bf16[4,288,128]{2,1,0:T(8,128)(2,1)S(1)}, u32[]{:S(2)}, u32[]{:S(2)}) async-start(bf16[4,288,128]{2,1,0:T(8,128)(2,1)} %shard_map.112), calls=%async_computation.2 | async-start | bytes 589824 | tf_op jit(solution)/shard_map/all_to_all | solution.py:178
  124.4 0.0 copy-done
  124.4 0.5 convolution_convert_fusion.weight_ref
  124.9 6.3 %all-to-all-done.2.in_ref = bf16[4,288,128]{2,1,0:T(8,128)(2,1)S(1)} async-done(((bf16[4,288,128]{2,1,0:T(8,128)(2,1)}), bf16[4,288,128]{2,1,0:T(8,128)(2,1)S(1)}, u32[]{:S(2)}, u32[]{:S(2)}) %all-to-all-start.2) | async-done | bytes 294944 | tf_op jit(solution)/shard_map/all_to_all | solution.py:178
  131.3 1.1 shard_map.113
  (1 shorter events, 0.0 us)
Async XLA Ops:
  0.6 123.8 %copy-start = (bf16[512,512]{1,0:T(8,128)(2,1)S(1)}, bf16[512,512]{1,0:T(8,128)(2,1)}, u32[]{:S(2)}) copy-start(bf16[512,512]{1,0:T(8,128)(2,1)} %param.12) | copy-start | bytes 1572868
  0.6 17.1 %copy-start.9 = (s32[1,8]{1,0:T(1,128)S(1)}, s32[1,8]{1,0:T(1,128)}, u32[]{:S(2)}) copy-start(s32[1,8]{1,0:T(1,128)} %refs_2_.5) | copy-start | bytes 100
  0.7 17.1 %copy-start.1 = (bf16[1,8,6,128,128]{4,3,2,1,0:T(8,128)(2,1)S(1)}, bf16[1,8,6,128,128]{4,3,2,1,0:T(8,128)(2,1)}, u32[]{:S(2)}) copy-start(bf16[1,8,6,128,128]{4,3,2,1,0:T(8,128)(2,1)} %tiles_ref.5) | copy-start | bytes 4718596
  0.7 17.1 %copy-start.8 = (s32[1,8,6]{1,0,2:T(1,128)S(1)}, s32[1,8,6]{1,0,2:T(1,128)}, u32[]{:S(2)}) copy-start(s32[1,8,6]{1,0,2:T(1,128)} %param.15) | copy-start | bytes 580
  0.7 17.1 %copy-start.7 = (s32[1,8,6]{1,0,2:T(1,128)S(1)}, s32[1,8,6]{1,0,2:T(1,128)}, u32[]{:S(2)}) copy-start(s32[1,8,6]{1,0,2:T(1,128)} %param.14) | copy-start | bytes 580
  2.8 18.2 %collective-permute-start.1 = (bf16[256,512]{1,0:T(8,128)(2,1)}, bf16[256,512]{1,0:T(8,128)(2,1)S(1)}, u32[]{:S(2)}, u32[]{:S(2)}) collective-permute-start(bf16[256,512]{1,0:T(8,128)(2,1)} %get-tuple-element.10.own_ref), channel_id=1, source_target_pairs={{0,31},{1,0},{2,1},{3,2},{4,3},{5,4},{6,5},{7,6},{8,7},{9,8},{10,9... | collective-permute-start | bytes 786440 | tf_op jit(solution)/shard_map/ppermute | solution.py:183
  5.4 15.5 %copy-start.3 = (bf16[256,512]{1,0:T(8,128)(2,1)S(1)}, bf16[256,512]{1,0:T(8,128)(2,1)}, u32[]{:S(2)}) copy-start(bf16[256,512]{1,0:T(8,128)(2,1)} %get-tuple-element.10.own_ref) | copy-start | bytes 786436
  5.4 15.5 %collective-permute-start = (bf16[256,256]{1,0:T(8,128)(2,1)}, bf16[256,256]{1,0:T(8,128)(2,1)S(1)}, u32[]{:S(2)}, u32[]{:S(2)}) collective-permute-start(bf16[256,256]{1,0:T(8,128)(2,1)} %get-tuple-element.9), channel_id=1, source_target_pairs={{0,31},{1,0},{2,1},{3,2},{4,3},{5,4},{6,5},{7,6},{8,7},{9,8},{10,9... | collective-permute-start | bytes 393224 | tf_op jit(solution)/shard_map/ppermute | solution.py:183
  18.8 0.7 copy-start.2
  21.3 0.7 copy-start.4
  22.0 40.7 %copy-start.5 = (bf16[512,512]{1,0:T(8,128)(2,1)S(1)}, bf16[512,512]{1,0:T(8,128)(2,1)}, u32[]{:S(2)}) copy-start(bf16[512,512]{1,0:T(8,128)(2,1)} %constant.8.clone.spread_ref) | copy-start | bytes 1572868
  23.0 15.7 %collective-permute-start.2 = (bf16[256,768]{1,0:T(8,128)(2,1)}, bf16[256,768]{1,0:T(8,128)(2,1)S(1)}, u32[]{:S(2)}, u32[]{:S(2)}) collective-permute-start(bf16[256,768]{1,0:T(8,128)(2,1)} %shard_map.108), channel_id=1, source_target_pairs={{0,31},{1,0},{2,1},{3,2},{4,3},{5,4},{6,5},{7,6},{8,7},{9,8},{10,9... | collective-permute-start | bytes 1179656 | tf_op jit(solution)/shard_map/ppermute | solution.py:183
  28.3 26.9 %collective-permute-start.3 = (bf16[256,512]{1,0:T(8,128)(2,1)}, bf16[256,512]{1,0:T(8,128)(2,1)S(1)}, u32[]{:S(2)}, u32[]{:S(2)}) collective-permute-start(bf16[256,512]{1,0:T(8,128)(2,1)} %copy-done.4), channel_id=1, source_target_pairs={{0,28},{2,30},{4,0},{6,2},{8,4},{10,6},{12,8},{14,10},{16,12},{18,... | collective-permute-start | bytes 786440 | tf_op jit(solution)/shard_map/ppermute | solution.py:193
  39.3 17.8 %collective-permute-start.4 = (bf16[256,512]{1,0:T(8,128)(2,1)S(1)}, bf16[256,512]{1,0:T(8,128)(2,1)S(1)}, u32[]{:S(2)}, u32[]{:S(2)}) collective-permute-start(bf16[256,512]{1,0:T(8,128)(2,1)S(1)} %get-tuple-element.12), channel_id=1, source_target_pairs={{0,30},{2,0},{4,2},{6,4},{8,6},{10,8},{12,10},{14,12},{16,14},{18,... | collective-permute-start | bytes 786440 | tf_op jit(solution)/shard_map/ppermute | solution.py:193
  53.3 9.5 %collective-permute-start.5 = (bf16[256,512]{1,0:T(8,128)(2,1)S(1)}, bf16[256,512]{1,0:T(8,128)(2,1)S(1)}, u32[]{:S(2)}, u32[]{:S(2)}) collective-permute-start(bf16[256,512]{1,0:T(8,128)(2,1)S(1)} %get-tuple-element.13), channel_id=1, source_target_pairs={{0,2},{2,4},{4,6},{6,8},{8,10},{10,12},{12,14},{14,16},{16,18},{18... | collective-permute-start | bytes 786440 | tf_op jit(solution)/shard_map/ppermute | solution.py:193
  62.8 35.6 %copy-start.6 = (bf16[256,512]{1,0:T(8,128)(2,1)S(1)}, bf16[256,512]{1,0:T(8,128)(2,1)}, u32[]{:S(2)}) copy-start(bf16[256,512]{1,0:T(8,128)(2,1)} %refs_4_.3) | copy-start | bytes 786436
  72.5 16.0 %collective-permute-start.9 = (bf16[256,128]{1,0:T(8,128)(2,1)S(1)}, bf16[256,128]{1,0:T(8,128)(2,1)S(1)}, u32[]{:S(2)}, u32[]{:S(2)}) collective-permute-start(bf16[256,128]{1,0:T(8,128)(2,1)S(1)} %get-tuple-element.16), channel_id=1, source_target_pairs={{0,30},{2,0},{4,2},{6,4},{8,6},{10,8},{12,10},{14,12},{16,14},{18,... | collective-permute-start | bytes 196616 | tf_op jit(solution)/shard_map/ppermute | solution.py:193
  74.4 14.1 %collective-permute-start.8 = (bf16[256,128]{1,0:T(8,128)(2,1)S(1)}, bf16[256,128]{1,0:T(8,128)(2,1)S(1)}, u32[]{:S(2)}, u32[]{:S(2)}) collective-permute-start(bf16[256,128]{1,0:T(8,128)(2,1)S(1)} %get-tuple-element.17), channel_id=1, source_target_pairs={{0,4},{2,6},{4,8},{6,10},{8,12},{10,14},{12,16},{14,18},{16,20},{1... | collective-permute-start | bytes 196616 | tf_op jit(solution)/shard_map/ppermute | solution.py:193
  76.6 11.9 %collective-permute-start.7 = (bf16[256,128]{1,0:T(8,128)(2,1)S(1)}, bf16[256,128]{1,0:T(8,128)(2,1)S(1)}, u32[]{:S(2)}, u32[]{:S(2)}) collective-permute-start(bf16[256,128]{1,0:T(8,128)(2,1)S(1)} %get-tuple-element.18), channel_id=1, source_target_pairs={{0,22},{2,24},{4,26},{6,28},{8,30},{10,0},{12,2},{14,4},{16,6},{18... | collective-permute-start | bytes 196616 | tf_op jit(solution)/shard_map/ppermute | solution.py:193
  85.3 13.1 %collective-permute-start.6 = (bf16[256,128]{1,0:T(8,128)(2,1)S(1)}, bf16[256,128]{1,0:T(8,128)(2,1)S(1)}, u32[]{:S(2)}, u32[]{:S(2)}) collective-permute-start(bf16[256,128]{1,0:T(8,128)(2,1)S(1)} %get-tuple-element.19), channel_id=1, source_target_pairs={{0,12},{2,14},{4,16},{6,18},{8,20},{10,22},{12,24},{14,26},{16,28}... | collective-permute-start | bytes 196616 | tf_op jit(solution)/shard_map/ppermute | solution.py:193
  121.0 10.3 %all-to-all-start.2 = ((bf16[4,288,128]{2,1,0:T(8,128)(2,1)}), bf16[4,288,128]{2,1,0:T(8,128)(2,1)S(1)}, u32[]{:S(2)}, u32[]{:S(2)}) async-start(bf16[4,288,128]{2,1,0:T(8,128)(2,1)} %shard_map.112), calls=%async_computation.2 | async-start | bytes 589824 | tf_op jit(solution)/shard_map/all_to_all | solution.py:178

commit v4 on v3

v4 whole, which is shorter than its diff:
```python
import functools

import jax
import jax.numpy as jnp
import numpy as np
from jax import lax
from jax.experimental import pallas as pl
from jax.experimental.pallas import tpu as pltpu
from jax.sharding import Mesh, PartitionSpec as P

ZH, ZL, YL, REP = 4, 4, 2, 4
BLK = ("zh", "zl", "yl")
BF16, F32 = jnp.bfloat16, jnp.float32


def contract_rows(left, right):
    return lax.dot_general(left, right, (((0,), (0,)), ((), ())), preferred_element_type=F32)


def hidden_order(width):
    units = np.arange(width).reshape(ZH * ZL * YL, REP, -1)
    return units.transpose(1, 2, 0).reshape(-1)


def dense_kernel(tiles_ref, *refs, places, masked, marks):
    lists, refs = refs[:3], refs[3:]
    if masked:
        (pre_ref, up_ref, *refs) = refs
        (*refs, pre_held, up_held, own_sems) = refs
        inputs = [
            pltpu.make_async_copy(source, held, own_sems.at[at])
            for at, (source, held) in enumerate(((pre_ref, pre_held), (up_ref, up_held)))
        ]
        for copy in inputs:
            copy.start()
    out_ref, mark_ref, rows_ref, cols_ref, count_ref, held_ref, acc_ref, sems, list_sems = refs[marks:]
    mark_ref[...] = jnp.zeros_like(mark_ref)
    _, slots, tile, _ = held_ref.shape
    fetches = [
        pltpu.make_async_copy(source, held, list_sems.at[at])
        for at, (source, held) in enumerate(zip(lists, (rows_ref, cols_ref, count_ref)))
    ]
    for fetch in fetches:
        fetch.start()
    steps = [2 * m + odd for m, odd in places]
    copies = [
        pltpu.make_async_copy(tiles_ref.at[0, step], held_ref.at[at], sems.at[at])
        for at, step in enumerate(steps)
    ]
    for copy in copies:
        copy.start()
    if masked:
        for copy in inputs:
            copy.wait()
        own = jnp.where(pre_held[...] > 0, up_held[...], jnp.zeros_like(up_held))
        out_ref[:, : own.shape[1]] = own
    for fetch in fetches:
        fetch.wait()
    for at, step in enumerate(steps):
        acc_ref[...] = jnp.zeros_like(acc_ref)
        live = count_ref[0, step]
        copies[at].wait()
        for q in range(slots):

            @pl.when(q < live)
            def _():
                row, col = rows_ref[q, 0, step], cols_ref[q, 0, step]
                acc_ref[row, col] += held_ref[at, q].astype(F32)

        for row in range(2):
            for col in range(2):
                left = out_ref.shape[1] + (2 * (at - len(places)) + col) * tile
                out_ref[row * tile : (row + 1) * tile, left : left + tile] = acc_ref[
                    row, col
                ].astype(BF16)


def partial_kernel(even_ref, own_ref, next_ref, *refs, first, kinds):
    rows = even_ref.shape[0]
    *refs, mark_ref = refs
    mark_ref[...] = jnp.zeros_like(mark_ref)
    out_refs = refs[len(refs) - kinds :]
    hidden = out_refs[0].shape[1]
    odd = refs[0][...] if first else next_ref[:, hidden:]
    for m, out_ref in enumerate(out_refs):
        span = slice(m * rows, (m + 1) * rows)
        far = slice((first + m) * rows, (first + m + 1) * rows)
        block = contract_rows(even_ref[:, far], own_ref[:, :hidden])
        block += contract_rows(odd[:, span], next_ref[:, :hidden])
        out_ref[...] = block.astype(out_ref.dtype)


def near_kernel(some_ref, first_ref, second_ref, spread_ref, out_ref):
    total = some_ref[...] + first_ref[...].astype(F32) + second_ref[...].astype(F32)
    low = total.astype(BF16)
    quarter = out_ref.shape[2]
    for q in range(REP):
        span = slice(q * quarter, (q + 1) * quarter)
        out_ref[q] = jnp.dot(
            low, spread_ref[:, span], preferred_element_type=F32
        ).astype(BF16)


def sum_kernel(left_ref, right_ref, out_ref):
    out_ref[...] = left_ref[...].astype(F32) + right_ref[...].astype(F32)


def weight_kernel(*refs, scale):
    *in_refs, feat_ref, p_ref, gw_ref, lines_ref = refs
    total = in_refs[0][...].astype(F32)
    for in_ref in in_refs[1:]:
        total += in_ref[...].astype(F32)
    p_ref[...] = total.astype(BF16)
    gw = contract_rows(p_ref[...], feat_ref[...]) * scale
    quarter = lines_ref.shape[1]
    spots = ZH * ZL * YL
    rows, pieces = gw.shape[0] // spots, gw.shape[1] // quarter
    for i in range(rows):
        for f in range(pieces):
            lines_ref[pl.ds(i * pieces + f, spots, rows * pieces), :] = gw[
                i * spots : (i + 1) * spots, f * quarter : (f + 1) * quarter
            ]
    gw_ref[...] = lines_ref[...].astype(BF16)


def feature_kernel(lane_ref, *refs):
    *in_refs, weight_ref, feat_ref = refs
    quarter = in_refs[0].shape[1]
    total = jnp.zeros(feat_ref.shape, F32)
    for back, in_ref in enumerate(in_refs):
        source = lax.rem(lane_ref[0] + REP - back, REP)
        span = pl.ds(pl.multiple_of(source * quarter, quarter), quarter)
        total += jnp.dot(in_ref[...], weight_ref[span, :], preferred_element_type=F32)
    feat_ref[...] = total.astype(BF16)


def copies_kernel(in_ref, out_ref):
    total = in_ref[0].astype(F32)
    for d in range(1, in_ref.shape[0]):
        total += in_ref[d].astype(F32)
    for r in range(out_ref.shape[0]):
        out_ref[r] = total


def lines_kernel(in_ref, gw_ref):
    lanes, lines, quarter = in_ref.shape
    pieces = gw_ref.shape[1] // quarter
    for q in range(lanes):
        for at in range(lines):
            row = q * (lines // pieces) + at // pieces
            left = at % pieces * quarter
            gw_ref[row : row + 1, left : left + quarter] = in_ref[q, at : at + 1, :]


def whole(kernel, outs, scalars, arrays, scratch=(), space=pltpu.VMEM, limit=48):
    return pl.pallas_call(
        kernel,
        in_specs=[pl.BlockSpec(memory_space=pltpu.SMEM)] * len(scalars)
        + [pl.BlockSpec(memory_space=space)] * len(arrays),
        out_specs=jax.tree.map(lambda _: pl.BlockSpec(memory_space=pltpu.VMEM), outs),
        out_shape=outs,
        scratch_shapes=scratch,
        compiler_params=pltpu.CompilerParams(vmem_limit_bytes=limit * 1024 * 1024),
    )(*scalars, *arrays)


def exchange(value, axes):
    return lax.all_to_all(value, axes, 0, 0)


def to_previous(value):
    count = ZH * ZL * YL
    return lax.ppermute(value, BLK, [(b, (b - 1) % count) for b in range(count)])


def along_z(value, shift):
    count = ZH * ZL
    return lax.ppermute(value, ("zh", "zl"), [(z, (z + shift) % count) for z in range(count)])


def shards(features, pre_act, upstream, weight, tile_values, tile_rows, tile_cols, tile_count):
    _, steps, slots, tile, _ = tile_values.shape
    nodes, width = features.shape
    hidden = upstream.shape[1]
    quarter = width // REP
    scale = float(nodes * ZH * ZL * YL) ** -0.5
    shape = jax.ShapeDtypeStruct

    lists = (tile_rows.transpose(2, 0, 1), tile_cols.transpose(2, 0, 1), tile_count)
    mark = shape((8, tile), F32)

    def dense(places, masked=(), marks=()):
        wide = len(places) * 2 * tile + (hidden if masked else 0)
        outs = (shape((nodes, wide), BF16), mark)
        held = [pltpu.VMEM(value.shape, value.dtype) for value in masked]
        return whole(
            functools.partial(
                dense_kernel, places=places, masked=bool(masked), marks=len(marks)
            ),
            outs,
            (),
            (tile_values, *lists, *masked, *marks),
            (
                *(pltpu.SMEM(listed.shape, listed.dtype) for listed in lists),
                pltpu.VMEM((len(places), slots, tile, tile), BF16),
                pltpu.VMEM((2, 2, tile, tile), F32),
                pltpu.SemaphoreType.DMA((len(places),)),
                pltpu.SemaphoreType.DMA((len(lists),)),
                *held,
                *((pltpu.SemaphoreType.DMA((len(held),)),) if held else ()),
            ),
            pltpu.HBM,
            60 if masked else 48,
        )

    def partial(odd, first, kinds):
        return whole(
            functools.partial(partial_kernel, first=first, kinds=len(kinds)),
            tuple(shape((nodes, hidden), kind) for kind in kinds) + (mark,),
            (),
            (even, first_part, following, *odd),
        )

    first_part, mark_first = dense(((0, 1),), (pre_act, upstream))
    even, mark_even = dense(((0, 0), (1, 0), (2, 0), (3, 0)), marks=(mark_first,))
    rest_odd, _ = dense(((1, 1), (2, 1), (3, 1)), marks=(mark_even,))
    following = to_previous(first_part)
    rest_odd = to_previous(rest_odd)
    two, mark_two = partial((), 0, (BF16,))
    one, keep, back, _ = partial((rest_odd, mark_two), 1, (BF16, F32, BF16))
    some = whole(sum_kernel, (shape((nodes, hidden), F32),), (), (keep, along_z(two, 2)))[0]
    one = along_z(one, 1)
    back = along_z(back, -1)

    spread = np.zeros((hidden, hidden), np.float32)
    spread[hidden_order(hidden), np.arange(hidden)] = 1.0
    spread = jnp.asarray(spread, BF16)
    weight = contract_rows(spread, weight).astype(BF16)
    parts = whole(
        near_kernel,
        (shape((REP, nodes, quarter), BF16),),
        (),
        (some, one, back, spread),
    )[0]
    parts = exchange(parts, "rep")
    hops = (-2, -6, 6, 2)
    parts = [along_z(parts[r], hops[r]) for r in range(REP)]
    far = whole(sum_kernel, (shape((nodes, quarter), F32),), (), (parts[1], parts[2]))[0]
    p_quarter, gw = whole(
        functools.partial(weight_kernel, scale=scale),
        (shape((nodes, quarter), BF16), shape((hidden, quarter), BF16)),
        (),
        (far, parts[0], parts[3], features),
        (pltpu.VMEM((hidden, quarter), F32),),
    )
    gw = exchange(gw.reshape(ZH * ZL * YL, -1, quarter), BLK)
    gw = whole(copies_kernel, (shape((REP,) + gw.shape[1:], F32),), (), (gw,))[0]
    gw = exchange(gw, "rep")
    lane = lax.axis_index("rep").reshape(1)
    p_all = [p_quarter] + [
        lax.ppermute(p_quarter, "rep", [(r, (r + back) % REP) for r in range(REP)])
        for back in range(1, REP)
    ]
    grad_feat = whole(
        feature_kernel, (shape((nodes, width), BF16),), (lane,), (*p_all, weight)
    )[0]
    rows = hidden // (ZH * ZL * YL)
    grad_weight = whole(lines_kernel, (shape((rows, width), F32),), (), (gw,))[0]
    return grad_feat, grad_weight


def solution(mesh):
    dp = mesh.shape["dp"]
    fine = Mesh(mesh.devices.reshape(dp, REP, ZH, ZL, YL), ("dp", "rep") + BLK)
    rows = ("dp",) + BLK
    return jax.shard_map(
        shards,
        mesh=fine,
        in_specs=(
            P(rows, None),
            P(rows, None),
            P(rows, None),
            P(),
            P(rows, "rep", None, None, None),
            P(rows, "rep", None),
            P(rows, "rep", None),
            P(rows, "rep"),
        ),
        out_specs=(P(rows, None), P(rows, None)),
        check_vma=False,
    )
```

time: 133 us -> 118 us (0.89)
  blocking collectives: 30.8 us -> 10.8 us
  starting transfers between devices: 59.6 us -> 67.2 us
  waiting for transfers between devices: 30 us -> 27.1 us
  Pallas kernels: 9.11 us -> 10.5 us
    all_to_all x2 -> x1, blocking collectives: 30.8 us -> 10.8 us  [exchange(): return lax.all_to_all(value, axes, 0, 0)]
    all_to_all x1 -> x2, starting transfers between devices: 3.45 us -> 11.5 us  [exchange(): return lax.all_to_all(value, axes, 0, 0)]
    ppermute x7 -> x10, waiting for transfers between devices: 17.4 us -> 12 us  [the longest x7 12 us: along_z(): lax.ppermute(value, ('zh', 'zl'), [(z, (z + shift) % count) for z in rang...]
    ppermute x3 -> x2, starting transfers between devices: 20.1 us -> 14.7 us  [to_previous(): lax.ppermute(value, BLK, [(b, (b - 1) % count) for b in range(count)])]
    ppermute x7 -> x10, starting transfers between devices: 36 us -> 41 us  [the longest x7 32 us: along_z(): lax.ppermute(value, ('zh', 'zl'), [(z, (z + shift) % count) for z in rang...]
    all_to_all x1 -> x2, waiting for transfers between devices: 6.34 us -> 9.34 us  [exchange(): return lax.all_to_all(value, axes, 0, 0)]
    pallas_call x9 -> x12, Pallas kernels: 8.1 us -> 10.5 us  [whole(): pl.pallas_call(kernel, in_specs=[pl.BlockSpec(memory_space=pltpu.SMEM)] *...]
    ppermute x3 -> x2, waiting for transfers between devices: 6.23 us -> 5.67 us  [to_previous(): lax.ppermute(value, BLK, [(b, (b - 1) % count) for b in range(count)])]
  transfers between devices with their start and end apart: 11 -> 14, of which waited for: 5 -> 6; matrix products, arithmetic and copies ran while one was open for 0% -> 0% of each run, Pallas kernels for 2% -> 5%
where the time goes in v4:
time: 118 us
  starting transfers between devices  67.2 us (57%)
  waiting for transfers between devices  27.1 us (23%)
  blocking collectives  10.8 us (9%)
  Pallas kernels  10.5 us (9%)
    ppermute x7, starting transfers between devices, along_z(): lax.ppermute(value, ('zh', 'zl'), [(z, (z + shift) % count) for z in rang...  32 us
    ppermute x2, starting transfers between devices, to_previous(): lax.ppermute(value, BLK, [(b, (b - 1) % count) for b in range(count)])  14.7 us
    ppermute x7, waiting for transfers between devices, along_z(): lax.ppermute(value, ('zh', 'zl'), [(z, (z + shift) % count) for z in rang...  12 us
    all_to_all x2, starting transfers between devices, exchange(): return lax.all_to_all(value, axes, 0, 0)  11.5 us
    all_to_all x1, blocking collectives, exchange(): return lax.all_to_all(value, axes, 0, 0)  10.8 us
    pallas_call x12, Pallas kernels, whole(): pl.pallas_call(kernel, in_specs=[pl.BlockSpec(memory_space=pltpu.SMEM)] *...  10.5 us
    all_to_all x2, waiting for transfers between devices, exchange(): return lax.all_to_all(value, axes, 0, 0)  9.34 us
    ppermute x3, starting transfers between devices, shards(): lax.ppermute(p_quarter, 'rep', [(r, (r + back) % REP) for r in range(REP)])  8.97 us
  transfers between devices with their start and end apart: 14, of which 6 were waited for; matrix products, arithmetic and copies ran while one was open for 0% of the time, Pallas kernels for 5%

profile of v4, /device:TPU:24, one launch (start us, length us, event | category | flops | bytes accessed | tf_op | source)
XLA Modules:
  0.0 117.8 jit_solution(12771484170303904197)
XLA Ops:
  0.6 0.0 copy-start
  0.6 0.0 copy-start.5
  0.7 0.0 copy-start.6
  0.7 0.0 copy-start.1
  0.7 0.0 copy-start.7
  0.7 2.1 %shard_map.104 = (bf16[256,768]{1,0:T(8,128)(2,1)}, f32[8,128]{1,0:T(8,128)}) custom-call(bf16[1,8,6,128,128]{4,3,2,1,0:T(8,128)(2,1)} %tiles_ref.5, s32[6,1,8]{2,1,0:T(1,128)} %bitcast.14, s32[6,1,8]{2,1,0:T(1,128)} %bitcast.17, s32[1,8]{1,0:T(1,128)} %refs_2_.5, bf16[256,512]{1,0:T(8,128)(2,1)} %refs_3_.2, bf16[256,512]{1,0:T(8,128)(2,1)} %refs_4_.1), custom_call_target="tpu_custom_call" | custom-call | tf_op jit(solution)/shard_map/pallas_call | solution.py:156
  2.8 2.7 %collective-permute-start = (bf16[256,768]{1,0:T(8,128)(2,1)}, bf16[256,768]{1,0:T(8,128)(2,1)S(1)}, u32[]{:S(2)}, u32[]{:S(2)}) collective-permute-start(bf16[256,768]{1,0:T(8,128)(2,1)} %get-tuple-element.16.own_ref), channel_id=1, source_target_pairs={{0,31},{1,0},{2,1},{3,2},{4,3},{5,4},{6,5},{7,6},{8,7},{9,8},{10,9... | collective-permute-start | bytes 1179656 | tf_op jit(solution)/shard_map/ppermute | solution.py:173
  5.5 0.0 copy-done.5
  5.5 0.0 copy-done.6
  5.5 0.0 copy-done.1
  5.5 0.0 copy-done.7
  5.5 0.0 copy-start.8
  5.5 0.7 copy-done.8
  6.2 0.0 copy-start.2
  6.2 1.5 %shard_map.105 = (bf16[256,1024]{1,0:T(8,128)(2,1)S(1)}, f32[8,128]{1,0:T(8,128)S(1)}) custom-call(bf16[1,8,6,128,128]{4,3,2,1,0:T(8,128)(2,1)S(1)} %copy-done.1, s32[6,1,8]{2,1,0:T(1,128)S(1)} %bitcast.15, s32[6,1,8]{2,1,0:T(1,128)S(1)} %bitcast.18, s32[1,8]{1,0:T(1,128)S(1)} %copy-done.7, f32[8,128]{1,0:T(8,128)S(1)} %copy-done.8), custom_call_target="tpu_custom_call" | custom-call | tf_op jit(solution)/shard_map/pallas_call | solution.py:156
  7.7 1.7 %shard_map.106 = (bf16[256,768]{1,0:T(8,128)(2,1)S(1)}, f32[8,128]{1,0:T(8,128)}) custom-call(bf16[1,8,6,128,128]{4,3,2,1,0:T(8,128)(2,1)S(1)} %copy-done.1, s32[6,1,8]{2,1,0:T(1,128)S(1)} %bitcast.16, s32[6,1,8]{2,1,0:T(1,128)S(1)} %bitcast.19, s32[1,8]{1,0:T(1,128)S(1)} %copy-done.7, f32[8,128]{1,0:T(8,128)S(1)} %get-tuple-element.17.refs_3_), custom_call_target="tpu_custom_call" | custom-call | tf_op jit(solution)/shard_map/pallas_call | solution.py:156
  9.4 12.1 %collective-permute-start.1 = (bf16[256,768]{1,0:T(8,128)(2,1)S(1)}, bf16[256,768]{1,0:T(8,128)(2,1)S(1)}, u32[]{:S(2)}, u32[]{:S(2)}) collective-permute-start(bf16[256,768]{1,0:T(8,128)(2,1)S(1)} %get-tuple-element.18), channel_id=1, source_target_pairs={{0,31},{1,0},{2,1},{3,2},{4,3},{5,4},{6,5},{7,6},{8,7},{9,8},{10,9... | collective-permute-start | bytes 1179656 | tf_op jit(solution)/shard_map/ppermute | solution.py:173
  21.5 0.0 collective-permute-done.next_ref
  21.5 0.0 copy-done.2
  21.5 0.3 shard_map.107
  21.8 0.0 copy-start.3
  21.8 2.1 %collective-permute-start.2 = (bf16[256,512]{1,0:T(8,128)(2,1)S(1)}, bf16[256,512]{1,0:T(8,128)(2,1)S(1)}, u32[]{:S(2)}, u32[]{:S(2)}) collective-permute-start(bf16[256,512]{1,0:T(8,128)(2,1)S(1)} %get-tuple-element.21), channel_id=1, source_target_pairs={{0,4},{2,6},{4,8},{6,10},{8,12},{10,14},{12,16},{14,18},{16,20},{1... | collective-permute-start | bytes 786440 | tf_op jit(solution)/shard_map/ppermute | solution.py:178
  23.9 5.7 %collective-permute-done.1.refs_0_ = bf16[256,768]{1,0:T(8,128)(2,1)S(1)} collective-permute-done((bf16[256,768]{1,0:T(8,128)(2,1)S(1)}, bf16[256,768]{1,0:T(8,128)(2,1)S(1)}, u32[]{:S(2)}, u32[]{:S(2)}) %collective-permute-start.1) | collective-permute-done | bytes 393248 | tf_op jit(solution)/shard_map/ppermute | solution.py:173
  29.6 1.1 shard_map.108
  30.6 1.9 %collective-permute-start.3 = (bf16[256,512]{1,0:T(8,128)(2,1)S(1)}, bf16[256,512]{1,0:T(8,128)(2,1)S(1)}, u32[]{:S(2)}, u32[]{:S(2)}) collective-permute-start(bf16[256,512]{1,0:T(8,128)(2,1)S(1)} %get-tuple-element.22), channel_id=1, source_target_pairs={{0,2},{2,4},{4,6},{6,8},{8,10},{10,12},{12,14},{14,16},{16,18},{18... | collective-permute-start | bytes 786440 | tf_op jit(solution)/shard_map/ppermute | solution.py:178
  32.5 8.2 %collective-permute-start.4 = (bf16[256,512]{1,0:T(8,128)(2,1)S(1)}, bf16[256,512]{1,0:T(8,128)(2,1)S(1)}, u32[]{:S(2)}, u32[]{:S(2)}) collective-permute-start(bf16[256,512]{1,0:T(8,128)(2,1)S(1)} %get-tuple-element.23), channel_id=1, source_target_pairs={{0,30},{2,0},{4,2},{6,4},{8,6},{10,8},{12,10},{14,12},{16,14},{18,... | collective-permute-start | bytes 786440 | tf_op jit(solution)/shard_map/ppermute | solution.py:178
  40.7 0.0 collective-permute-done.2.right_ref
  40.8 0.0 copy-start.4
  40.8 4.9 %collective-permute-done.3.first_ref = bf16[256,512]{1,0:T(8,128)(2,1)S(1)} collective-permute-done((bf16[256,512]{1,0:T(8,128)(2,1)S(1)}, bf16[256,512]{1,0:T(8,128)(2,1)S(1)}, u32[]{:S(2)}, u32[]{:S(2)}) %collective-permute-start.3) | collective-permute-done | bytes 262176 | tf_op jit(solution)/shard_map/ppermute | solution.py:178
  45.7 0.0 collective-permute-done.4.second_ref
  45.7 0.0 copy-done.3
  45.7 0.4 shard_map.110
  46.1 10.8 %all_to_all.15 = bf16[4,256,128]{2,1,0:T(8,128)(2,1)S(1)} all-to-all(bf16[4,256,128]{2,1,0:T(8,128)(2,1)S(1)} %shard_map.110), channel_id=1, replica_groups=mesh['dp'=4,'rep'=4,'zh'=4,'zl'=4,'yl'=2] {'rep'}, dimensions={0} | all-to-all | bytes 524288 | tf_op jit(solution)/shard_map/all_to_all | solution.py:168
  57.0 8.2 %collective-permute-start.5 = (bf16[256,128]{1,0:T(8,128)(2,1)S(1)}, bf16[256,128]{1,0:T(8,128)(2,1)S(1)}, u32[]{:S(2)}, u32[]{:S(2)}) collective-permute-start(bf16[256,128]{1,0:T(8,128)(2,1)S(1)} %get-tuple-element.29), channel_id=1, source_target_pairs={{0,20},{2,22},{4,24},{6,26},{8,28},{10,30},{12,0},{14,2},{16,4},{1... | collective-permute-start | bytes 196616 | tf_op jit(solution)/shard_map/ppermute | solution.py:178
  65.2 3.4 %collective-permute-start.6 = (bf16[256,128]{1,0:T(8,128)(2,1)S(1)}, bf16[256,128]{1,0:T(8,128)(2,1)S(1)}, u32[]{:S(2)}, u32[]{:S(2)}) collective-permute-start(bf16[256,128]{1,0:T(8,128)(2,1)S(1)} %get-tuple-element.28), channel_id=1, source_target_pairs={{0,12},{2,14},{4,16},{6,18},{8,20},{10,22},{12,24},{14,26},{16,28}... | collective-permute-start | bytes 196616 | tf_op jit(solution)/shard_map/ppermute | solution.py:178
  68.5 6.4 %collective-permute-start.7 = (bf16[256,128]{1,0:T(8,128)(2,1)S(1)}, bf16[256,128]{1,0:T(8,128)(2,1)S(1)}, u32[]{:S(2)}, u32[]{:S(2)}) collective-permute-start(bf16[256,128]{1,0:T(8,128)(2,1)S(1)} %get-tuple-element.27), channel_id=1, source_target_pairs={{0,28},{2,30},{4,0},{6,2},{8,4},{10,6},{12,8},{14,10},{16,12},{18,... | collective-permute-start | bytes 196616 | tf_op jit(solution)/shard_map/ppermute | solution.py:178
  74.9 1.9 %collective-permute-start.8 = (bf16[256,128]{1,0:T(8,128)(2,1)S(1)}, bf16[256,128]{1,0:T(8,128)(2,1)S(1)}, u32[]{:S(2)}, u32[]{:S(2)}) collective-permute-start(bf16[256,128]{1,0:T(8,128)(2,1)S(1)} %get-tuple-element.26), channel_id=1, source_target_pairs={{0,4},{2,6},{4,8},{6,10},{8,12},{10,14},{12,16},{14,18},{16,20},{1... | collective-permute-start | bytes 196616 | tf_op jit(solution)/shard_map/ppermute | solution.py:178
  76.9 0.0 collective-permute-done.5.left_ref
  76.9 6.7 %collective-permute-done.6.right_ref = bf16[256,128]{1,0:T(8,128)(2,1)S(1)} collective-permute-done((bf16[256,128]{1,0:T(8,128)(2,1)S(1)}, bf16[256,128]{1,0:T(8,128)(2,1)S(1)}, u32[]{:S(2)}, u32[]{:S(2)}) %collective-permute-start.6) | collective-permute-done | bytes 65568 | tf_op jit(solution)/shard_map/ppermute | solution.py:178
  83.6 0.0 collective-permute-done.7.refs_1_
  83.6 0.4 collective-permute-done.8.refs_2_
  84.1 0.0 copy-done.4
  84.1 0.9 shard_map.112
  85.0 8.2 %all-to-all-start.1 = ((bf16[32,16,128]{2,1,0:T(8,128)(2,1)}), bf16[32,16,128]{2,1,0:T(8,128)(2,1)S(1)}, u32[]{:S(2)}, u32[]{:S(2)}) async-start(bf16[32,16,128]{2,1,0:T(8,128)(2,1)} %bitcast.7), calls=%async_computation.1 | async-start | bytes 262144 | tf_op jit(solution)/shard_map/all_to_all | solution.py:168
  93.2 2.7 %collective-permute-start.10 = (bf16[256,128]{1,0:T(8,128)(2,1)S(1)}, bf16[256,128]{1,0:T(8,128)(2,1)S(1)}, u32[]{:S(2)}, u32[]{:S(2)}) collective-permute-start(bf16[256,128]{1,0:T(8,128)(2,1)S(1)} %get-tuple-element.24.refs_0_), channel_id=1, source_target_pairs={{0,64},{32,96},{64,0},{96,32},{1,65},{33,97},{65,1},{97,33},{2,66}... | collective-permute-start | bytes 196616 | tf_op jit(solution)/shard_map/ppermute | solution.py:261
  96.0 4.3 %collective-permute-start.11 = (bf16[256,128]{1,0:T(8,128)(2,1)S(1)}, bf16[256,128]{1,0:T(8,128)(2,1)S(1)}, u32[]{:S(2)}, u32[]{:S(2)}) collective-permute-start(bf16[256,128]{1,0:T(8,128)(2,1)S(1)} %get-tuple-element.24.refs_0_), channel_id=1, source_target_pairs={{0,96},{32,0},{64,32},{96,64},{1,97},{33,1},{65,33},{97,65},{2,98}... | collective-permute-start | bytes 196616 | tf_op jit(solution)/shard_map/ppermute | solution.py:261
  100.3 1.9 %collective-permute-start.9 = (bf16[256,128]{1,0:T(8,128)(2,1)S(1)}, bf16[256,128]{1,0:T(8,128)(2,1)S(1)}, u32[]{:S(2)}, u32[]{:S(2)}) collective-permute-start(bf16[256,128]{1,0:T(8,128)(2,1)S(1)} %get-tuple-element.24.refs_0_), channel_id=1, source_target_pairs={{0,32},{32,64},{64,96},{96,0},{1,33},{33,65},{65,97},{97,1},{2,34}... | collective-permute-start | bytes 196616 | tf_op jit(solution)/shard_map/ppermute | solution.py:261
  102.2 5.6 %all-to-all-done.1.in_ref = bf16[32,16,128]{2,1,0:T(8,128)(2,1)S(1)} async-done(((bf16[32,16,128]{2,1,0:T(8,128)(2,1)}), bf16[32,16,128]{2,1,0:T(8,128)(2,1)S(1)}, u32[]{:S(2)}, u32[]{:S(2)}) %all-to-all-start.1) | async-done | bytes 131104 | tf_op jit(solution)/shard_map/all_to_all | solution.py:168
  107.8 0.7 shard_map.114
  108.5 3.3 %all-to-all-start.2 = ((f32[4,16,128]{2,1,0:T(8,128)}), f32[4,16,128]{2,1,0:T(8,128)S(1)}, u32[]{:S(2)}, u32[]{:S(2)}) async-start(f32[4,16,128]{2,1,0:T(8,128)} %shard_map.114), calls=%async_computation.2 | async-start | bytes 65536 | tf_op jit(solution)/shard_map/all_to_all | solution.py:168
  111.7 0.0 copy-done
  111.7 0.5 convolution_convert_fusion.refs_4_
  112.2 0.0 collective-permute-done.10.refs_2_
  112.2 0.0 collective-permute-done.11.refs_3_
  112.2 0.0 collective-permute-done.9.refs_1_
  112.2 1.1 shard_map.113
  113.4 3.8 %all-to-all-done.2.in_ref = f32[4,16,128]{2,1,0:T(8,128)S(1)} async-done(((f32[4,16,128]{2,1,0:T(8,128)}), f32[4,16,128]{2,1,0:T(8,128)S(1)}, u32[]{:S(2)}, u32[]{:S(2)}) %all-to-all-start.2) | async-done | bytes 32800 | tf_op jit(solution)/shard_map/all_to_all | solution.py:168
  117.1 0.6 shard_map.115
  (3 shorter events, 0.1 us)
Async XLA Ops:
  0.6 111.1 %copy-start = (bf16[512,512]{1,0:T(8,128)(2,1)S(1)}, bf16[512,512]{1,0:T(8,128)(2,1)}, u32[]{:S(2)}) copy-start(bf16[512,512]{1,0:T(8,128)(2,1)} %param.12) | copy-start | bytes 1572868
  0.6 4.8 %copy-start.5 = (s32[1,8,6]{1,0,2:T(1,128)S(1)}, s32[1,8,6]{1,0,2:T(1,128)}, u32[]{:S(2)}) copy-start(s32[1,8,6]{1,0,2:T(1,128)} %param.14) | copy-start | bytes 580
  0.7 4.8 %copy-start.6 = (s32[1,8,6]{1,0,2:T(1,128)S(1)}, s32[1,8,6]{1,0,2:T(1,128)}, u32[]{:S(2)}) copy-start(s32[1,8,6]{1,0,2:T(1,128)} %param.15) | copy-start | bytes 580
  0.7 4.8 %copy-start.1 = (bf16[1,8,6,128,128]{4,3,2,1,0:T(8,128)(2,1)S(1)}, bf16[1,8,6,128,128]{4,3,2,1,0:T(8,128)(2,1)}, u32[]{:S(2)}) copy-start(bf16[1,8,6,128,128]{4,3,2,1,0:T(8,128)(2,1)} %tiles_ref.5) | copy-start | bytes 4718596
  0.7 4.8 %copy-start.7 = (s32[1,8]{1,0:T(1,128)S(1)}, s32[1,8]{1,0:T(1,128)}, u32[]{:S(2)}) copy-start(s32[1,8]{1,0:T(1,128)} %refs_2_.5) | copy-start | bytes 100
  2.8 18.6 %collective-permute-start = (bf16[256,768]{1,0:T(8,128)(2,1)}, bf16[256,768]{1,0:T(8,128)(2,1)S(1)}, u32[]{:S(2)}, u32[]{:S(2)}) collective-permute-start(bf16[256,768]{1,0:T(8,128)(2,1)} %get-tuple-element.16.own_ref), channel_id=1, source_target_pairs={{0,31},{1,0},{2,1},{3,2},{4,3},{5,4},{6,5},{7,6},{8,7},{9,8},{10,9... | collective-permute-start | bytes 1179656 | tf_op jit(solution)/shard_map/ppermute | solution.py:173
  5.5 0.7 copy-start.8
  6.2 15.3 %copy-start.2 = (bf16[256,768]{1,0:T(8,128)(2,1)S(1)}, bf16[256,768]{1,0:T(8,128)(2,1)}, u32[]{:S(2)}) copy-start(bf16[256,768]{1,0:T(8,128)(2,1)} %get-tuple-element.16.own_ref) | copy-start | bytes 1179652
  9.4 20.2 %collective-permute-start.1 = (bf16[256,768]{1,0:T(8,128)(2,1)S(1)}, bf16[256,768]{1,0:T(8,128)(2,1)S(1)}, u32[]{:S(2)}, u32[]{:S(2)}) collective-permute-start(bf16[256,768]{1,0:T(8,128)(2,1)S(1)} %get-tuple-element.18), channel_id=1, source_target_pairs={{0,31},{1,0},{2,1},{3,2},{4,3},{5,4},{6,5},{7,6},{8,7},{9,8},{10,9... | collective-permute-start | bytes 1179656 | tf_op jit(solution)/shard_map/ppermute | solution.py:173
  21.8 23.9 %copy-start.3 = (bf16[512,512]{1,0:T(8,128)(2,1)S(1)}, bf16[512,512]{1,0:T(8,128)(2,1)}, u32[]{:S(2)}) copy-start(bf16[512,512]{1,0:T(8,128)(2,1)} %constant.8.clone.spread_ref) | copy-start | bytes 1572868
  21.8 18.9 %collective-permute-start.2 = (bf16[256,512]{1,0:T(8,128)(2,1)S(1)}, bf16[256,512]{1,0:T(8,128)(2,1)S(1)}, u32[]{:S(2)}, u32[]{:S(2)}) collective-permute-start(bf16[256,512]{1,0:T(8,128)(2,1)S(1)} %get-tuple-element.21), channel_id=1, source_target_pairs={{0,4},{2,6},{4,8},{6,10},{8,12},{10,14},{12,16},{14,18},{16,20},{1... | collective-permute-start | bytes 786440 | tf_op jit(solution)/shard_map/ppermute | solution.py:178
  30.6 15.1 %collective-permute-start.3 = (bf16[256,512]{1,0:T(8,128)(2,1)S(1)}, bf16[256,512]{1,0:T(8,128)(2,1)S(1)}, u32[]{:S(2)}, u32[]{:S(2)}) collective-permute-start(bf16[256,512]{1,0:T(8,128)(2,1)S(1)} %get-tuple-element.22), channel_id=1, source_target_pairs={{0,2},{2,4},{4,6},{6,8},{8,10},{10,12},{12,14},{14,16},{16,18},{18... | collective-permute-start | bytes 786440 | tf_op jit(solution)/shard_map/ppermute | solution.py:178
  32.5 13.1 %collective-permute-start.4 = (bf16[256,512]{1,0:T(8,128)(2,1)S(1)}, bf16[256,512]{1,0:T(8,128)(2,1)S(1)}, u32[]{:S(2)}, u32[]{:S(2)}) collective-permute-start(bf16[256,512]{1,0:T(8,128)(2,1)S(1)} %get-tuple-element.23), channel_id=1, source_target_pairs={{0,30},{2,0},{4,2},{6,4},{8,6},{10,8},{12,10},{14,12},{16,14},{18,... | collective-permute-start | bytes 786440 | tf_op jit(solution)/shard_map/ppermute | solution.py:178
  40.8 43.3 %copy-start.4 = (bf16[256,512]{1,0:T(8,128)(2,1)S(1)}, bf16[256,512]{1,0:T(8,128)(2,1)}, u32[]{:S(2)}) copy-start(bf16[256,512]{1,0:T(8,128)(2,1)} %refs_3_.3) | copy-start | bytes 786436
  57.0 19.9 %collective-permute-start.5 = (bf16[256,128]{1,0:T(8,128)(2,1)S(1)}, bf16[256,128]{1,0:T(8,128)(2,1)S(1)}, u32[]{:S(2)}, u32[]{:S(2)}) collective-permute-start(bf16[256,128]{1,0:T(8,128)(2,1)S(1)} %get-tuple-element.29), channel_id=1, source_target_pairs={{0,20},{2,22},{4,24},{6,26},{8,28},{10,30},{12,0},{14,2},{16,4},{1... | collective-permute-start | bytes 196616 | tf_op jit(solution)/shard_map/ppermute | solution.py:178
  65.2 18.4 %collective-permute-start.6 = (bf16[256,128]{1,0:T(8,128)(2,1)S(1)}, bf16[256,128]{1,0:T(8,128)(2,1)S(1)}, u32[]{:S(2)}, u32[]{:S(2)}) collective-permute-start(bf16[256,128]{1,0:T(8,128)(2,1)S(1)} %get-tuple-element.28), channel_id=1, source_target_pairs={{0,12},{2,14},{4,16},{6,18},{8,20},{10,22},{12,24},{14,26},{16,28}... | collective-permute-start | bytes 196616 | tf_op jit(solution)/shard_map/ppermute | solution.py:178
  68.5 15.1 %collective-permute-start.7 = (bf16[256,128]{1,0:T(8,128)(2,1)S(1)}, bf16[256,128]{1,0:T(8,128)(2,1)S(1)}, u32[]{:S(2)}, u32[]{:S(2)}) collective-permute-start(bf16[256,128]{1,0:T(8,128)(2,1)S(1)} %get-tuple-element.27), channel_id=1, source_target_pairs={{0,28},{2,30},{4,0},{6,2},{8,4},{10,6},{12,8},{14,10},{16,12},{18,... | collective-permute-start | bytes 196616 | tf_op jit(solution)/shard_map/ppermute | solution.py:178
  74.9 9.1 %collective-permute-start.8 = (bf16[256,128]{1,0:T(8,128)(2,1)S(1)}, bf16[256,128]{1,0:T(8,128)(2,1)S(1)}, u32[]{:S(2)}, u32[]{:S(2)}) collective-permute-start(bf16[256,128]{1,0:T(8,128)(2,1)S(1)} %get-tuple-element.26), channel_id=1, source_target_pairs={{0,4},{2,6},{4,8},{6,10},{8,12},{10,14},{12,16},{14,18},{16,20},{1... | collective-permute-start | bytes 196616 | tf_op jit(solution)/shard_map/ppermute | solution.py:178
  85.0 22.8 %all-to-all-start.1 = ((bf16[32,16,128]{2,1,0:T(8,128)(2,1)}), bf16[32,16,128]{2,1,0:T(8,128)(2,1)S(1)}, u32[]{:S(2)}, u32[]{:S(2)}) async-start(bf16[32,16,128]{2,1,0:T(8,128)(2,1)} %bitcast.7), calls=%async_computation.1 | async-start | bytes 262144 | tf_op jit(solution)/shard_map/all_to_all | solution.py:168
  93.2 19.0 %collective-permute-start.10 = (bf16[256,128]{1,0:T(8,128)(2,1)S(1)}, bf16[256,128]{1,0:T(8,128)(2,1)S(1)}, u32[]{:S(2)}, u32[]{:S(2)}) collective-permute-start(bf16[256,128]{1,0:T(8,128)(2,1)S(1)} %get-tuple-element.24.refs_0_), channel_id=1, source_target_pairs={{0,64},{32,96},{64,0},{96,32},{1,65},{33,97},{65,1},{97,33},{2,66}... | collective-permute-start | bytes 196616 | tf_op jit(solution)/shard_map/ppermute | solution.py:261
  96.0 16.3 %collective-permute-start.11 = (bf16[256,128]{1,0:T(8,128)(2,1)S(1)}, bf16[256,128]{1,0:T(8,128)(2,1)S(1)}, u32[]{:S(2)}, u32[]{:S(2)}) collective-permute-start(bf16[256,128]{1,0:T(8,128)(2,1)S(1)} %get-tuple-element.24.refs_0_), channel_id=1, source_target_pairs={{0,96},{32,0},{64,32},{96,64},{1,97},{33,1},{65,33},{97,65},{2,98}... | collective-permute-start | bytes 196616 | tf_op jit(solution)/shard_map/ppermute | solution.py:261
  100.3 11.9 %collective-permute-start.9 = (bf16[256,128]{1,0:T(8,128)(2,1)S(1)}, bf16[256,128]{1,0:T(8,128)(2,1)S(1)}, u32[]{:S(2)}, u32[]{:S(2)}) collective-permute-start(bf16[256,128]{1,0:T(8,128)(2,1)S(1)} %get-tuple-element.24.refs_0_), channel_id=1, source_target_pairs={{0,32},{32,64},{64,96},{96,0},{1,33},{33,65},{65,97},{97,1},{2,34}... | collective-permute-start | bytes 196616 | tf_op jit(solution)/shard_map/ppermute | solution.py:261
  108.5 8.7 %all-to-all-start.2 = ((f32[4,16,128]{2,1,0:T(8,128)}), f32[4,16,128]{2,1,0:T(8,128)S(1)}, u32[]{:S(2)}, u32[]{:S(2)}) async-start(f32[4,16,128]{2,1,0:T(8,128)} %shard_map.114), calls=%async_computation.2 | async-start | bytes 65536 | tf_op jit(solution)/shard_map/all_to_all | solution.py:168

commit v5 on v4

--- a/solution.py
+++ b/solution.py
@@ -102,7 +102,8 @@
 
 
 def sum_kernel(left_ref, right_ref, out_ref):
-    out_ref[...] = left_ref[...].astype(F32) + right_ref[...].astype(F32)
+    total = left_ref[...].astype(F32) + right_ref[...].astype(F32)
+    out_ref[...] = total.astype(out_ref.dtype)
 
 
 def weight_kernel(*refs, scale):
@@ -227,9 +228,9 @@
     following = to_previous(first_part)
     rest_odd = to_previous(rest_odd)
     two, mark_two = partial((), 0, (BF16,))
-    one, keep, back, _ = partial((rest_odd, mark_two), 1, (BF16, F32, BF16))
-    some = whole(sum_kernel, (shape((nodes, hidden), F32),), (), (keep, along_z(two, 2)))[0]
-    one = along_z(one, 1)
+    one, keep, back, _ = partial((rest_odd, mark_two), 1, (F32, F32, BF16))
+    two = along_z(two, 1)
+    one = along_z(whole(sum_kernel, (shape((nodes, hidden), BF16),), (), (one, two))[0], 1)
     back = along_z(back, -1)
 
     spread = np.zeros((hidden, hidden), np.float32)
@@ -240,7 +241,7 @@
         near_kernel,
         (shape((REP, nodes, quarter), BF16),),
         (),
-        (some, one, back, spread),
+        (keep, one, back, spread),
     )[0]
     parts = exchange(parts, "rep")
     hops = (-2, -6, 6, 2)

time: 118 us -> 116 us (0.983)
  starting transfers between devices: 67.2 us -> 64.9 us
    ppermute x7, starting transfers between devices: 32 us -> 30.5 us  [along_z(): lax.ppermute(value, ('zh', 'zl'), [(z, (z + shift) % count) for z in rang...]
  transfers between devices with their start and end apart: 14 -> 14, of which waited for: 6 -> 7; matrix products, arithmetic and copies ran while one was open for 0% -> 0% of each run, Pallas kernels for 5% -> 6%
where the time goes in v5:
time: 116 us
  starting transfers between devices  64.9 us (56%)
  waiting for transfers between devices  27.3 us (24%)
  blocking collectives  10.8 us (9%)
  Pallas kernels  10.5 us (9%)
    ppermute x7, starting transfers between devices, along_z(): lax.ppermute(value, ('zh', 'zl'), [(z, (z + shift) % count) for z in rang...  30.5 us
    ppermute x2, starting transfers between devices, to_previous(): lax.ppermute(value, BLK, [(b, (b - 1) % count) for b in range(count)])  14.8 us
    ppermute x7, waiting for transfers between devices, along_z(): lax.ppermute(value, ('zh', 'zl'), [(z, (z + shift) % count) for z in rang...  12.4 us
    all_to_all x1, blocking collectives, exchange(): return lax.all_to_all(value, axes, 0, 0)  10.8 us
    all_to_all x2, starting transfers between devices, exchange(): return lax.all_to_all(value, axes, 0, 0)  10.7 us
    pallas_call x12, Pallas kernels, whole(): pl.pallas_call(kernel, in_specs=[pl.BlockSpec(memory_space=pltpu.SMEM)] *...  10.5 us
    all_to_all x2, waiting for transfers between devices, exchange(): return lax.all_to_all(value, axes, 0, 0)  9.35 us
    ppermute x3, starting transfers between devices, shards(): lax.ppermute(p_quarter, 'rep', [(r, (r + back) % REP) for r in range(REP)])  8.97 us
  transfers between devices with their start and end apart: 14, of which 7 were waited for; matrix products, arithmetic and copies ran while one was open for 0% of the time, Pallas kernels for 6%

profile of v5, /device:TPU:24, one launch (start us, length us, event | category | flops | bytes accessed | tf_op | source)
XLA Modules:
  0.0 115.8 jit_solution(10035431970098601041)
XLA Ops:
  0.6 0.0 copy-start
  0.6 0.0 copy-start.5
  0.7 0.0 copy-start.6
  0.7 0.0 copy-start.1
  0.7 0.0 copy-start.7
  0.7 2.1 %shard_map.104 = (bf16[256,768]{1,0:T(8,128)(2,1)}, f32[8,128]{1,0:T(8,128)}) custom-call(bf16[1,8,6,128,128]{4,3,2,1,0:T(8,128)(2,1)} %tiles_ref.5, s32[6,1,8]{2,1,0:T(1,128)} %bitcast.14, s32[6,1,8]{2,1,0:T(1,128)} %bitcast.17, s32[1,8]{1,0:T(1,128)} %refs_2_.5, bf16[256,512]{1,0:T(8,128)(2,1)} %refs_3_.2, bf16[256,512]{1,0:T(8,128)(2,1)} %refs_4_.1), custom_call_target="tpu_custom_call" | custom-call | tf_op jit(solution)/shard_map/pallas_call | solution.py:157
  2.8 2.7 %collective-permute-start = (bf16[256,768]{1,0:T(8,128)(2,1)}, bf16[256,768]{1,0:T(8,128)(2,1)S(1)}, u32[]{:S(2)}, u32[]{:S(2)}) collective-permute-start(bf16[256,768]{1,0:T(8,128)(2,1)} %get-tuple-element.16.own_ref), channel_id=1, source_target_pairs={{0,31},{1,0},{2,1},{3,2},{4,3},{5,4},{6,5},{7,6},{8,7},{9,8},{10,9... | collective-permute-start | bytes 1179656 | tf_op jit(solution)/shard_map/ppermute | solution.py:174
  5.5 0.0 copy-done.5
  5.5 0.0 copy-done.6
  5.5 0.0 copy-done.1
  5.5 0.0 copy-done.7
  5.5 0.0 copy-start.8
  5.5 0.7 copy-done.8
  6.2 0.0 copy-start.2
  6.2 1.5 %shard_map.105 = (bf16[256,1024]{1,0:T(8,128)(2,1)S(1)}, f32[8,128]{1,0:T(8,128)S(1)}) custom-call(bf16[1,8,6,128,128]{4,3,2,1,0:T(8,128)(2,1)S(1)} %copy-done.1, s32[6,1,8]{2,1,0:T(1,128)S(1)} %bitcast.15, s32[6,1,8]{2,1,0:T(1,128)S(1)} %bitcast.18, s32[1,8]{1,0:T(1,128)S(1)} %copy-done.7, f32[8,128]{1,0:T(8,128)S(1)} %copy-done.8), custom_call_target="tpu_custom_call" | custom-call | tf_op jit(solution)/shard_map/pallas_call | solution.py:157
  7.7 1.7 %shard_map.106 = (bf16[256,768]{1,0:T(8,128)(2,1)S(1)}, f32[8,128]{1,0:T(8,128)}) custom-call(bf16[1,8,6,128,128]{4,3,2,1,0:T(8,128)(2,1)S(1)} %copy-done.1, s32[6,1,8]{2,1,0:T(1,128)S(1)} %bitcast.16, s32[6,1,8]{2,1,0:T(1,128)S(1)} %bitcast.19, s32[1,8]{1,0:T(1,128)S(1)} %copy-done.7, f32[8,128]{1,0:T(8,128)S(1)} %get-tuple-element.17.refs_3_), custom_call_target="tpu_custom_call" | custom-call | tf_op jit(solution)/shard_map/pallas_call | solution.py:157
  9.4 12.1 %collective-permute-start.1 = (bf16[256,768]{1,0:T(8,128)(2,1)S(1)}, bf16[256,768]{1,0:T(8,128)(2,1)S(1)}, u32[]{:S(2)}, u32[]{:S(2)}) collective-permute-start(bf16[256,768]{1,0:T(8,128)(2,1)S(1)} %get-tuple-element.18), channel_id=1, source_target_pairs={{0,31},{1,0},{2,1},{3,2},{4,3},{5,4},{6,5},{7,6},{8,7},{9,8},{10,9... | collective-permute-start | bytes 1179656 | tf_op jit(solution)/shard_map/ppermute | solution.py:174
  21.5 0.0 collective-permute-done.next_ref
  21.5 0.0 copy-done.2
  21.5 0.3 shard_map.107
  21.8 0.0 copy-start.3
  21.8 2.1 %collective-permute-start.2 = (bf16[256,512]{1,0:T(8,128)(2,1)S(1)}, bf16[256,512]{1,0:T(8,128)(2,1)S(1)}, u32[]{:S(2)}, u32[]{:S(2)}) collective-permute-start(bf16[256,512]{1,0:T(8,128)(2,1)S(1)} %get-tuple-element.22), channel_id=1, source_target_pairs={{0,2},{2,4},{4,6},{6,8},{8,10},{10,12},{12,14},{14,16},{16,18},{18... | collective-permute-start | bytes 786440 | tf_op jit(solution)/shard_map/ppermute | solution.py:179
  23.9 5.6 %collective-permute-done.1.refs_0_ = bf16[256,768]{1,0:T(8,128)(2,1)S(1)} collective-permute-done((bf16[256,768]{1,0:T(8,128)(2,1)S(1)}, bf16[256,768]{1,0:T(8,128)(2,1)S(1)}, u32[]{:S(2)}, u32[]{:S(2)}) %collective-permute-start.1) | collective-permute-done | bytes 393248 | tf_op jit(solution)/shard_map/ppermute | solution.py:174
  29.5 1.1 shard_map.108
  30.6 8.2 %collective-permute-start.4 = (bf16[256,512]{1,0:T(8,128)(2,1)S(1)}, bf16[256,512]{1,0:T(8,128)(2,1)S(1)}, u32[]{:S(2)}, u32[]{:S(2)}) collective-permute-start(bf16[256,512]{1,0:T(8,128)(2,1)S(1)} %get-tuple-element.23), channel_id=1, source_target_pairs={{0,30},{2,0},{4,2},{6,4},{8,6},{10,8},{12,10},{14,12},{16,14},{18,... | collective-permute-start | bytes 786440 | tf_op jit(solution)/shard_map/ppermute | solution.py:179
  38.8 0.0 collective-permute-done.2.right_ref
  38.8 1.9 %collective-permute-start.3 = (bf16[256,512]{1,0:T(8,128)(2,1)S(1)}, bf16[256,512]{1,0:T(8,128)(2,1)S(1)}, u32[]{:S(2)}, u32[]{:S(2)}) collective-permute-start(bf16[256,512]{1,0:T(8,128)(2,1)S(1)} %shard_map.109), channel_id=1, source_target_pairs={{0,2},{2,4},{4,6},{6,8},{8,10},{10,12},{12,14},{14,16},{16,18},{18... | collective-permute-start | bytes 786440 | tf_op jit(solution)/shard_map/ppermute | solution.py:179
  40.8 2.6 %collective-permute-done.4.second_ref = bf16[256,512]{1,0:T(8,128)(2,1)S(1)} collective-permute-done((bf16[256,512]{1,0:T(8,128)(2,1)S(1)}, bf16[256,512]{1,0:T(8,128)(2,1)S(1)}, u32[]{:S(2)}, u32[]{:S(2)}) %collective-permute-start.4) | collective-permute-done | bytes 262176 | tf_op jit(solution)/shard_map/ppermute | solution.py:179
  43.4 5.4 %collective-permute-done.3.first_ref = bf16[256,512]{1,0:T(8,128)(2,1)S(1)} collective-permute-done((bf16[256,512]{1,0:T(8,128)(2,1)S(1)}, bf16[256,512]{1,0:T(8,128)(2,1)S(1)}, u32[]{:S(2)}, u32[]{:S(2)}) %collective-permute-start.3) | collective-permute-done | bytes 262176 | tf_op jit(solution)/shard_map/ppermute | solution.py:179
  48.8 0.0 copy-done.3
  48.8 0.0 copy-start.4
  48.8 0.4 shard_map.110
  49.3 10.8 %all_to_all.15 = bf16[4,256,128]{2,1,0:T(8,128)(2,1)S(1)} all-to-all(bf16[4,256,128]{2,1,0:T(8,128)(2,1)S(1)} %shard_map.110), channel_id=1, replica_groups=mesh['dp'=4,'rep'=4,'zh'=4,'zl'=4,'yl'=2] {'rep'}, dimensions={0} | all-to-all | bytes 524288 | tf_op jit(solution)/shard_map/all_to_all | solution.py:169
  60.1 3.9 %collective-permute-start.5 = (bf16[256,128]{1,0:T(8,128)(2,1)S(1)}, bf16[256,128]{1,0:T(8,128)(2,1)S(1)}, u32[]{:S(2)}, u32[]{:S(2)}) collective-permute-start(bf16[256,128]{1,0:T(8,128)(2,1)S(1)} %get-tuple-element.29), channel_id=1, source_target_pairs={{0,20},{2,22},{4,24},{6,26},{8,28},{10,30},{12,0},{14,2},{16,4},{1... | collective-permute-start | bytes 196616 | tf_op jit(solution)/shard_map/ppermute | solution.py:179
  64.0 7.6 %collective-permute-start.6 = (bf16[256,128]{1,0:T(8,128)(2,1)S(1)}, bf16[256,128]{1,0:T(8,128)(2,1)S(1)}, u32[]{:S(2)}, u32[]{:S(2)}) collective-permute-start(bf16[256,128]{1,0:T(8,128)(2,1)S(1)} %get-tuple-element.28), channel_id=1, source_target_pairs={{0,12},{2,14},{4,16},{6,18},{8,20},{10,22},{12,24},{14,26},{16,28}... | collective-permute-start | bytes 196616 | tf_op jit(solution)/shard_map/ppermute | solution.py:179
  71.7 2.1 %collective-permute-start.7 = (bf16[256,128]{1,0:T(8,128)(2,1)S(1)}, bf16[256,128]{1,0:T(8,128)(2,1)S(1)}, u32[]{:S(2)}, u32[]{:S(2)}) collective-permute-start(bf16[256,128]{1,0:T(8,128)(2,1)S(1)} %get-tuple-element.27), channel_id=1, source_target_pairs={{0,28},{2,30},{4,0},{6,2},{8,4},{10,6},{12,8},{14,10},{16,12},{18,... | collective-permute-start | bytes 196616 | tf_op jit(solution)/shard_map/ppermute | solution.py:179
  73.8 4.6 %collective-permute-start.8 = (bf16[256,128]{1,0:T(8,128)(2,1)S(1)}, bf16[256,128]{1,0:T(8,128)(2,1)S(1)}, u32[]{:S(2)}, u32[]{:S(2)}) collective-permute-start(bf16[256,128]{1,0:T(8,128)(2,1)S(1)} %get-tuple-element.26), channel_id=1, source_target_pairs={{0,4},{2,6},{4,8},{6,10},{8,12},{10,14},{12,16},{14,18},{16,20},{1... | collective-permute-start | bytes 196616 | tf_op jit(solution)/shard_map/ppermute | solution.py:179
  78.4 0.0 collective-permute-done.5.left_ref
  78.4 0.0 collective-permute-done.6.right_ref
  78.5 0.3 collective-permute-done.7.refs_1_
  78.7 4.1 %collective-permute-done.8.refs_2_ = bf16[256,128]{1,0:T(8,128)(2,1)S(1)} collective-permute-done((bf16[256,128]{1,0:T(8,128)(2,1)S(1)}, bf16[256,128]{1,0:T(8,128)(2,1)S(1)}, u32[]{:S(2)}, u32[]{:S(2)}) %collective-permute-start.8) | collective-permute-done | bytes 65568 | tf_op jit(solution)/shard_map/ppermute | solution.py:179
  82.8 0.0 copy-done.4
  82.8 0.9 shard_map.112
  83.7 7.5 %all-to-all-start.1 = ((bf16[32,16,128]{2,1,0:T(8,128)(2,1)}), bf16[32,16,128]{2,1,0:T(8,128)(2,1)S(1)}, u32[]{:S(2)}, u32[]{:S(2)}) async-start(bf16[32,16,128]{2,1,0:T(8,128)(2,1)} %bitcast.7), calls=%async_computation.1 | async-start | bytes 262144 | tf_op jit(solution)/shard_map/all_to_all | solution.py:169
  91.2 2.7 %collective-permute-start.10 = (bf16[256,128]{1,0:T(8,128)(2,1)S(1)}, bf16[256,128]{1,0:T(8,128)(2,1)S(1)}, u32[]{:S(2)}, u32[]{:S(2)}) collective-permute-start(bf16[256,128]{1,0:T(8,128)(2,1)S(1)} %get-tuple-element.24.refs_0_), channel_id=1, source_target_pairs={{0,64},{32,96},{64,0},{96,32},{1,65},{33,97},{65,1},{97,33},{2,66}... | collective-permute-start | bytes 196616 | tf_op jit(solution)/shard_map/ppermute | solution.py:262
  94.0 4.3 %collective-permute-start.11 = (bf16[256,128]{1,0:T(8,128)(2,1)S(1)}, bf16[256,128]{1,0:T(8,128)(2,1)S(1)}, u32[]{:S(2)}, u32[]{:S(2)}) collective-permute-start(bf16[256,128]{1,0:T(8,128)(2,1)S(1)} %get-tuple-element.24.refs_0_), channel_id=1, source_target_pairs={{0,96},{32,0},{64,32},{96,64},{1,97},{33,1},{65,33},{97,65},{2,98}... | collective-permute-start | bytes 196616 | tf_op jit(solution)/shard_map/ppermute | solution.py:262
  98.3 1.9 %collective-permute-start.9 = (bf16[256,128]{1,0:T(8,128)(2,1)S(1)}, bf16[256,128]{1,0:T(8,128)(2,1)S(1)}, u32[]{:S(2)}, u32[]{:S(2)}) collective-permute-start(bf16[256,128]{1,0:T(8,128)(2,1)S(1)} %get-tuple-element.24.refs_0_), channel_id=1, source_target_pairs={{0,32},{32,64},{64,96},{96,0},{1,33},{33,65},{65,97},{97,1},{2,34}... | collective-permute-start | bytes 196616 | tf_op jit(solution)/shard_map/ppermute | solution.py:262
  100.2 5.6 %all-to-all-done.1.in_ref = bf16[32,16,128]{2,1,0:T(8,128)(2,1)S(1)} async-done(((bf16[32,16,128]{2,1,0:T(8,128)(2,1)}), bf16[32,16,128]{2,1,0:T(8,128)(2,1)S(1)}, u32[]{:S(2)}, u32[]{:S(2)}) %all-to-all-start.1) | async-done | bytes 131104 | tf_op jit(solution)/shard_map/all_to_all | solution.py:169
  105.8 0.7 shard_map.114
  106.5 3.3 %all-to-all-start.2 = ((f32[4,16,128]{2,1,0:T(8,128)}), f32[4,16,128]{2,1,0:T(8,128)S(1)}, u32[]{:S(2)}, u32[]{:S(2)}) async-start(f32[4,16,128]{2,1,0:T(8,128)} %shard_map.114), calls=%async_computation.2 | async-start | bytes 65536 | tf_op jit(solution)/shard_map/all_to_all | solution.py:169
  109.7 0.0 copy-done
  109.7 0.5 convolution_convert_fusion.refs_4_
  110.2 0.0 collective-permute-done.10.refs_2_
  110.2 0.0 collective-permute-done.11.refs_3_
  110.2 0.0 collective-permute-done.9.refs_1_
  110.2 1.1 shard_map.113
  111.4 3.8 %all-to-all-done.2.in_ref = f32[4,16,128]{2,1,0:T(8,128)S(1)} async-done(((f32[4,16,128]{2,1,0:T(8,128)}), f32[4,16,128]{2,1,0:T(8,128)S(1)}, u32[]{:S(2)}, u32[]{:S(2)}) %all-to-all-start.2) | async-done | bytes 32800 | tf_op jit(solution)/shard_map/all_to_all | solution.py:169
  115.1 0.6 shard_map.115
  (3 shorter events, 0.1 us)
Async XLA Ops:
  0.6 109.1 %copy-start = (bf16[512,512]{1,0:T(8,128)(2,1)S(1)}, bf16[512,512]{1,0:T(8,128)(2,1)}, u32[]{:S(2)}) copy-start(bf16[512,512]{1,0:T(8,128)(2,1)} %param.12) | copy-start | bytes 1572868
  0.6 4.8 %copy-start.5 = (s32[1,8,6]{1,0,2:T(1,128)S(1)}, s32[1,8,6]{1,0,2:T(1,128)}, u32[]{:S(2)}) copy-start(s32[1,8,6]{1,0,2:T(1,128)} %param.14) | copy-start | bytes 580
  0.7 4.8 %copy-start.6 = (s32[1,8,6]{1,0,2:T(1,128)S(1)}, s32[1,8,6]{1,0,2:T(1,128)}, u32[]{:S(2)}) copy-start(s32[1,8,6]{1,0,2:T(1,128)} %param.15) | copy-start | bytes 580
  0.7 4.8 %copy-start.1 = (bf16[1,8,6,128,128]{4,3,2,1,0:T(8,128)(2,1)S(1)}, bf16[1,8,6,128,128]{4,3,2,1,0:T(8,128)(2,1)}, u32[]{:S(2)}) copy-start(bf16[1,8,6,128,128]{4,3,2,1,0:T(8,128)(2,1)} %tiles_ref.5) | copy-start | bytes 4718596
  0.7 4.8 %copy-start.7 = (s32[1,8]{1,0:T(1,128)S(1)}, s32[1,8]{1,0:T(1,128)}, u32[]{:S(2)}) copy-start(s32[1,8]{1,0:T(1,128)} %refs_2_.5) | copy-start | bytes 100
  2.8 18.7 %collective-permute-start = (bf16[256,768]{1,0:T(8,128)(2,1)}, bf16[256,768]{1,0:T(8,128)(2,1)S(1)}, u32[]{:S(2)}, u32[]{:S(2)}) collective-permute-start(bf16[256,768]{1,0:T(8,128)(2,1)} %get-tuple-element.16.own_ref), channel_id=1, source_target_pairs={{0,31},{1,0},{2,1},{3,2},{4,3},{5,4},{6,5},{7,6},{8,7},{9,8},{10,9... | collective-permute-start | bytes 1179656 | tf_op jit(solution)/shard_map/ppermute | solution.py:174
  5.5 0.7 copy-start.8
  6.2 15.3 %copy-start.2 = (bf16[256,768]{1,0:T(8,128)(2,1)S(1)}, bf16[256,768]{1,0:T(8,128)(2,1)}, u32[]{:S(2)}) copy-start(bf16[256,768]{1,0:T(8,128)(2,1)} %get-tuple-element.16.own_ref) | copy-start | bytes 1179652
  9.4 20.1 %collective-permute-start.1 = (bf16[256,768]{1,0:T(8,128)(2,1)S(1)}, bf16[256,768]{1,0:T(8,128)(2,1)S(1)}, u32[]{:S(2)}, u32[]{:S(2)}) collective-permute-start(bf16[256,768]{1,0:T(8,128)(2,1)S(1)} %get-tuple-element.18), channel_id=1, source_target_pairs={{0,31},{1,0},{2,1},{3,2},{4,3},{5,4},{6,5},{7,6},{8,7},{9,8},{10,9... | collective-permute-start | bytes 1179656 | tf_op jit(solution)/shard_map/ppermute | solution.py:174
  21.8 27.0 %copy-start.3 = (bf16[512,512]{1,0:T(8,128)(2,1)S(1)}, bf16[512,512]{1,0:T(8,128)(2,1)}, u32[]{:S(2)}) copy-start(bf16[512,512]{1,0:T(8,128)(2,1)} %constant.8.clone.spread_ref) | copy-start | bytes 1572868
  21.8 16.9 %collective-permute-start.2 = (bf16[256,512]{1,0:T(8,128)(2,1)S(1)}, bf16[256,512]{1,0:T(8,128)(2,1)S(1)}, u32[]{:S(2)}, u32[]{:S(2)}) collective-permute-start(bf16[256,512]{1,0:T(8,128)(2,1)S(1)} %get-tuple-element.22), channel_id=1, source_target_pairs={{0,2},{2,4},{4,6},{6,8},{8,10},{10,12},{12,14},{14,16},{16,18},{18... | collective-permute-start | bytes 786440 | tf_op jit(solution)/shard_map/ppermute | solution.py:179
  30.6 12.9 %collective-permute-start.4 = (bf16[256,512]{1,0:T(8,128)(2,1)S(1)}, bf16[256,512]{1,0:T(8,128)(2,1)S(1)}, u32[]{:S(2)}, u32[]{:S(2)}) collective-permute-start(bf16[256,512]{1,0:T(8,128)(2,1)S(1)} %get-tuple-element.23), channel_id=1, source_target_pairs={{0,30},{2,0},{4,2},{6,4},{8,6},{10,8},{12,10},{14,12},{16,14},{18,... | collective-permute-start | bytes 786440 | tf_op jit(solution)/shard_map/ppermute | solution.py:179
  38.8 10.0 %collective-permute-start.3 = (bf16[256,512]{1,0:T(8,128)(2,1)S(1)}, bf16[256,512]{1,0:T(8,128)(2,1)S(1)}, u32[]{:S(2)}, u32[]{:S(2)}) collective-permute-start(bf16[256,512]{1,0:T(8,128)(2,1)S(1)} %shard_map.109), channel_id=1, source_target_pairs={{0,2},{2,4},{4,6},{6,8},{8,10},{10,12},{12,14},{14,16},{16,18},{18... | collective-permute-start | bytes 786440 | tf_op jit(solution)/shard_map/ppermute | solution.py:179
  48.8 34.0 %copy-start.4 = (bf16[256,512]{1,0:T(8,128)(2,1)S(1)}, bf16[256,512]{1,0:T(8,128)(2,1)}, u32[]{:S(2)}) copy-start(bf16[256,512]{1,0:T(8,128)(2,1)} %refs_3_.3) | copy-start | bytes 786436
  60.1 18.3 %collective-permute-start.5 = (bf16[256,128]{1,0:T(8,128)(2,1)S(1)}, bf16[256,128]{1,0:T(8,128)(2,1)S(1)}, u32[]{:S(2)}, u32[]{:S(2)}) collective-permute-start(bf16[256,128]{1,0:T(8,128)(2,1)S(1)} %get-tuple-element.29), channel_id=1, source_target_pairs={{0,20},{2,22},{4,24},{6,26},{8,28},{10,30},{12,0},{14,2},{16,4},{1... | collective-permute-start | bytes 196616 | tf_op jit(solution)/shard_map/ppermute | solution.py:179
  64.0 14.4 %collective-permute-start.6 = (bf16[256,128]{1,0:T(8,128)(2,1)S(1)}, bf16[256,128]{1,0:T(8,128)(2,1)S(1)}, u32[]{:S(2)}, u32[]{:S(2)}) collective-permute-start(bf16[256,128]{1,0:T(8,128)(2,1)S(1)} %get-tuple-element.28), channel_id=1, source_target_pairs={{0,12},{2,14},{4,16},{6,18},{8,20},{10,22},{12,24},{14,26},{16,28}... | collective-permute-start | bytes 196616 | tf_op jit(solution)/shard_map/ppermute | solution.py:179
  71.7 7.1 %collective-permute-start.7 = (bf16[256,128]{1,0:T(8,128)(2,1)S(1)}, bf16[256,128]{1,0:T(8,128)(2,1)S(1)}, u32[]{:S(2)}, u32[]{:S(2)}) collective-permute-start(bf16[256,128]{1,0:T(8,128)(2,1)S(1)} %get-tuple-element.27), channel_id=1, source_target_pairs={{0,28},{2,30},{4,0},{6,2},{8,4},{10,6},{12,8},{14,10},{16,12},{18,... | collective-permute-start | bytes 196616 | tf_op jit(solution)/shard_map/ppermute | solution.py:179
  73.8 9.0 %collective-permute-start.8 = (bf16[256,128]{1,0:T(8,128)(2,1)S(1)}, bf16[256,128]{1,0:T(8,128)(2,1)S(1)}, u32[]{:S(2)}, u32[]{:S(2)}) collective-permute-start(bf16[256,128]{1,0:T(8,128)(2,1)S(1)} %get-tuple-element.26), channel_id=1, source_target_pairs={{0,4},{2,6},{4,8},{6,10},{8,12},{10,14},{12,16},{14,18},{16,20},{1... | collective-permute-start | bytes 196616 | tf_op jit(solution)/shard_map/ppermute | solution.py:179
  83.7 22.1 %all-to-all-start.1 = ((bf16[32,16,128]{2,1,0:T(8,128)(2,1)}), bf16[32,16,128]{2,1,0:T(8,128)(2,1)S(1)}, u32[]{:S(2)}, u32[]{:S(2)}) async-start(bf16[32,16,128]{2,1,0:T(8,128)(2,1)} %bitcast.7), calls=%async_computation.1 | async-start | bytes 262144 | tf_op jit(solution)/shard_map/all_to_all | solution.py:169
  91.2 19.0 %collective-permute-start.10 = (bf16[256,128]{1,0:T(8,128)(2,1)S(1)}, bf16[256,128]{1,0:T(8,128)(2,1)S(1)}, u32[]{:S(2)}, u32[]{:S(2)}) collective-permute-start(bf16[256,128]{1,0:T(8,128)(2,1)S(1)} %get-tuple-element.24.refs_0_), channel_id=1, source_target_pairs={{0,64},{32,96},{64,0},{96,32},{1,65},{33,97},{65,1},{97,33},{2,66}... | collective-permute-start | bytes 196616 | tf_op jit(solution)/shard_map/ppermute | solution.py:262
  94.0 16.3 %collective-permute-start.11 = (bf16[256,128]{1,0:T(8,128)(2,1)S(1)}, bf16[256,128]{1,0:T(8,128)(2,1)S(1)}, u32[]{:S(2)}, u32[]{:S(2)}) collective-permute-start(bf16[256,128]{1,0:T(8,128)(2,1)S(1)} %get-tuple-element.24.refs_0_), channel_id=1, source_target_pairs={{0,96},{32,0},{64,32},{96,64},{1,97},{33,1},{65,33},{97,65},{2,98}... | collective-permute-start | bytes 196616 | tf_op jit(solution)/shard_map/ppermute | solution.py:262
  98.3 11.9 %collective-permute-start.9 = (bf16[256,128]{1,0:T(8,128)(2,1)S(1)}, bf16[256,128]{1,0:T(8,128)(2,1)S(1)}, u32[]{:S(2)}, u32[]{:S(2)}) collective-permute-start(bf16[256,128]{1,0:T(8,128)(2,1)S(1)} %get-tuple-element.24.refs_0_), channel_id=1, source_target_pairs={{0,32},{32,64},{64,96},{96,0},{1,33},{33,65},{65,97},{97,1},{2,34}... | collective-permute-start | bytes 196616 | tf_op jit(solution)/shard_map/ppermute | solution.py:262
  106.5 8.7 %all-to-all-start.2 = ((f32[4,16,128]{2,1,0:T(8,128)}), f32[4,16,128]{2,1,0:T(8,128)S(1)}, u32[]{:S(2)}, u32[]{:S(2)}) async-start(f32[4,16,128]{2,1,0:T(8,128)} %shard_map.114), calls=%async_computation.2 | async-start | bytes 65536 | tf_op jit(solution)/shard_map/all_to_all | solution.py:169

commit v6 on v5

v6 whole, which is shorter than its diff:
```python
import functools

import jax
import jax.numpy as jnp
import numpy as np
from jax import lax
from jax.experimental import pallas as pl
from jax.experimental.pallas import tpu as pltpu
from jax.sharding import Mesh, PartitionSpec as P

ZH, ZL, YL, REP = 4, 4, 2, 4
BLK = ("zh", "zl", "yl")
BF16, F32 = jnp.bfloat16, jnp.float32


def contract_rows(left, right):
    return lax.dot_general(left, right, (((0,), (0,)), ((), ())), preferred_element_type=F32)


def hidden_order(width):
    units = np.arange(width).reshape(ZH * ZL * YL, REP, -1)
    return units.transpose(1, 2, 0).reshape(-1)


def masked(pre_act, upstream):
    return jnp.where(pre_act > 0, upstream, jnp.zeros_like(upstream))


def step_of(odd, role, yl, last):
    return 2 * jnp.where(yl == 0, last - role, role) + 1 if odd else 2 * role


def term(tile_at, rows_ref, cols_ref, count_ref, step, own, out_ref, acc_ref):
    acc_ref[...] = jnp.zeros_like(acc_ref)
    live = count_ref[0, step]
    for q in range(rows_ref.shape[0]):

        @pl.when(q < live)
        def _():
            acc_ref[rows_ref[q, 0, step], cols_ref[q, 0, step]] += tile_at(q).astype(F32)

    dense = jnp.concatenate(
        [jnp.concatenate([acc_ref[row, col] for col in range(2)], axis=1) for row in range(2)],
        axis=0,
    ).astype(BF16)
    out_ref[...] = contract_rows(dense, own).astype(out_ref.dtype)


def first_kernel(yl_ref, *refs, odd, role):
    tiles_ref, *sources, out_ref, held_ref = refs[:8]
    *held, acc_ref, sems = refs[8:]
    step = step_of(odd, role, yl_ref[0], tiles_ref.shape[1] // 2 - 1)
    copies = [
        pltpu.make_async_copy(source, kept, sems.at[at])
        for at, (source, kept) in enumerate(
            [*zip(sources, held), (tiles_ref.at[0, step], held_ref)]
        )
    ]
    for copy in copies:
        copy.start()
    for copy in copies:
        copy.wait()
    rows_ref, cols_ref, count_ref, pre_ref, up_ref = held
    own = masked(pre_ref[...], up_ref[...])
    term(lambda q: held_ref[q], rows_ref, cols_ref, count_ref, step, own, out_ref, acc_ref)


def terms_kernel(yl_ref, rows_ref, cols_ref, count_ref, tiles_ref, pre_ref, up_ref, *refs, roles):
    *out_refs, mark_ref, acc_ref, own_ref = refs[len(refs) - len(roles) - 3 :]
    mark_ref[...] = jnp.zeros_like(mark_ref)
    own_ref[...] = masked(pre_ref[...], up_ref[...])
    last = tiles_ref.shape[1] // 2 - 1
    for (odd, role), out_ref in zip(roles, out_refs):
        step = step_of(odd, role, yl_ref[0], last)
        term(
            lambda q: tiles_ref[0, step, q],
            rows_ref,
            cols_ref,
            count_ref,
            step,
            own_ref[...],
            out_ref,
            acc_ref,
        )


def gather_kernel(keep_ref, first_ref, second_ref, out_ref):
    total = keep_ref[...] + first_ref[...].astype(F32) + second_ref[...].astype(F32)
    out_ref[...] = total.astype(BF16)


def near_kernel(yl_ref, other_ref, keep_ref, first_ref, second_ref, spread_ref, out_ref):
    quarter = out_ref.shape[2]
    total = keep_ref[...] + first_ref[...].astype(F32) + second_ref[...].astype(F32)
    for low, lane in ((total.astype(BF16), yl_ref[0]), (other_ref[...], 1 - yl_ref[0])):
        for q in range(REP):
            span = slice(q * quarter, (q + 1) * quarter)
            out_ref[YL * q + lane] = jnp.dot(
                low, spread_ref[:, span], preferred_element_type=F32
            ).astype(BF16)


def sides_kernel(in_ref, *out_refs):
    for r, out_ref in enumerate(out_refs):
        total = in_ref[YL * r].astype(F32)
        for side in range(1, YL):
            total += in_ref[YL * r + side].astype(F32)
        out_ref[...] = total.astype(BF16)


def sum_kernel(left_ref, right_ref, out_ref, *mark_refs):
    for mark_ref in mark_refs:
        mark_ref[...] = jnp.zeros_like(mark_ref)
    total = left_ref[...].astype(F32) + right_ref[...].astype(F32)
    out_ref[...] = total.astype(out_ref.dtype)


def weight_kernel(*refs, scale):
    *in_refs, feat_ref, p_ref, gw_ref, lines_ref = refs
    total = in_refs[0][...].astype(F32)
    for in_ref in in_refs[1:]:
        total += in_ref[...].astype(F32)
    p_ref[...] = total.astype(BF16)
    gw = contract_rows(p_ref[...], feat_ref[...]) * scale
    quarter = lines_ref.shape[1]
    spots = ZH * ZL * YL
    rows, pieces = gw.shape[0] // spots, gw.shape[1] // quarter
    for i in range(rows):
        for f in range(pieces):
            lines_ref[pl.ds(f * rows + i, spots, rows * pieces), :] = gw[
                i * spots : (i + 1) * spots, f * quarter : (f + 1) * quarter
            ]
    gw_ref[...] = lines_ref[...].astype(BF16)


def pair_kernel(own_ref, other_ref, out_ref):
    out_ref[0] = own_ref[...]
    out_ref[1] = other_ref[...]


def feature_kernel(lane_ref, own_ref, other_ref, weight_ref, feat_ref):
    quarter = own_ref.shape[2]
    total = jnp.zeros(feat_ref.shape, F32)
    for at in range(REP):
        source = lane_ref[0] ^ at
        span = pl.ds(pl.multiple_of(source * quarter, quarter), quarter)
        part = (own_ref if at < 2 else other_ref)[at % 2]
        total += jnp.dot(part, weight_ref[span, :], preferred_element_type=F32)
    feat_ref[...] = total.astype(BF16)


def copies_kernel(in_ref, out_ref):
    total = in_ref[0].astype(F32)
    for d in range(1, in_ref.shape[0]):
        total += in_ref[d].astype(F32)
    for r in range(out_ref.shape[0]):
        out_ref[r] = total


def lines_kernel(in_ref, gw_ref):
    lanes, lines, quarter = in_ref.shape
    pieces = gw_ref.shape[1] // quarter
    rows = lines // pieces
    for q in range(lanes):
        for f in range(pieces):
            gw_ref[q * rows : (q + 1) * rows, f * quarter : (f + 1) * quarter] = in_ref[
                q, f * rows : (f + 1) * rows, :
            ]


def whole(kernel, outs, scalars, arrays, scratch=(), space=pltpu.VMEM, limit=48):
    return pl.pallas_call(
        kernel,
        in_specs=[pl.BlockSpec(memory_space=pltpu.SMEM)] * len(scalars)
        + [pl.BlockSpec(memory_space=space)] * len(arrays),
        out_specs=jax.tree.map(lambda _: pl.BlockSpec(memory_space=pltpu.VMEM), outs),
        out_shape=outs,
        scratch_shapes=scratch,
        compiler_params=pltpu.CompilerParams(vmem_limit_bytes=limit * 1024 * 1024),
    )(*scalars, *arrays)


def exchange(value, axes):
    return lax.all_to_all(value, axes, 0, 0)


def along_z(value, shift):
    count = ZH * ZL
    return lax.ppermute(value, ("zh", "zl"), [(z, (z + shift) % count) for z in range(count)])


def turned_along_z(value, shift):
    count = ZH * ZL
    pairs = [
        (z * YL + y, (z + (shift if y else -shift)) % count * YL + y)
        for z in range(count)
        for y in range(YL)
    ]
    return lax.ppermute(value, BLK, pairs)


def shards(features, pre_act, upstream, weight, tile_values, tile_rows, tile_cols, tile_count):
    _, steps, slots, tile, _ = tile_values.shape
    nodes, width = features.shape
    hidden = upstream.shape[1]
    quarter = width // REP
    scale = float(nodes * ZH * ZL * YL) ** -0.5
    shape = jax.ShapeDtypeStruct

    lists = (tile_rows.transpose(2, 0, 1), tile_cols.transpose(2, 0, 1), tile_count)
    mark = shape((8, tile), F32)

    yl = lax.axis_index("yl").reshape(1)

    gates = (pre_act, upstream)
    block = shape((nodes, hidden), BF16)
    acc = pltpu.VMEM((2, 2, tile, tile), F32)

    def terms(roles, kinds, marks=()):
        return whole(
            functools.partial(terms_kernel, roles=roles),
            tuple(shape((nodes, hidden), kind) for kind in kinds) + (mark,),
            (yl, *lists),
            (tile_values, *gates, *marks),
            (acc, pltpu.VMEM(block.shape, block.dtype)),
        )

    far_other = whole(
        functools.partial(first_kernel, odd=1, role=0),
        (block,),
        (yl,),
        (tile_values, *lists, *gates),
        (
            pltpu.VMEM((slots, tile, tile), BF16),
            *(pltpu.SMEM(listed.shape, listed.dtype) for listed in lists),
            *(pltpu.VMEM(gate.shape, gate.dtype) for gate in gates),
            acc,
            pltpu.SemaphoreType.DMA((6,)),
        ),
        pltpu.HBM,
        60,
    )[0]
    far_same, back_other, mid_other, _ = terms(((0, 0), (1, 3), (1, 1)), (BF16, BF16, F32))
    mid_other, mark_other = whole(
        sum_kernel, (block, mark), (), (mid_other, turned_along_z(far_other, 1))
    )
    mid_same, back_same, keep_other, keep_same, _ = terms(
        ((0, 1), (0, 3), (1, 2), (0, 2)), (F32, BF16, F32, F32), (mark_other,)
    )
    mid_same = whole(sum_kernel, (block,), (), (mid_same, along_z(far_same, 1)))[0]
    mid_other = turned_along_z(mid_other, 1)
    back_other = turned_along_z(back_other, -1)
    mid_same = along_z(mid_same, 1)
    back_same = along_z(back_same, -1)
    other = whole(gather_kernel, (block,), (), (keep_other, mid_other, back_other))[0]

    spread = np.zeros((hidden, hidden), np.float32)
    spread[hidden_order(hidden), np.arange(hidden)] = 1.0
    spread = jnp.asarray(spread, BF16)
    weight = contract_rows(spread, weight).astype(BF16)
    parts = whole(
        near_kernel,
        (shape((REP * YL, nodes, quarter), BF16),),
        (yl,),
        (other, keep_same, mid_same, back_same, spread),
    )[0]
    parts = exchange(parts, ("rep", "yl"))
    parts = whole(sides_kernel, (shape((nodes, quarter), BF16),) * REP, (), (parts,))
    hops = (-2, -6, 6, 2)
    parts = [along_z(parts[r], hops[r]) for r in range(REP)]
    far = whole(sum_kernel, (shape((nodes, quarter), F32),), (), (parts[1], parts[2]))[0]
    p_quarter, gw = whole(
        functools.partial(weight_kernel, scale=scale),
        (shape((nodes, quarter), BF16), shape((hidden, quarter), BF16)),
        (),
        (far, parts[0], parts[3], features),
        (pltpu.VMEM((hidden, quarter), F32),),
    )
    gw = exchange(gw.reshape(ZH * ZL * YL, -1, quarter), BLK)
    gw = whole(copies_kernel, (shape((REP,) + gw.shape[1:], F32),), (), (gw,))[0]
    gw = exchange(gw, "rep")
    lane = lax.axis_index("rep").reshape(1)
    other = lax.ppermute(p_quarter, "rep", [(r, r ^ 1) for r in range(REP)])
    pair = whole(pair_kernel, (shape((2, nodes, quarter), BF16),), (), (p_quarter, other))[0]
    others = lax.ppermute(pair, "rep", [(r, r ^ 2) for r in range(REP)])
    grad_feat = whole(
        feature_kernel, (shape((nodes, width), BF16),), (lane,), (pair, others, weight)
    )[0]
    rows = hidden // (ZH * ZL * YL)
    grad_weight = whole(lines_kernel, (shape((rows, width), F32),), (), (gw,))[0]
    return grad_feat, grad_weight


def solution(mesh):
    dp = mesh.shape["dp"]
    fine = Mesh(mesh.devices.reshape(dp, REP, ZH, ZL, YL), ("dp", "rep") + BLK)
    rows = ("dp",) + BLK
    return jax.shard_map(
        shards,
        mesh=fine,
        in_specs=(
            P(rows, None),
            P(rows, None),
            P(rows, None),
            P(),
            P(rows, "rep", None, None, None),
            P(rows, "rep", None),
            P(rows, "rep", None),
            P(rows, "rep"),
        ),
        out_specs=(P(rows, None), P(rows, None)),
        check_vma=False,
    )
```

time: 116 us -> 115 us (level)
  blocking collectives: 10.8 us -> 13 us
  starting transfers between devices: 64.9 us -> 62.9 us
    ppermute x5, starting transfers between devices: 23.7 us -> 19.4 us  [the longest x3 13.5 us: turned_along_z(): return lax.ppermute(value, BLK, pairs)]
    all_to_all x2, starting transfers between devices: 10.7 us -> 14.2 us  [exchange(): return lax.all_to_all(value, axes, 0, 0)]
    ppermute x7, waiting for transfers between devices: 12.4 us -> 10.1 us  [along_z(): lax.ppermute(value, ('zh', 'zl'), [(z, (z + shift) % count) for z in rang...]
    all_to_all x1, blocking collectives: 10.8 us -> 13 us  [exchange(): return lax.all_to_all(value, axes, 0, 0)]
    ppermute x5, waiting for transfers between devices: 5.61 us -> 7.71 us  [the longest x3 4.02 us: turned_along_z(): return lax.ppermute(value, BLK, pairs)]
    ppermute x7, starting transfers between devices: 30.5 us -> 29.3 us  [along_z(): lax.ppermute(value, ('zh', 'zl'), [(z, (z + shift) % count) for z in rang...]
    pallas_call x12 -> x14, Pallas kernels: 10.5 us -> 10.6 us  [whole(): pl.pallas_call(kernel, in_specs=[pl.BlockSpec(memory_space=pltpu.SMEM)] *...]
  transfers between devices with their start and end apart: 14 -> 14, of which waited for: 7 -> 9; matrix products, arithmetic and copies ran while one was open for 0% -> 0% of each run, Pallas kernels for 6% -> 5%
where the time goes in v6:
time: 115 us
  starting transfers between devices  62.9 us (55%)
  waiting for transfers between devices  26.5 us (23%)
  blocking collectives  13 us (11%)
  Pallas kernels  10.6 us (9%)
    ppermute x7, starting transfers between devices, along_z(): lax.ppermute(value, ('zh', 'zl'), [(z, (z + shift) % count) for z in rang...  29.3 us
    all_to_all x2, starting transfers between devices, exchange(): return lax.all_to_all(value, axes, 0, 0)  14.2 us
    ppermute x3, starting transfers between devices, turned_along_z(): return lax.ppermute(value, BLK, pairs)  13.5 us
    all_to_all x1, blocking collectives, exchange(): return lax.all_to_all(value, axes, 0, 0)  13 us
    pallas_call x14, Pallas kernels, whole(): pl.pallas_call(kernel, in_specs=[pl.BlockSpec(memory_space=pltpu.SMEM)] *...  10.6 us
    ppermute x7, waiting for transfers between devices, along_z(): lax.ppermute(value, ('zh', 'zl'), [(z, (z + shift) % count) for z in rang...  10.1 us
    all_to_all x2, waiting for transfers between devices, exchange(): return lax.all_to_all(value, axes, 0, 0)  8.77 us
    ppermute x3, waiting for transfers between devices, turned_along_z(): return lax.ppermute(value, BLK, pairs)  4.02 us
  transfers between devices with their start and end apart: 14, of which 9 were waited for; matrix products, arithmetic and copies ran while one was open for 0% of the time, Pallas kernels for 5%

profile of v6, /device:TPU:24, one launch (start us, length us, event | category | flops | bytes accessed | tf_op | source)
XLA Modules:
  0.0 114.5 jit_solution(1205149250916686394)
XLA Ops:
  0.6 0.0 copy-start
  0.6 0.0 copy-start.6
  0.7 0.0 copy-start.7
  0.7 0.0 copy-start.2
  0.7 0.0 copy-start.3
  0.7 0.0 copy-start.1
  0.7 0.0 copy-start.8
  0.7 2.3 %shard_map.105 = bf16[256,512]{1,0:T(8,128)(2,1)} custom-call(s32[1]{0:T(128)} %bitcast.1.yl_ref, bf16[1,8,6,128,128]{4,3,2,1,0:T(8,128)(2,1)} %tiles_ref.3, s32[6,1,8]{2,1,0:T(1,128)} %bitcast.7, s32[6,1,8]{2,1,0:T(1,128)} %bitcast.10, s32[1,8]{1,0:T(1,128)} %count_ref.3, bf16[256,512]{1,0:T(8,128)(2,1)} %pre_ref.3, bf16[256,512]{1,0:T(8,128)(2,1)} %up_ref.3), custom_call_target="tpu_custom_call" | custom-call | tf_op jit(solution)/shard_map/pallas_call | solution.py:172
  3.0 3.9 %collective-permute-start = (bf16[256,512]{1,0:T(8,128)(2,1)}, bf16[256,512]{1,0:T(8,128)(2,1)S(1)}, u32[]{:S(2)}, u32[]{:S(2)}) collective-permute-start(bf16[256,512]{1,0:T(8,128)(2,1)} %shard_map.105), channel_id=1, source_target_pairs={{0,30},{1,3},{2,0},{3,5},{4,2},{5,7},{6,4},{7,9},{8,6},{9,11},{10,... | collective-permute-start | bytes 786440 | tf_op jit(solution)/shard_map/ppermute | solution.py:199
  6.9 0.0 copy-done.6
  6.9 0.0 copy-done.7
  6.9 0.0 copy-done.2
  6.9 0.0 copy-done.3
  6.9 0.0 copy-done.1
  6.9 0.0 copy-done.8
  7.0 1.9 %shard_map.104 = (bf16[256,512]{1,0:T(8,128)(2,1)S(1)}, bf16[256,512]{1,0:T(8,128)(2,1)S(1)}, f32[256,512]{1,0:T(8,128)S(1)}, f32[8,128]{1,0:T(8,128)}) custom-call(s32[1]{0:T(128)} %bitcast.1.yl_ref, s32[6,1,8]{2,1,0:T(1,128)S(1)} %bitcast.8, s32[6,1,8]{2,1,0:T(1,128)S(1)} %bitcast.11, s32[1,8]{1,0:T(1,128)S(1)} %copy-done.8, ...), custom_call_target="tpu_custom_call" | custom-call | tf_op jit(solution)/shard_map/pallas_call | solution.py:172
  8.8 3.8 %collective-permute-start.3 = (bf16[256,512]{1,0:T(8,128)(2,1)S(1)}, bf16[256,512]{1,0:T(8,128)(2,1)S(1)}, u32[]{:S(2)}, u32[]{:S(2)}) collective-permute-start(bf16[256,512]{1,0:T(8,128)(2,1)S(1)} %get-tuple-element.24), channel_id=1, source_target_pairs={{0,2},{2,4},{4,6},{6,8},{8,10},{10,12},{12,14},{14,16},{16,18},{18... | collective-permute-start | bytes 786440 | tf_op jit(solution)/shard_map/ppermute | solution.py:189
  12.7 7.6 %collective-permute-start.2 = (bf16[256,512]{1,0:T(8,128)(2,1)S(1)}, bf16[256,512]{1,0:T(8,128)(2,1)S(1)}, u32[]{:S(2)}, u32[]{:S(2)}) collective-permute-start(bf16[256,512]{1,0:T(8,128)(2,1)S(1)} %get-tuple-element.21), channel_id=1, source_target_pairs={{0,2},{1,31},{2,4},{3,1},{4,6},{5,3},{6,8},{7,5},{8,10},{9,7},{10,... | collective-permute-start | bytes 786440 | tf_op jit(solution)/shard_map/ppermute | solution.py:199
  20.3 1.5 %collective-permute-done.right_ref = bf16[256,512]{1,0:T(8,128)(2,1)S(1)} collective-permute-done((bf16[256,512]{1,0:T(8,128)(2,1)}, bf16[256,512]{1,0:T(8,128)(2,1)S(1)}, u32[]{:S(2)}, u32[]{:S(2)}) %collective-permute-start) | collective-permute-done | bytes 262176 | tf_op jit(solution)/shard_map/ppermute | solution.py:199
  21.8 2.2 %shard_map.107 = (f32[256,512]{1,0:T(8,128)S(1)}, bf16[256,512]{1,0:T(8,128)(2,1)S(1)}, f32[256,512]{1,0:T(8,128)S(1)}, f32[256,512]{1,0:T(8,128)S(1)}, f32[8,128]{1,0:T(8,128)}) custom-call(s32[1]{0:T(128)} %bitcast.1.yl_ref, s32[6,1,8]{2,1,0:T(1,128)S(1)} %bitcast.9, s32[6,1,8]{2,1,0:T(1,128)S(1)} %bitcast.12, s32[1,8]{1,0:T(1,128)S(1)} %copy-done.8, ...), custom_call_target="tpu_custom_call" | custom-call | tf_op jit(solution)/shard_map/pallas_call | solution.py:172
  24.0 0.0 copy-start.4
  24.0 2.0 %collective-permute-start.1 = (bf16[256,512]{1,0:T(8,128)(2,1)S(1)}, bf16[256,512]{1,0:T(8,128)(2,1)S(1)}, u32[]{:S(2)}, u32[]{:S(2)}) collective-permute-start(bf16[256,512]{1,0:T(8,128)(2,1)S(1)} %get-tuple-element.20), channel_id=1, source_target_pairs={{0,30},{1,3},{2,0},{3,5},{4,2},{5,7},{6,4},{7,9},{8,6},{9,11},{10,... | collective-permute-start | bytes 786440 | tf_op jit(solution)/shard_map/ppermute | solution.py:199
  26.1 0.5 collective-permute-done.3.right_ref
  26.6 1.9 %collective-permute-start.4 = (bf16[256,512]{1,0:T(8,128)(2,1)S(1)}, bf16[256,512]{1,0:T(8,128)(2,1)S(1)}, u32[]{:S(2)}, u32[]{:S(2)}) collective-permute-start(bf16[256,512]{1,0:T(8,128)(2,1)S(1)} %shard_map.109), channel_id=1, source_target_pairs={{0,2},{2,4},{4,6},{6,8},{8,10},{10,12},{12,14},{14,16},{16,18},{18... | collective-permute-start | bytes 786440 | tf_op jit(solution)/shard_map/ppermute | solution.py:189
  28.6 5.1 %collective-permute-start.5 = (bf16[256,512]{1,0:T(8,128)(2,1)S(1)}, bf16[256,512]{1,0:T(8,128)(2,1)S(1)}, u32[]{:S(2)}, u32[]{:S(2)}) collective-permute-start(bf16[256,512]{1,0:T(8,128)(2,1)S(1)} %get-tuple-element.25), channel_id=1, source_target_pairs={{0,30},{2,0},{4,2},{6,4},{8,6},{10,8},{12,10},{14,12},{16,14},{18,... | collective-permute-start | bytes 786440 | tf_op jit(solution)/shard_map/ppermute | solution.py:189
  33.7 0.0 collective-permute-done.2.second_ref
  33.7 2.5 %collective-permute-done.1.first_ref = bf16[256,512]{1,0:T(8,128)(2,1)S(1)} collective-permute-done((bf16[256,512]{1,0:T(8,128)(2,1)S(1)}, bf16[256,512]{1,0:T(8,128)(2,1)S(1)}, u32[]{:S(2)}, u32[]{:S(2)}) %collective-permute-start.1) | collective-permute-done | bytes 262176 | tf_op jit(solution)/shard_map/ppermute | solution.py:199
  36.2 0.1 shard_map.108.other_ref
  36.3 3.2 %collective-permute-done.4.first_ref = bf16[256,512]{1,0:T(8,128)(2,1)S(1)} collective-permute-done((bf16[256,512]{1,0:T(8,128)(2,1)S(1)}, bf16[256,512]{1,0:T(8,128)(2,1)S(1)}, u32[]{:S(2)}, u32[]{:S(2)}) %collective-permute-start.4) | collective-permute-done | bytes 262176 | tf_op jit(solution)/shard_map/ppermute | solution.py:189
  39.5 0.0 collective-permute-done.5.second_ref
  39.5 0.0 copy-done.4
  39.5 0.0 copy-start.5
  39.6 0.7 shard_map.110
  40.3 13.0 %all_to_all.15.in_ref = bf16[8,256,128]{2,1,0:T(8,128)(2,1)S(1)} all-to-all(bf16[8,256,128]{2,1,0:T(8,128)(2,1)S(1)} %shard_map.110), channel_id=1, replica_groups=mesh['dp'=4,'rep'=4,'zh'=4,'zl'=4,'yl'=2] {'rep','yl'}, dimensions={0} | all-to-all | bytes 1048576 | tf_op jit(solution)/shard_map/all_to_all | solution.py:184
  53.3 0.1 shard_map.111
  53.4 7.5 %collective-permute-start.6 = (bf16[256,128]{1,0:T(8,128)(2,1)S(1)}, bf16[256,128]{1,0:T(8,128)(2,1)S(1)}, u32[]{:S(2)}, u32[]{:S(2)}) collective-permute-start(bf16[256,128]{1,0:T(8,128)(2,1)S(1)} %get-tuple-element.26), channel_id=1, source_target_pairs={{0,20},{2,22},{4,24},{6,26},{8,28},{10,30},{12,0},{14,2},{16,4},{1... | collective-permute-start | bytes 196616 | tf_op jit(solution)/shard_map/ppermute | solution.py:189
  60.8 4.1 %collective-permute-start.7 = (bf16[256,128]{1,0:T(8,128)(2,1)S(1)}, bf16[256,128]{1,0:T(8,128)(2,1)S(1)}, u32[]{:S(2)}, u32[]{:S(2)}) collective-permute-start(bf16[256,128]{1,0:T(8,128)(2,1)S(1)} %get-tuple-element.27), channel_id=1, source_target_pairs={{0,12},{2,14},{4,16},{6,18},{8,20},{10,22},{12,24},{14,26},{16,28}... | collective-permute-start | bytes 196616 | tf_op jit(solution)/shard_map/ppermute | solution.py:189
  64.9 4.9 %collective-permute-start.8 = (bf16[256,128]{1,0:T(8,128)(2,1)S(1)}, bf16[256,128]{1,0:T(8,128)(2,1)S(1)}, u32[]{:S(2)}, u32[]{:S(2)}) collective-permute-start(bf16[256,128]{1,0:T(8,128)(2,1)S(1)} %get-tuple-element.28), channel_id=1, source_target_pairs={{0,28},{2,30},{4,0},{6,2},{8,4},{10,6},{12,8},{14,10},{16,12},{18,... | collective-permute-start | bytes 196616 | tf_op jit(solution)/shard_map/ppermute | solution.py:189
  69.9 1.9 %collective-permute-start.9 = (bf16[256,128]{1,0:T(8,128)(2,1)S(1)}, bf16[256,128]{1,0:T(8,128)(2,1)S(1)}, u32[]{:S(2)}, u32[]{:S(2)}) collective-permute-start(bf16[256,128]{1,0:T(8,128)(2,1)S(1)} %get-tuple-element.29), channel_id=1, source_target_pairs={{0,4},{2,6},{4,8},{6,10},{8,12},{10,14},{12,16},{14,18},{16,20},{1... | collective-permute-start | bytes 196616 | tf_op jit(solution)/shard_map/ppermute | solution.py:189
  71.8 0.0 collective-permute-done.6.left_ref
  71.8 2.7 %collective-permute-done.7.right_ref = bf16[256,128]{1,0:T(8,128)(2,1)S(1)} collective-permute-done((bf16[256,128]{1,0:T(8,128)(2,1)S(1)}, bf16[256,128]{1,0:T(8,128)(2,1)S(1)}, u32[]{:S(2)}, u32[]{:S(2)}) %collective-permute-start.7) | collective-permute-done | bytes 65568 | tf_op jit(solution)/shard_map/ppermute | solution.py:189
  74.5 0.0 collective-permute-done.8.refs_1_
  74.5 3.6 %collective-permute-done.9.refs_2_ = bf16[256,128]{1,0:T(8,128)(2,1)S(1)} collective-permute-done((bf16[256,128]{1,0:T(8,128)(2,1)S(1)}, bf16[256,128]{1,0:T(8,128)(2,1)S(1)}, u32[]{:S(2)}, u32[]{:S(2)}) %collective-permute-start.9) | collective-permute-done | bytes 65568 | tf_op jit(solution)/shard_map/ppermute | solution.py:189
  78.2 0.0 copy-done.5
  78.2 0.9 shard_map.113
  79.1 10.9 %all-to-all-start.1 = ((bf16[32,16,128]{2,1,0:T(8,128)(2,1)}), bf16[32,16,128]{2,1,0:T(8,128)(2,1)S(1)}, u32[]{:S(2)}, u32[]{:S(2)}) async-start(bf16[32,16,128]{2,1,0:T(8,128)(2,1)} %bitcast.4), calls=%async_computation.1 | async-start | bytes 262144 | tf_op jit(solution)/shard_map/all_to_all | solution.py:184
  90.0 2.5 %collective-permute-start.10 = (bf16[256,128]{1,0:T(8,128)(2,1)S(1)}, bf16[256,128]{1,0:T(8,128)(2,1)S(1)}, u32[]{:S(2)}, u32[]{:S(2)}) collective-permute-start(bf16[256,128]{1,0:T(8,128)(2,1)S(1)} %get-tuple-element.30.own_ref), channel_id=1, source_target_pairs={{0,32},{32,0},{64,96},{96,64},{1,33},{33,1},{65,97},{97,65},{2,34}... | collective-permute-start | bytes 196616 | tf_op jit(solution)/shard_map/ppermute | solution.py:283
  92.5 3.7 %collective-permute-done.10.other_ref = bf16[256,128]{1,0:T(8,128)(2,1)S(1)} collective-permute-done((bf16[256,128]{1,0:T(8,128)(2,1)S(1)}, bf16[256,128]{1,0:T(8,128)(2,1)S(1)}, u32[]{:S(2)}, u32[]{:S(2)}) %collective-permute-start.10) | collective-permute-done | bytes 65568 | tf_op jit(solution)/shard_map/ppermute | solution.py:283
  96.2 3.4 %collective-permute-start.11 = (bf16[2,256,128]{2,1,0:T(8,128)(2,1)S(1)}, bf16[2,256,128]{2,1,0:T(8,128)(2,1)S(1)}, u32[]{:S(2)}, u32[]{:S(2)}) collective-permute-start(bf16[2,256,128]{2,1,0:T(8,128)(2,1)S(1)} %shard_map.114.own_ref), channel_id=1, source_target_pairs={{0,64},{32,96},{64,0},{96,32},{1,65},{33,97},{65,1},{97,33},{2,66}... | collective-permute-start | bytes 393224 | tf_op jit(solution)/shard_map/ppermute | solution.py:285
  99.6 5.0 %all-to-all-done.1.in_ref = bf16[32,16,128]{2,1,0:T(8,128)(2,1)S(1)} async-done(((bf16[32,16,128]{2,1,0:T(8,128)(2,1)}), bf16[32,16,128]{2,1,0:T(8,128)(2,1)S(1)}, u32[]{:S(2)}, u32[]{:S(2)}) %all-to-all-start.1) | async-done | bytes 131104 | tf_op jit(solution)/shard_map/all_to_all | solution.py:184
  104.6 0.7 shard_map.116
  105.2 3.3 %all-to-all-start.2 = ((f32[4,16,128]{2,1,0:T(8,128)}), f32[4,16,128]{2,1,0:T(8,128)S(1)}, u32[]{:S(2)}, u32[]{:S(2)}) async-start(f32[4,16,128]{2,1,0:T(8,128)} %shard_map.116), calls=%async_computation.2 | async-start | bytes 65536 | tf_op jit(solution)/shard_map/all_to_all | solution.py:184
  108.5 0.0 copy-done
  108.5 0.5 convolution_convert_fusion.weight_ref
  109.0 0.0 collective-permute-done.11.other_ref
  109.0 1.1 shard_map.115
  110.1 3.8 %all-to-all-done.2.in_ref = f32[4,16,128]{2,1,0:T(8,128)S(1)} async-done(((f32[4,16,128]{2,1,0:T(8,128)}), f32[4,16,128]{2,1,0:T(8,128)S(1)}, u32[]{:S(2)}, u32[]{:S(2)}) %all-to-all-start.2) | async-done | bytes 32800 | tf_op jit(solution)/shard_map/all_to_all | solution.py:184
  113.9 0.6 shard_map.117
  (4 shorter events, 0.1 us)
Async XLA Ops:
  0.6 107.9 %copy-start = (bf16[512,512]{1,0:T(8,128)(2,1)S(1)}, bf16[512,512]{1,0:T(8,128)(2,1)}, u32[]{:S(2)}) copy-start(bf16[512,512]{1,0:T(8,128)(2,1)} %param.12) | copy-start | bytes 1572868
  0.6 6.2 %copy-start.6 = (s32[1,8,6]{1,0,2:T(1,128)S(1)}, s32[1,8,6]{1,0,2:T(1,128)}, u32[]{:S(2)}) copy-start(s32[1,8,6]{1,0,2:T(1,128)} %param.14) | copy-start | bytes 580
  0.7 6.2 %copy-start.7 = (s32[1,8,6]{1,0,2:T(1,128)S(1)}, s32[1,8,6]{1,0,2:T(1,128)}, u32[]{:S(2)}) copy-start(s32[1,8,6]{1,0,2:T(1,128)} %param.15) | copy-start | bytes 580
  0.7 6.2 %copy-start.2 = (bf16[256,512]{1,0:T(8,128)(2,1)S(1)}, bf16[256,512]{1,0:T(8,128)(2,1)}, u32[]{:S(2)}) copy-start(bf16[256,512]{1,0:T(8,128)(2,1)} %pre_ref.3) | copy-start | bytes 786436
  0.7 6.2 %copy-start.3 = (bf16[256,512]{1,0:T(8,128)(2,1)S(1)}, bf16[256,512]{1,0:T(8,128)(2,1)}, u32[]{:S(2)}) copy-start(bf16[256,512]{1,0:T(8,128)(2,1)} %up_ref.3) | copy-start | bytes 786436
  0.7 6.2 %copy-start.1 = (bf16[1,8,6,128,128]{4,3,2,1,0:T(8,128)(2,1)S(1)}, bf16[1,8,6,128,128]{4,3,2,1,0:T(8,128)(2,1)}, u32[]{:S(2)}) copy-start(bf16[1,8,6,128,128]{4,3,2,1,0:T(8,128)(2,1)} %tiles_ref.3) | copy-start | bytes 4718596
  0.7 6.2 %copy-start.8 = (s32[1,8]{1,0:T(1,128)S(1)}, s32[1,8]{1,0:T(1,128)}, u32[]{:S(2)}) copy-start(s32[1,8]{1,0:T(1,128)} %count_ref.3) | copy-start | bytes 100
  3.0 18.8 %collective-permute-start = (bf16[256,512]{1,0:T(8,128)(2,1)}, bf16[256,512]{1,0:T(8,128)(2,1)S(1)}, u32[]{:S(2)}, u32[]{:S(2)}) collective-permute-start(bf16[256,512]{1,0:T(8,128)(2,1)} %shard_map.105), channel_id=1, source_target_pairs={{0,30},{1,3},{2,0},{3,5},{4,2},{5,7},{6,4},{7,9},{8,6},{9,11},{10,... | collective-permute-start | bytes 786440 | tf_op jit(solution)/shard_map/ppermute | solution.py:199
  8.8 17.8 %collective-permute-start.3 = (bf16[256,512]{1,0:T(8,128)(2,1)S(1)}, bf16[256,512]{1,0:T(8,128)(2,1)S(1)}, u32[]{:S(2)}, u32[]{:S(2)}) collective-permute-start(bf16[256,512]{1,0:T(8,128)(2,1)S(1)} %get-tuple-element.24), channel_id=1, source_target_pairs={{0,2},{2,4},{4,6},{6,8},{8,10},{10,12},{12,14},{14,16},{16,18},{18... | collective-permute-start | bytes 786440 | tf_op jit(solution)/shard_map/ppermute | solution.py:189
  12.7 21.0 %collective-permute-start.2 = (bf16[256,512]{1,0:T(8,128)(2,1)S(1)}, bf16[256,512]{1,0:T(8,128)(2,1)S(1)}, u32[]{:S(2)}, u32[]{:S(2)}) collective-permute-start(bf16[256,512]{1,0:T(8,128)(2,1)S(1)} %get-tuple-element.21), channel_id=1, source_target_pairs={{0,2},{1,31},{2,4},{3,1},{4,6},{5,3},{6,8},{7,5},{8,10},{9,7},{10,... | collective-permute-start | bytes 786440 | tf_op jit(solution)/shard_map/ppermute | solution.py:199
  24.0 15.5 %copy-start.4 = (bf16[512,512]{1,0:T(8,128)(2,1)S(1)}, bf16[512,512]{1,0:T(8,128)(2,1)}, u32[]{:S(2)}) copy-start(bf16[512,512]{1,0:T(8,128)(2,1)} %constant.12.clone.spread_ref) | copy-start | bytes 1572868
  24.0 12.2 %collective-permute-start.1 = (bf16[256,512]{1,0:T(8,128)(2,1)S(1)}, bf16[256,512]{1,0:T(8,128)(2,1)S(1)}, u32[]{:S(2)}, u32[]{:S(2)}) collective-permute-start(bf16[256,512]{1,0:T(8,128)(2,1)S(1)} %get-tuple-element.20), channel_id=1, source_target_pairs={{0,30},{1,3},{2,0},{3,5},{4,2},{5,7},{6,4},{7,9},{8,6},{9,11},{10,... | collective-permute-start | bytes 786440 | tf_op jit(solution)/shard_map/ppermute | solution.py:199
  26.6 12.9 %collective-permute-start.4 = (bf16[256,512]{1,0:T(8,128)(2,1)S(1)}, bf16[256,512]{1,0:T(8,128)(2,1)S(1)}, u32[]{:S(2)}, u32[]{:S(2)}) collective-permute-start(bf16[256,512]{1,0:T(8,128)(2,1)S(1)} %shard_map.109), channel_id=1, source_target_pairs={{0,2},{2,4},{4,6},{6,8},{8,10},{10,12},{12,14},{14,16},{16,18},{18... | collective-permute-start | bytes 786440 | tf_op jit(solution)/shard_map/ppermute | solution.py:189
  28.6 11.0 %collective-permute-start.5 = (bf16[256,512]{1,0:T(8,128)(2,1)S(1)}, bf16[256,512]{1,0:T(8,128)(2,1)S(1)}, u32[]{:S(2)}, u32[]{:S(2)}) collective-permute-start(bf16[256,512]{1,0:T(8,128)(2,1)S(1)} %get-tuple-element.25), channel_id=1, source_target_pairs={{0,30},{2,0},{4,2},{6,4},{8,6},{10,8},{12,10},{14,12},{16,14},{18,... | collective-permute-start | bytes 786440 | tf_op jit(solution)/shard_map/ppermute | solution.py:189
  39.5 38.6 %copy-start.5 = (bf16[256,512]{1,0:T(8,128)(2,1)S(1)}, bf16[256,512]{1,0:T(8,128)(2,1)}, u32[]{:S(2)}) copy-start(bf16[256,512]{1,0:T(8,128)(2,1)} %refs_3_.3) | copy-start | bytes 786436
  53.4 18.4 %collective-permute-start.6 = (bf16[256,128]{1,0:T(8,128)(2,1)S(1)}, bf16[256,128]{1,0:T(8,128)(2,1)S(1)}, u32[]{:S(2)}, u32[]{:S(2)}) collective-permute-start(bf16[256,128]{1,0:T(8,128)(2,1)S(1)} %get-tuple-element.26), channel_id=1, source_target_pairs={{0,20},{2,22},{4,24},{6,26},{8,28},{10,30},{12,0},{14,2},{16,4},{1... | collective-permute-start | bytes 196616 | tf_op jit(solution)/shard_map/ppermute | solution.py:189
  60.8 13.6 %collective-permute-start.7 = (bf16[256,128]{1,0:T(8,128)(2,1)S(1)}, bf16[256,128]{1,0:T(8,128)(2,1)S(1)}, u32[]{:S(2)}, u32[]{:S(2)}) collective-permute-start(bf16[256,128]{1,0:T(8,128)(2,1)S(1)} %get-tuple-element.27), channel_id=1, source_target_pairs={{0,12},{2,14},{4,16},{6,18},{8,20},{10,22},{12,24},{14,26},{16,28}... | collective-permute-start | bytes 196616 | tf_op jit(solution)/shard_map/ppermute | solution.py:189
  64.9 9.6 %collective-permute-start.8 = (bf16[256,128]{1,0:T(8,128)(2,1)S(1)}, bf16[256,128]{1,0:T(8,128)(2,1)S(1)}, u32[]{:S(2)}, u32[]{:S(2)}) collective-permute-start(bf16[256,128]{1,0:T(8,128)(2,1)S(1)} %get-tuple-element.28), channel_id=1, source_target_pairs={{0,28},{2,30},{4,0},{6,2},{8,4},{10,6},{12,8},{14,10},{16,12},{18,... | collective-permute-start | bytes 196616 | tf_op jit(solution)/shard_map/ppermute | solution.py:189
  69.9 8.3 %collective-permute-start.9 = (bf16[256,128]{1,0:T(8,128)(2,1)S(1)}, bf16[256,128]{1,0:T(8,128)(2,1)S(1)}, u32[]{:S(2)}, u32[]{:S(2)}) collective-permute-start(bf16[256,128]{1,0:T(8,128)(2,1)S(1)} %get-tuple-element.29), channel_id=1, source_target_pairs={{0,4},{2,6},{4,8},{6,10},{8,12},{10,14},{12,16},{14,18},{16,20},{1... | collective-permute-start | bytes 196616 | tf_op jit(solution)/shard_map/ppermute | solution.py:189
  79.1 25.5 %all-to-all-start.1 = ((bf16[32,16,128]{2,1,0:T(8,128)(2,1)}), bf16[32,16,128]{2,1,0:T(8,128)(2,1)S(1)}, u32[]{:S(2)}, u32[]{:S(2)}) async-start(bf16[32,16,128]{2,1,0:T(8,128)(2,1)} %bitcast.4), calls=%async_computation.1 | async-start | bytes 262144 | tf_op jit(solution)/shard_map/all_to_all | solution.py:184
  90.0 6.2 %collective-permute-start.10 = (bf16[256,128]{1,0:T(8,128)(2,1)S(1)}, bf16[256,128]{1,0:T(8,128)(2,1)S(1)}, u32[]{:S(2)}, u32[]{:S(2)}) collective-permute-start(bf16[256,128]{1,0:T(8,128)(2,1)S(1)} %get-tuple-element.30.own_ref), channel_id=1, source_target_pairs={{0,32},{32,0},{64,96},{96,64},{1,33},{33,1},{65,97},{97,65},{2,34}... | collective-permute-start | bytes 196616 | tf_op jit(solution)/shard_map/ppermute | solution.py:283
  96.2 12.8 %collective-permute-start.11 = (bf16[2,256,128]{2,1,0:T(8,128)(2,1)S(1)}, bf16[2,256,128]{2,1,0:T(8,128)(2,1)S(1)}, u32[]{:S(2)}, u32[]{:S(2)}) collective-permute-start(bf16[2,256,128]{2,1,0:T(8,128)(2,1)S(1)} %shard_map.114.own_ref), channel_id=1, source_target_pairs={{0,64},{32,96},{64,0},{96,32},{1,65},{33,97},{65,1},{97,33},{2,66}... | collective-permute-start | bytes 393224 | tf_op jit(solution)/shard_map/ppermute | solution.py:285
  105.2 8.7 %all-to-all-start.2 = ((f32[4,16,128]{2,1,0:T(8,128)}), f32[4,16,128]{2,1,0:T(8,128)S(1)}, u32[]{:S(2)}, u32[]{:S(2)}) async-start(f32[4,16,128]{2,1,0:T(8,128)} %shard_map.116), calls=%async_computation.2 | async-start | bytes 65536 | tf_op jit(solution)/shard_map/all_to_all | solution.py:184

commit v7 on v6

--- a/solution.py
+++ b/solution.py
@@ -120,8 +120,10 @@
     total = in_refs[0][...].astype(F32)
     for in_ref in in_refs[1:]:
         total += in_ref[...].astype(F32)
-    p_ref[...] = total.astype(BF16)
-    gw = contract_rows(p_ref[...], feat_ref[...]) * scale
+    high = total.astype(BF16)
+    low = (total - high.astype(F32)).astype(BF16)
+    p_ref[0], p_ref[1] = high, low
+    gw = (contract_rows(high, feat_ref[...]) + contract_rows(low, feat_ref[...])) * scale
     quarter = lines_ref.shape[1]
     spots = ZH * ZL * YL
     rows, pieces = gw.shape[0] // spots, gw.shape[1] // quarter
@@ -139,13 +141,14 @@
 
 
 def feature_kernel(lane_ref, own_ref, other_ref, weight_ref, feat_ref):
-    quarter = own_ref.shape[2]
+    quarter = own_ref.shape[3]
     total = jnp.zeros(feat_ref.shape, F32)
     for at in range(REP):
         source = lane_ref[0] ^ at
         span = pl.ds(pl.multiple_of(source * quarter, quarter), quarter)
-        part = (own_ref if at < 2 else other_ref)[at % 2]
-        total += jnp.dot(part, weight_ref[span, :], preferred_element_type=F32)
+        for half in range(2):
+            part = (own_ref if at < 2 else other_ref)[at % 2, half]
+            total += jnp.dot(part, weight_ref[span, :], preferred_element_type=F32)
     feat_ref[...] = total.astype(BF16)
 
 
@@ -244,9 +247,8 @@
     mid_other, mark_other = whole(
         sum_kernel, (block, mark), (), (mid_other, turned_along_z(far_other, 1))
     )
-    mid_same, back_same, keep_other, keep_same, _ = terms(
-        ((0, 1), (0, 3), (1, 2), (0, 2)), (F32, BF16, F32, F32), (mark_other,)
-    )
+    mid_same, back_same, mark_same = terms(((0, 1), (0, 3)), (F32, BF16), (mark_other,))
+    keep_other, keep_same, _ = terms(((1, 2), (0, 2)), (F32, F32), (mark_same,))
     mid_same = whole(sum_kernel, (block,), (), (mid_same, along_z(far_same, 1)))[0]
     mid_other = turned_along_z(mid_other, 1)
     back_other = turned_along_z(back_other, -1)
@@ -271,7 +273,7 @@
     far = whole(sum_kernel, (shape((nodes, quarter), F32),), (), (parts[1], parts[2]))[0]
     p_quarter, gw = whole(
         functools.partial(weight_kernel, scale=scale),
-        (shape((nodes, quarter), BF16), shape((hidden, quarter), BF16)),
+        (shape((2, nodes, quarter), BF16), shape((hidden, quarter), BF16)),
         (),
         (far, parts[0], parts[3], features),
         (pltpu.VMEM((hidden, quarter), F32),),
@@ -281,7 +283,7 @@
     gw = exchange(gw, "rep")
     lane = lax.axis_index("rep").reshape(1)
     other = lax.ppermute(p_quarter, "rep", [(r, r ^ 1) for r in range(REP)])
-    pair = whole(pair_kernel, (shape((2, nodes, quarter), BF16),), (), (p_quarter, other))[0]
+    pair = whole(pair_kernel, (shape((2, 2, nodes, quarter), BF16),), (), (p_quarter, other))[0]
     others = lax.ppermute(pair, "rep", [(r, r ^ 2) for r in range(REP)])
     grad_feat = whole(
         feature_kernel, (shape((nodes, width), BF16),), (lane,), (pair, others, weight)

time: 115 us -> 115 us (level)
  Pallas kernels: 10.6 us -> 11.8 us
    ppermute x3, waiting for transfers between devices: 4.02 us -> 1.51 us  [turned_along_z(): return lax.ppermute(value, BLK, pairs)]
    ppermute x1, waiting for transfers between devices: 3.68 us -> 5.79 us  [shards(): other = lax.ppermute(p_quarter, 'rep', [(r, r ^ 1) for r in range(REP)])]
    all_to_all x2, waiting for transfers between devices: 8.77 us -> 7.41 us  [exchange(): return lax.all_to_all(value, axes, 0, 0)]
    pallas_call x14 -> x15, Pallas kernels: 10.6 us -> 11.8 us  [whole(): pl.pallas_call(kernel, in_specs=[pl.BlockSpec(memory_space=pltpu.SMEM)] *...]
  transfers between devices with their start and end apart: 14 -> 14, of which waited for: 9 -> 9; matrix products, arithmetic and copies ran while one was open for 0% -> 0% of each run, Pallas kernels for 5% -> 6%
where the time goes in v7:
time: 115 us; the launch traced here: 114 us
  starting transfers between devices  61.8 us (54%)
  waiting for transfers between devices  25.5 us (22%)
  blocking collectives  13.7 us (12%)
  Pallas kernels  11.8 us (10%)
    ppermute x7, starting transfers between devices, along_z(): lax.ppermute(value, ('zh', 'zl'), [(z, (z + shift) % count) for z in rang...  29.7 us
    all_to_all x2, starting transfers between devices, exchange(): return lax.all_to_all(value, axes, 0, 0)  14 us
    all_to_all x1, blocking collectives, exchange(): return lax.all_to_all(value, axes, 0, 0)  13.7 us
    ppermute x3, starting transfers between devices, turned_along_z(): return lax.ppermute(value, BLK, pairs)  13.2 us
    pallas_call x15, Pallas kernels, whole(): pl.pallas_call(kernel, in_specs=[pl.BlockSpec(memory_space=pltpu.SMEM)] *...  11.8 us
    ppermute x7, waiting for transfers between devices, along_z(): lax.ppermute(value, ('zh', 'zl'), [(z, (z + shift) % count) for z in rang...  10.8 us
    all_to_all x2, waiting for transfers between devices, exchange(): return lax.all_to_all(value, axes, 0, 0)  7.41 us
    ppermute x1, waiting for transfers between devices, shards(): other = lax.ppermute(p_quarter, 'rep', [(r, r ^ 1) for r in range(REP)])  5.79 us
  transfers between devices with their start and end apart: 14, of which 9 were waited for; matrix products, arithmetic and copies ran while one was open for 0% of the time, Pallas kernels for 6%

profile of v7, /device:TPU:24, one launch (start us, length us, event | category | flops | bytes accessed | tf_op | source)
XLA Modules:
  0.0 114.3 jit_solution(9721516067535284267)
XLA Ops:
  0.6 0.0 copy-start
  0.6 0.0 copy-start.8
  0.7 0.0 copy-start.1
  0.7 0.0 copy-start.3
  0.7 0.0 copy-start.2
  0.7 0.0 copy-start.7
  0.7 0.0 copy-start.6
  0.7 2.4 %shard_map.105 = bf16[256,512]{1,0:T(8,128)(2,1)} custom-call(s32[1]{0:T(128)} %bitcast.1.yl_ref, bf16[1,8,6,128,128]{4,3,2,1,0:T(8,128)(2,1)} %tiles_ref.5, s32[6,1,8]{2,1,0:T(1,128)} %bitcast.7, s32[6,1,8]{2,1,0:T(1,128)} %bitcast.11, s32[1,8]{1,0:T(1,128)} %count_ref.5, bf16[256,512]{1,0:T(8,128)(2,1)} %pre_ref.5, bf16[256,512]{1,0:T(8,128)(2,1)} %up_ref.5), custom_call_target="tpu_custom_call" | custom-call | tf_op jit(solution)/shard_map/pallas_call | solution.py:175
  3.1 3.8 %collective-permute-start = (bf16[256,512]{1,0:T(8,128)(2,1)}, bf16[256,512]{1,0:T(8,128)(2,1)S(1)}, u32[]{:S(2)}, u32[]{:S(2)}) collective-permute-start(bf16[256,512]{1,0:T(8,128)(2,1)} %shard_map.105), channel_id=1, source_target_pairs={{0,30},{1,3},{2,0},{3,5},{4,2},{5,7},{6,4},{7,9},{8,6},{9,11},{10,... | collective-permute-start | bytes 786440 | tf_op jit(solution)/shard_map/ppermute | solution.py:202
  6.9 0.0 copy-done.8
  6.9 0.0 copy-done.1
  6.9 0.0 copy-done.3
  6.9 0.0 copy-done.2
  6.9 0.0 copy-done.7
  6.9 0.0 copy-done.6
  6.9 1.9 %shard_map.104 = (bf16[256,512]{1,0:T(8,128)(2,1)S(1)}, bf16[256,512]{1,0:T(8,128)(2,1)S(1)}, f32[256,512]{1,0:T(8,128)S(1)}, f32[8,128]{1,0:T(8,128)}) custom-call(s32[1]{0:T(128)} %bitcast.1.yl_ref, s32[6,1,8]{2,1,0:T(1,128)S(1)} %bitcast.8, s32[6,1,8]{2,1,0:T(1,128)S(1)} %bitcast.12, s32[1,8]{1,0:T(1,128)S(1)} %copy-done.8, ...), custom_call_target="tpu_custom_call" | custom-call | tf_op jit(solution)/shard_map/pallas_call | solution.py:175
  8.8 3.9 %collective-permute-start.3 = (bf16[256,512]{1,0:T(8,128)(2,1)S(1)}, bf16[256,512]{1,0:T(8,128)(2,1)S(1)}, u32[]{:S(2)}, u32[]{:S(2)}) collective-permute-start(bf16[256,512]{1,0:T(8,128)(2,1)S(1)} %get-tuple-element.26), channel_id=1, source_target_pairs={{0,2},{2,4},{4,6},{6,8},{8,10},{10,12},{12,14},{14,16},{16,18},{18... | collective-permute-start | bytes 786440 | tf_op jit(solution)/shard_map/ppermute | solution.py:192
  12.8 7.5 %collective-permute-start.2 = (bf16[256,512]{1,0:T(8,128)(2,1)S(1)}, bf16[256,512]{1,0:T(8,128)(2,1)S(1)}, u32[]{:S(2)}, u32[]{:S(2)}) collective-permute-start(bf16[256,512]{1,0:T(8,128)(2,1)S(1)} %get-tuple-element.23), channel_id=1, source_target_pairs={{0,2},{1,31},{2,4},{3,1},{4,6},{5,3},{6,8},{7,5},{8,10},{9,7},{10,... | collective-permute-start | bytes 786440 | tf_op jit(solution)/shard_map/ppermute | solution.py:202
  20.3 1.5 %collective-permute-done.right_ref = bf16[256,512]{1,0:T(8,128)(2,1)S(1)} collective-permute-done((bf16[256,512]{1,0:T(8,128)(2,1)}, bf16[256,512]{1,0:T(8,128)(2,1)S(1)}, u32[]{:S(2)}, u32[]{:S(2)}) %collective-permute-start) | collective-permute-done | bytes 262176 | tf_op jit(solution)/shard_map/ppermute | solution.py:202
  21.8 1.9 %collective-permute-start.1 = (bf16[256,512]{1,0:T(8,128)(2,1)S(1)}, bf16[256,512]{1,0:T(8,128)(2,1)S(1)}, u32[]{:S(2)}, u32[]{:S(2)}) collective-permute-start(bf16[256,512]{1,0:T(8,128)(2,1)S(1)} %get-tuple-element.22), channel_id=1, source_target_pairs={{0,30},{1,3},{2,0},{3,5},{4,2},{5,7},{6,4},{7,9},{8,6},{9,11},{10,... | collective-permute-start | bytes 786440 | tf_op jit(solution)/shard_map/ppermute | solution.py:202
  23.8 1.3 %shard_map.107 = (f32[256,512]{1,0:T(8,128)S(1)}, bf16[256,512]{1,0:T(8,128)(2,1)S(1)}, f32[8,128]{1,0:T(8,128)S(1)}) custom-call(s32[1]{0:T(128)} %bitcast.1.yl_ref, s32[6,1,8]{2,1,0:T(1,128)S(1)} %bitcast.9, s32[6,1,8]{2,1,0:T(1,128)S(1)} %bitcast.13, s32[1,8]{1,0:T(1,128)S(1)} %copy-done.8, bf16[1,8,6,128,128]{4,3,2,1,0:T(8,128)(2,1)S(1)} %copy-done.1, ...), custom_call_target="tpu_custom_call" | custom-call | tf_op jit(solution)/shard_map/pallas_call | solution.py:175
  25.0 2.1 %collective-permute-done.3.right_ref = bf16[256,512]{1,0:T(8,128)(2,1)S(1)} collective-permute-done((bf16[256,512]{1,0:T(8,128)(2,1)S(1)}, bf16[256,512]{1,0:T(8,128)(2,1)S(1)}, u32[]{:S(2)}, u32[]{:S(2)}) %collective-permute-start.3) | collective-permute-done | bytes 262176 | tf_op jit(solution)/shard_map/ppermute | solution.py:192
  27.1 0.1 shard_map.110
  27.1 1.9 %collective-permute-start.4 = (bf16[256,512]{1,0:T(8,128)(2,1)S(1)}, bf16[256,512]{1,0:T(8,128)(2,1)S(1)}, u32[]{:S(2)}, u32[]{:S(2)}) collective-permute-start(bf16[256,512]{1,0:T(8,128)(2,1)S(1)} %shard_map.110), channel_id=1, source_target_pairs={{0,2},{2,4},{4,6},{6,8},{8,10},{10,12},{12,14},{14,16},{16,18},{18... | collective-permute-start | bytes 786440 | tf_op jit(solution)/shard_map/ppermute | solution.py:192
  29.1 5.1 %collective-permute-start.5 = (bf16[256,512]{1,0:T(8,128)(2,1)S(1)}, bf16[256,512]{1,0:T(8,128)(2,1)S(1)}, u32[]{:S(2)}, u32[]{:S(2)}) collective-permute-start(bf16[256,512]{1,0:T(8,128)(2,1)S(1)} %get-tuple-element.27), channel_id=1, source_target_pairs={{0,30},{2,0},{4,2},{6,4},{8,6},{10,8},{12,10},{14,12},{16,14},{18,... | collective-permute-start | bytes 786440 | tf_op jit(solution)/shard_map/ppermute | solution.py:192
  34.2 0.0 copy-start.4
  34.2 1.6 %shard_map.108 = (f32[256,512]{1,0:T(8,128)S(1)}, f32[256,512]{1,0:T(8,128)S(1)}, f32[8,128]{1,0:T(8,128)}) custom-call(s32[1]{0:T(128)} %bitcast.1.yl_ref, s32[6,1,8]{2,1,0:T(1,128)S(1)} %bitcast.10, s32[6,1,8]{2,1,0:T(1,128)S(1)} %bitcast.14, s32[1,8]{1,0:T(1,128)S(1)} %copy-done.8, bf16[1,8,6,128,128]{4,3,2,1,0:T(8,128)(2,1)S(1)} %copy-done.1, ...), custom_call_target="tpu_custom_call" | custom-call | tf_op jit(solution)/shard_map/pallas_call | solution.py:175
  35.9 0.0 collective-permute-done.2.second_ref
  35.9 0.0 collective-permute-done.1.first_ref
  35.9 0.1 shard_map.109.other_ref
  36.0 1.8 %collective-permute-done.4.first_ref = bf16[256,512]{1,0:T(8,128)(2,1)S(1)} collective-permute-done((bf16[256,512]{1,0:T(8,128)(2,1)S(1)}, bf16[256,512]{1,0:T(8,128)(2,1)S(1)}, u32[]{:S(2)}, u32[]{:S(2)}) %collective-permute-start.4) | collective-permute-done | bytes 262176 | tf_op jit(solution)/shard_map/ppermute | solution.py:192
  37.8 0.6 collective-permute-done.5.second_ref
  38.4 0.0 copy-done.4
  38.4 0.0 copy-start.5
  38.4 0.7 shard_map.111
  39.1 13.7 %all_to_all.15.in_ref = bf16[8,256,128]{2,1,0:T(8,128)(2,1)S(1)} all-to-all(bf16[8,256,128]{2,1,0:T(8,128)(2,1)S(1)} %shard_map.111), channel_id=1, replica_groups=mesh['dp'=4,'rep'=4,'zh'=4,'zl'=4,'yl'=2] {'rep','yl'}, dimensions={0} | all-to-all | bytes 1048576 | tf_op jit(solution)/shard_map/all_to_all | solution.py:187
  52.8 0.1 shard_map.112
  52.9 7.0 %collective-permute-start.6 = (bf16[256,128]{1,0:T(8,128)(2,1)S(1)}, bf16[256,128]{1,0:T(8,128)(2,1)S(1)}, u32[]{:S(2)}, u32[]{:S(2)}) collective-permute-start(bf16[256,128]{1,0:T(8,128)(2,1)S(1)} %get-tuple-element.28), channel_id=1, source_target_pairs={{0,20},{2,22},{4,24},{6,26},{8,28},{10,30},{12,0},{14,2},{16,4},{1... | collective-permute-start | bytes 196616 | tf_op jit(solution)/shard_map/ppermute | solution.py:192
  59.9 4.5 %collective-permute-start.7 = (bf16[256,128]{1,0:T(8,128)(2,1)S(1)}, bf16[256,128]{1,0:T(8,128)(2,1)S(1)}, u32[]{:S(2)}, u32[]{:S(2)}) collective-permute-start(bf16[256,128]{1,0:T(8,128)(2,1)S(1)} %get-tuple-element.29), channel_id=1, source_target_pairs={{0,12},{2,14},{4,16},{6,18},{8,20},{10,22},{12,24},{14,26},{16,28}... | collective-permute-start | bytes 196616 | tf_op jit(solution)/shard_map/ppermute | solution.py:192
  64.5 5.2 %collective-permute-start.8 = (bf16[256,128]{1,0:T(8,128)(2,1)S(1)}, bf16[256,128]{1,0:T(8,128)(2,1)S(1)}, u32[]{:S(2)}, u32[]{:S(2)}) collective-permute-start(bf16[256,128]{1,0:T(8,128)(2,1)S(1)} %get-tuple-element.30), channel_id=1, source_target_pairs={{0,28},{2,30},{4,0},{6,2},{8,4},{10,6},{12,8},{14,10},{16,12},{18,... | collective-permute-start | bytes 196616 | tf_op jit(solution)/shard_map/ppermute | solution.py:192
  69.7 1.9 %collective-permute-start.9 = (bf16[256,128]{1,0:T(8,128)(2,1)S(1)}, bf16[256,128]{1,0:T(8,128)(2,1)S(1)}, u32[]{:S(2)}, u32[]{:S(2)}) collective-permute-start(bf16[256,128]{1,0:T(8,128)(2,1)S(1)} %get-tuple-element.31), channel_id=1, source_target_pairs={{0,4},{2,6},{4,8},{6,10},{8,12},{10,14},{12,16},{14,18},{16,20},{1... | collective-permute-start | bytes 196616 | tf_op jit(solution)/shard_map/ppermute | solution.py:192
  71.6 0.0 collective-permute-done.6.left_ref
  71.7 2.0 %collective-permute-done.7.right_ref = bf16[256,128]{1,0:T(8,128)(2,1)S(1)} collective-permute-done((bf16[256,128]{1,0:T(8,128)(2,1)S(1)}, bf16[256,128]{1,0:T(8,128)(2,1)S(1)}, u32[]{:S(2)}, u32[]{:S(2)}) %collective-permute-start.7) | collective-permute-done | bytes 65568 | tf_op jit(solution)/shard_map/ppermute | solution.py:192
  73.6 0.0 collective-permute-done.8.refs_1_
  73.7 4.3 %collective-permute-done.9.refs_2_ = bf16[256,128]{1,0:T(8,128)(2,1)S(1)} collective-permute-done((bf16[256,128]{1,0:T(8,128)(2,1)S(1)}, bf16[256,128]{1,0:T(8,128)(2,1)S(1)}, u32[]{:S(2)}, u32[]{:S(2)}) %collective-permute-start.9) | collective-permute-done | bytes 65568 | tf_op jit(solution)/shard_map/ppermute | solution.py:192
  78.0 0.0 copy-done.5
  78.0 1.0 shard_map.114
  79.0 10.8 %all-to-all-start.1 = ((bf16[32,16,128]{2,1,0:T(8,128)(2,1)}), bf16[32,16,128]{2,1,0:T(8,128)(2,1)S(1)}, u32[]{:S(2)}, u32[]{:S(2)}) async-start(bf16[32,16,128]{2,1,0:T(8,128)(2,1)} %bitcast.4), calls=%async_computation.1 | async-start | bytes 262144 | tf_op jit(solution)/shard_map/all_to_all | solution.py:187
  89.8 2.5 %collective-permute-start.10 = (bf16[2,256,128]{2,1,0:T(8,128)(2,1)S(1)}, bf16[2,256,128]{2,1,0:T(8,128)(2,1)S(1)}, u32[]{:S(2)}, u32[]{:S(2)}) collective-permute-start(bf16[2,256,128]{2,1,0:T(8,128)(2,1)S(1)} %get-tuple-element.32.own_ref), channel_id=1, source_target_pairs={{0,32},{32,0},{64,96},{96,64},{1,33},{33,1},{65,97},{97,65},{2,34}... | collective-permute-start | bytes 393224 | tf_op jit(solution)/shard_map/ppermute | solution.py:285
  92.2 5.8 %collective-permute-done.10.other_ref = bf16[2,256,128]{2,1,0:T(8,128)(2,1)S(1)} collective-permute-done((bf16[2,256,128]{2,1,0:T(8,128)(2,1)S(1)}, bf16[2,256,128]{2,1,0:T(8,128)(2,1)S(1)}, u32[]{:S(2)}, u32[]{:S(2)}) %collective-permute-start.10) | collective-permute-done | bytes 131104 | tf_op jit(solution)/shard_map/ppermute | solution.py:285
  98.0 2.4 %collective-permute-start.11 = (bf16[2,2,256,128]{3,2,1,0:T(8,128)(2,1)S(1)}, bf16[2,2,256,128]{3,2,1,0:T(8,128)(2,1)S(1)}, u32[]{:S(2)}, u32[]{:S(2)}) collective-permute-start(bf16[2,2,256,128]{3,2,1,0:T(8,128)(2,1)S(1)} %shard_map.115.own_ref), channel_id=1, source_target_pairs={{0,64},{32,96},{64,0},{96,32},{1,65},{33,97},{65,1},{97,33},{2,66}... | collective-permute-start | bytes 786440 | tf_op jit(solution)/shard_map/ppermute | solution.py:287
  100.5 3.9 %all-to-all-done.1.in_ref = bf16[32,16,128]{2,1,0:T(8,128)(2,1)S(1)} async-done(((bf16[32,16,128]{2,1,0:T(8,128)(2,1)}), bf16[32,16,128]{2,1,0:T(8,128)(2,1)S(1)}, u32[]{:S(2)}, u32[]{:S(2)}) %all-to-all-start.1) | async-done | bytes 131104 | tf_op jit(solution)/shard_map/all_to_all | solution.py:187
  104.3 0.7 shard_map.117
  105.0 3.3 %all-to-all-start.2 = ((f32[4,16,128]{2,1,0:T(8,128)}), f32[4,16,128]{2,1,0:T(8,128)S(1)}, u32[]{:S(2)}, u32[]{:S(2)}) async-start(f32[4,16,128]{2,1,0:T(8,128)} %shard_map.117), calls=%async_computation.2 | async-start | bytes 65536 | tf_op jit(solution)/shard_map/all_to_all | solution.py:187
  108.3 0.0 copy-done
  108.3 0.5 convolution_convert_fusion.weight_ref
  108.7 0.0 collective-permute-done.11.other_ref
  108.8 1.4 %shard_map.116 = bf16[256,512]{1,0:T(8,128)(2,1)} custom-call(s32[1]{0:T(128)} %bitcast.lane_ref, bf16[2,2,256,128]{3,2,1,0:T(8,128)(2,1)S(1)} %shard_map.115.own_ref, bf16[2,2,256,128]{3,2,1,0:T(8,128)(2,1)S(1)} %collective-permute-done.11.other_ref, bf16[512,512]{1,0:T(8,128)(2,1)S(1)} %convolution_convert_fusion.weight_ref), custom_call_target="tpu_custom_call" | custom-call | tf_op jit(solution)/shard_map/pallas_call | solution.py:175
  110.1 3.5 %all-to-all-done.2.in_ref = f32[4,16,128]{2,1,0:T(8,128)S(1)} async-done(((f32[4,16,128]{2,1,0:T(8,128)}), f32[4,16,128]{2,1,0:T(8,128)S(1)}, u32[]{:S(2)}, u32[]{:S(2)}) %all-to-all-start.2) | async-done | bytes 32800 | tf_op jit(solution)/shard_map/all_to_all | solution.py:187
  113.7 0.6 shard_map.118
  (3 shorter events, 0.1 us)
Async XLA Ops:
  0.6 107.6 %copy-start = (bf16[512,512]{1,0:T(8,128)(2,1)S(1)}, bf16[512,512]{1,0:T(8,128)(2,1)}, u32[]{:S(2)}) copy-start(bf16[512,512]{1,0:T(8,128)(2,1)} %param.12) | copy-start | bytes 1572868
  0.6 6.2 %copy-start.8 = (s32[1,8]{1,0:T(1,128)S(1)}, s32[1,8]{1,0:T(1,128)}, u32[]{:S(2)}) copy-start(s32[1,8]{1,0:T(1,128)} %count_ref.5) | copy-start | bytes 100
  0.7 6.2 %copy-start.1 = (bf16[1,8,6,128,128]{4,3,2,1,0:T(8,128)(2,1)S(1)}, bf16[1,8,6,128,128]{4,3,2,1,0:T(8,128)(2,1)}, u32[]{:S(2)}) copy-start(bf16[1,8,6,128,128]{4,3,2,1,0:T(8,128)(2,1)} %tiles_ref.5) | copy-start | bytes 4718596
  0.7 6.2 %copy-start.3 = (bf16[256,512]{1,0:T(8,128)(2,1)S(1)}, bf16[256,512]{1,0:T(8,128)(2,1)}, u32[]{:S(2)}) copy-start(bf16[256,512]{1,0:T(8,128)(2,1)} %up_ref.5) | copy-start | bytes 786436
  0.7 6.2 %copy-start.2 = (bf16[256,512]{1,0:T(8,128)(2,1)S(1)}, bf16[256,512]{1,0:T(8,128)(2,1)}, u32[]{:S(2)}) copy-start(bf16[256,512]{1,0:T(8,128)(2,1)} %pre_ref.5) | copy-start | bytes 786436
  0.7 6.2 %copy-start.7 = (s32[1,8,6]{1,0,2:T(1,128)S(1)}, s32[1,8,6]{1,0,2:T(1,128)}, u32[]{:S(2)}) copy-start(s32[1,8,6]{1,0,2:T(1,128)} %param.15) | copy-start | bytes 580
  0.7 6.2 %copy-start.6 = (s32[1,8,6]{1,0,2:T(1,128)S(1)}, s32[1,8,6]{1,0,2:T(1,128)}, u32[]{:S(2)}) copy-start(s32[1,8,6]{1,0,2:T(1,128)} %param.14) | copy-start | bytes 580
  3.1 18.7 %collective-permute-start = (bf16[256,512]{1,0:T(8,128)(2,1)}, bf16[256,512]{1,0:T(8,128)(2,1)S(1)}, u32[]{:S(2)}, u32[]{:S(2)}) collective-permute-start(bf16[256,512]{1,0:T(8,128)(2,1)} %shard_map.105), channel_id=1, source_target_pairs={{0,30},{1,3},{2,0},{3,5},{4,2},{5,7},{6,4},{7,9},{8,6},{9,11},{10,... | collective-permute-start | bytes 786440 | tf_op jit(solution)/shard_map/ppermute | solution.py:202
  8.8 18.2 %collective-permute-start.3 = (bf16[256,512]{1,0:T(8,128)(2,1)S(1)}, bf16[256,512]{1,0:T(8,128)(2,1)S(1)}, u32[]{:S(2)}, u32[]{:S(2)}) collective-permute-start(bf16[256,512]{1,0:T(8,128)(2,1)S(1)} %get-tuple-element.26), channel_id=1, source_target_pairs={{0,2},{2,4},{4,6},{6,8},{8,10},{10,12},{12,14},{14,16},{16,18},{18... | collective-permute-start | bytes 786440 | tf_op jit(solution)/shard_map/ppermute | solution.py:192
  12.8 23.1 %collective-permute-start.2 = (bf16[256,512]{1,0:T(8,128)(2,1)S(1)}, bf16[256,512]{1,0:T(8,128)(2,1)S(1)}, u32[]{:S(2)}, u32[]{:S(2)}) collective-permute-start(bf16[256,512]{1,0:T(8,128)(2,1)S(1)} %get-tuple-element.23), channel_id=1, source_target_pairs={{0,2},{1,31},{2,4},{3,1},{4,6},{5,3},{6,8},{7,5},{8,10},{9,7},{10,... | collective-permute-start | bytes 786440 | tf_op jit(solution)/shard_map/ppermute | solution.py:202
  21.8 14.1 %collective-permute-start.1 = (bf16[256,512]{1,0:T(8,128)(2,1)S(1)}, bf16[256,512]{1,0:T(8,128)(2,1)S(1)}, u32[]{:S(2)}, u32[]{:S(2)}) collective-permute-start(bf16[256,512]{1,0:T(8,128)(2,1)S(1)} %get-tuple-element.22), channel_id=1, source_target_pairs={{0,30},{1,3},{2,0},{3,5},{4,2},{5,7},{6,4},{7,9},{8,6},{9,11},{10,... | collective-permute-start | bytes 786440 | tf_op jit(solution)/shard_map/ppermute | solution.py:202
  27.1 10.6 %collective-permute-start.4 = (bf16[256,512]{1,0:T(8,128)(2,1)S(1)}, bf16[256,512]{1,0:T(8,128)(2,1)S(1)}, u32[]{:S(2)}, u32[]{:S(2)}) collective-permute-start(bf16[256,512]{1,0:T(8,128)(2,1)S(1)} %shard_map.110), channel_id=1, source_target_pairs={{0,2},{2,4},{4,6},{6,8},{8,10},{10,12},{12,14},{14,16},{16,18},{18... | collective-permute-start | bytes 786440 | tf_op jit(solution)/shard_map/ppermute | solution.py:192
  29.1 9.3 %collective-permute-start.5 = (bf16[256,512]{1,0:T(8,128)(2,1)S(1)}, bf16[256,512]{1,0:T(8,128)(2,1)S(1)}, u32[]{:S(2)}, u32[]{:S(2)}) collective-permute-start(bf16[256,512]{1,0:T(8,128)(2,1)S(1)} %get-tuple-element.27), channel_id=1, source_target_pairs={{0,30},{2,0},{4,2},{6,4},{8,6},{10,8},{12,10},{14,12},{16,14},{18,... | collective-permute-start | bytes 786440 | tf_op jit(solution)/shard_map/ppermute | solution.py:192
  34.2 4.2 %copy-start.4 = (bf16[512,512]{1,0:T(8,128)(2,1)S(1)}, bf16[512,512]{1,0:T(8,128)(2,1)}, u32[]{:S(2)}) copy-start(bf16[512,512]{1,0:T(8,128)(2,1)} %constant.12.clone.spread_ref) | copy-start | bytes 1572868
  38.4 39.6 %copy-start.5 = (bf16[256,512]{1,0:T(8,128)(2,1)S(1)}, bf16[256,512]{1,0:T(8,128)(2,1)}, u32[]{:S(2)}) copy-start(bf16[256,512]{1,0:T(8,128)(2,1)} %refs_3_.3) | copy-start | bytes 786436
  52.9 18.7 %collective-permute-start.6 = (bf16[256,128]{1,0:T(8,128)(2,1)S(1)}, bf16[256,128]{1,0:T(8,128)(2,1)S(1)}, u32[]{:S(2)}, u32[]{:S(2)}) collective-permute-start(bf16[256,128]{1,0:T(8,128)(2,1)S(1)} %get-tuple-element.28), channel_id=1, source_target_pairs={{0,20},{2,22},{4,24},{6,26},{8,28},{10,30},{12,0},{14,2},{16,4},{1... | collective-permute-start | bytes 196616 | tf_op jit(solution)/shard_map/ppermute | solution.py:192
  59.9 13.7 %collective-permute-start.7 = (bf16[256,128]{1,0:T(8,128)(2,1)S(1)}, bf16[256,128]{1,0:T(8,128)(2,1)S(1)}, u32[]{:S(2)}, u32[]{:S(2)}) collective-permute-start(bf16[256,128]{1,0:T(8,128)(2,1)S(1)} %get-tuple-element.29), channel_id=1, source_target_pairs={{0,12},{2,14},{4,16},{6,18},{8,20},{10,22},{12,24},{14,26},{16,28}... | collective-permute-start | bytes 196616 | tf_op jit(solution)/shard_map/ppermute | solution.py:192
  64.5 9.2 %collective-permute-start.8 = (bf16[256,128]{1,0:T(8,128)(2,1)S(1)}, bf16[256,128]{1,0:T(8,128)(2,1)S(1)}, u32[]{:S(2)}, u32[]{:S(2)}) collective-permute-start(bf16[256,128]{1,0:T(8,128)(2,1)S(1)} %get-tuple-element.30), channel_id=1, source_target_pairs={{0,28},{2,30},{4,0},{6,2},{8,4},{10,6},{12,8},{14,10},{16,12},{18,... | collective-permute-start | bytes 196616 | tf_op jit(solution)/shard_map/ppermute | solution.py:192
  69.7 8.3 %collective-permute-start.9 = (bf16[256,128]{1,0:T(8,128)(2,1)S(1)}, bf16[256,128]{1,0:T(8,128)(2,1)S(1)}, u32[]{:S(2)}, u32[]{:S(2)}) collective-permute-start(bf16[256,128]{1,0:T(8,128)(2,1)S(1)} %get-tuple-element.31), channel_id=1, source_target_pairs={{0,4},{2,6},{4,8},{6,10},{8,12},{10,14},{12,16},{14,18},{16,20},{1... | collective-permute-start | bytes 196616 | tf_op jit(solution)/shard_map/ppermute | solution.py:192
  79.0 25.4 %all-to-all-start.1 = ((bf16[32,16,128]{2,1,0:T(8,128)(2,1)}), bf16[32,16,128]{2,1,0:T(8,128)(2,1)S(1)}, u32[]{:S(2)}, u32[]{:S(2)}) async-start(bf16[32,16,128]{2,1,0:T(8,128)(2,1)} %bitcast.4), calls=%async_computation.1 | async-start | bytes 262144 | tf_op jit(solution)/shard_map/all_to_all | solution.py:187
  89.8 8.3 %collective-permute-start.10 = (bf16[2,256,128]{2,1,0:T(8,128)(2,1)S(1)}, bf16[2,256,128]{2,1,0:T(8,128)(2,1)S(1)}, u32[]{:S(2)}, u32[]{:S(2)}) collective-permute-start(bf16[2,256,128]{2,1,0:T(8,128)(2,1)S(1)} %get-tuple-element.32.own_ref), channel_id=1, source_target_pairs={{0,32},{32,0},{64,96},{96,64},{1,33},{33,1},{65,97},{97,65},{2,34}... | collective-permute-start | bytes 393224 | tf_op jit(solution)/shard_map/ppermute | solution.py:285
  98.0 10.7 %collective-permute-start.11 = (bf16[2,2,256,128]{3,2,1,0:T(8,128)(2,1)S(1)}, bf16[2,2,256,128]{3,2,1,0:T(8,128)(2,1)S(1)}, u32[]{:S(2)}, u32[]{:S(2)}) collective-permute-start(bf16[2,2,256,128]{3,2,1,0:T(8,128)(2,1)S(1)} %shard_map.115.own_ref), channel_id=1, source_target_pairs={{0,64},{32,96},{64,0},{96,32},{1,65},{33,97},{65,1},{97,33},{2,66}... | collective-permute-start | bytes 786440 | tf_op jit(solution)/shard_map/ppermute | solution.py:287
  105.0 8.7 %all-to-all-start.2 = ((f32[4,16,128]{2,1,0:T(8,128)}), f32[4,16,128]{2,1,0:T(8,128)S(1)}, u32[]{:S(2)}, u32[]{:S(2)}) async-start(f32[4,16,128]{2,1,0:T(8,128)} %shard_map.117), calls=%async_computation.2 | async-start | bytes 65536 | tf_op jit(solution)/shard_map/all_to_all | solution.py:187

commit v8 on v7

--- a/solution.py
+++ b/solution.py
@@ -105,7 +105,7 @@
         total = in_ref[YL * r].astype(F32)
         for side in range(1, YL):
             total += in_ref[YL * r + side].astype(F32)
-        out_ref[...] = total.astype(BF16)
+        out_ref[...] = total.astype(out_ref.dtype)
 
 
 def sum_kernel(left_ref, right_ref, out_ref, *mark_refs):
@@ -135,20 +135,15 @@
     gw_ref[...] = lines_ref[...].astype(BF16)
 
 
-def pair_kernel(own_ref, other_ref, out_ref):
-    out_ref[0] = own_ref[...]
-    out_ref[1] = other_ref[...]
-
-
-def feature_kernel(lane_ref, own_ref, other_ref, weight_ref, feat_ref):
-    quarter = own_ref.shape[3]
+def feature_kernel(lane_ref, *refs):
+    *in_refs, weight_ref, feat_ref = refs
+    quarter = in_refs[0].shape[2]
     total = jnp.zeros(feat_ref.shape, F32)
-    for at in range(REP):
-        source = lane_ref[0] ^ at
+    for back, in_ref in enumerate(in_refs):
+        source = lax.rem(lane_ref[0] + REP - back, REP)
         span = pl.ds(pl.multiple_of(source * quarter, quarter), quarter)
         for half in range(2):
-            part = (own_ref if at < 2 else other_ref)[at % 2, half]
-            total += jnp.dot(part, weight_ref[span, :], preferred_element_type=F32)
+            total += jnp.dot(in_ref[half], weight_ref[span, :], preferred_element_type=F32)
     feat_ref[...] = total.astype(BF16)
 
 
@@ -267,26 +262,29 @@
         (other, keep_same, mid_same, back_same, spread),
     )[0]
     parts = exchange(parts, ("rep", "yl"))
-    parts = whole(sides_kernel, (shape((nodes, quarter), BF16),) * REP, (), (parts,))
-    hops = (-2, -6, 6, 2)
-    parts = [along_z(parts[r], hops[r]) for r in range(REP)]
-    far = whole(sum_kernel, (shape((nodes, quarter), F32),), (), (parts[1], parts[2]))[0]
+    piece = shape((nodes, quarter), BF16)
+    kept = shape((nodes, quarter), F32)
+    down, down_far, up_far, up = whole(sides_kernel, (kept, piece, piece, kept), (), (parts,))
+    down = whole(sum_kernel, (piece,), (), (down, along_z(down_far, -4)))[0]
+    up = whole(sum_kernel, (piece,), (), (up, along_z(up_far, 4)))[0]
+    down, up = along_z(down, -2), along_z(up, 2)
     p_quarter, gw = whole(
         functools.partial(weight_kernel, scale=scale),
         (shape((2, nodes, quarter), BF16), shape((hidden, quarter), BF16)),
         (),
-        (far, parts[0], parts[3], features),
+        (down, up, features),
         (pltpu.VMEM((hidden, quarter), F32),),
     )
     gw = exchange(gw.reshape(ZH * ZL * YL, -1, quarter), BLK)
     gw = whole(copies_kernel, (shape((REP,) + gw.shape[1:], F32),), (), (gw,))[0]
     gw = exchange(gw, "rep")
     lane = lax.axis_index("rep").reshape(1)
-    other = lax.ppermute(p_quarter, "rep", [(r, r ^ 1) for r in range(REP)])
-    pair = whole(pair_kernel, (shape((2, 2, nodes, quarter), BF16),), (), (p_quarter, other))[0]
-    others = lax.ppermute(pair, "rep", [(r, r ^ 2) for r in range(REP)])
+    p_all = [p_quarter] + [
+        lax.ppermute(p_quarter, "rep", [(r, (r + back) % REP) for r in range(REP)])
+        for back in range(1, REP)
+    ]
     grad_feat = whole(
-        feature_kernel, (shape((nodes, width), BF16),), (lane,), (pair, others, weight)
+        feature_kernel, (shape((nodes, width), BF16),), (lane,), (*p_all, weight)
     )[0]
     rows = hidden // (ZH * ZL * YL)
     grad_weight = whole(lines_kernel, (shape((rows, width), F32),), (), (gw,))[0]

time: 115 us -> 114 us (level)
  waiting for transfers between devices: 25.5 us -> 21 us
  starting transfers between devices: 61.8 us -> 64.9 us
    ppermute x2 -> x3, waiting for transfers between devices: 5.79 us -> 0.01 us  [shards(): lax.ppermute(p_quarter, 'rep', [(r, (r + back) % REP) for r in range(REP)])]
    ppermute x2 -> x3, starting transfers between devices: 4.87 us -> 8.49 us  [shards(): lax.ppermute(p_quarter, 'rep', [(r, (r + back) % REP) for r in range(REP)])]
    all_to_all x2, waiting for transfers between devices: 7.41 us -> 9.62 us  [exchange(): return lax.all_to_all(value, axes, 0, 0)]
  transfers between devices with their start and end apart: 14 -> 15, of which waited for: 9 -> 9; matrix products, arithmetic and copies ran while one was open for 0% -> 0% of each run, Pallas kernels for 6% -> 6%
where the time goes in v8:
time: 114 us; the launch traced here: 113 us
  starting transfers between devices  64.9 us (57%)
  waiting for transfers between devices  21 us (18%)
  blocking collectives  13.8 us (12%)
  Pallas kernels  11.8 us (10%)
    ppermute x7, starting transfers between devices, along_z(): lax.ppermute(value, ('zh', 'zl'), [(z, (z + shift) % count) for z in rang...  29.4 us
    all_to_all x1, blocking collectives, exchange(): return lax.all_to_all(value, axes, 0, 0)  13.8 us
    all_to_all x2, starting transfers between devices, exchange(): return lax.all_to_all(value, axes, 0, 0)  13.7 us
    ppermute x3, starting transfers between devices, turned_along_z(): return lax.ppermute(value, BLK, pairs)  13.4 us
    pallas_call x15, Pallas kernels, whole(): pl.pallas_call(kernel, in_specs=[pl.BlockSpec(memory_space=pltpu.SMEM)] *...  11.8 us
    ppermute x7, waiting for transfers between devices, along_z(): lax.ppermute(value, ('zh', 'zl'), [(z, (z + shift) % count) for z in rang...  9.87 us
    all_to_all x2, waiting for transfers between devices, exchange(): return lax.all_to_all(value, axes, 0, 0)  9.62 us
    ppermute x3, starting transfers between devices, shards(): lax.ppermute(p_quarter, 'rep', [(r, (r + back) % REP) for r in range(REP)])  8.49 us
  transfers between devices with their start and end apart: 15, of which 9 were waited for; matrix products, arithmetic and copies ran while one was open for 0% of the time, Pallas kernels for 6%

profile of v8, /device:TPU:24, one launch (start us, length us, event | category | flops | bytes accessed | tf_op | source)
XLA Modules:
  0.0 113.0 jit_solution(3149657537388134483)
XLA Ops:
  0.6 0.0 copy-start
  0.6 0.0 copy-start.8
  0.7 0.0 copy-start.1
  0.7 0.0 copy-start.3
  0.7 0.0 copy-start.2
  0.7 0.0 copy-start.7
  0.7 0.0 copy-start.6
  0.7 2.3 %shard_map.105 = bf16[256,512]{1,0:T(8,128)(2,1)} custom-call(s32[1]{0:T(128)} %bitcast.1.yl_ref, bf16[1,8,6,128,128]{4,3,2,1,0:T(8,128)(2,1)} %tiles_ref.5, s32[6,1,8]{2,1,0:T(1,128)} %bitcast.7, s32[6,1,8]{2,1,0:T(1,128)} %bitcast.11, s32[1,8]{1,0:T(1,128)} %count_ref.5, bf16[256,512]{1,0:T(8,128)(2,1)} %pre_ref.5, bf16[256,512]{1,0:T(8,128)(2,1)} %up_ref.5), custom_call_target="tpu_custom_call" | custom-call | tf_op jit(solution)/shard_map/pallas_call | solution.py:170
  3.0 3.8 %collective-permute-start = (bf16[256,512]{1,0:T(8,128)(2,1)}, bf16[256,512]{1,0:T(8,128)(2,1)S(1)}, u32[]{:S(2)}, u32[]{:S(2)}) collective-permute-start(bf16[256,512]{1,0:T(8,128)(2,1)} %shard_map.105), channel_id=1, source_target_pairs={{0,30},{1,3},{2,0},{3,5},{4,2},{5,7},{6,4},{7,9},{8,6},{9,11},{10,... | collective-permute-start | bytes 786440 | tf_op jit(solution)/shard_map/ppermute | solution.py:197
  6.9 0.0 copy-done.8
  6.9 0.0 copy-done.1
  6.9 0.0 copy-done.3
  6.9 0.0 copy-done.2
  6.9 0.0 copy-done.7
  6.9 0.0 copy-done.6
  6.9 1.9 %shard_map.104 = (bf16[256,512]{1,0:T(8,128)(2,1)S(1)}, bf16[256,512]{1,0:T(8,128)(2,1)S(1)}, f32[256,512]{1,0:T(8,128)S(1)}, f32[8,128]{1,0:T(8,128)}) custom-call(s32[1]{0:T(128)} %bitcast.1.yl_ref, s32[6,1,8]{2,1,0:T(1,128)S(1)} %bitcast.8, s32[6,1,8]{2,1,0:T(1,128)S(1)} %bitcast.12, s32[1,8]{1,0:T(1,128)S(1)} %copy-done.8, ...), custom_call_target="tpu_custom_call" | custom-call | tf_op jit(solution)/shard_map/pallas_call | solution.py:170
  8.9 3.7 %collective-permute-start.3 = (bf16[256,512]{1,0:T(8,128)(2,1)S(1)}, bf16[256,512]{1,0:T(8,128)(2,1)S(1)}, u32[]{:S(2)}, u32[]{:S(2)}) collective-permute-start(bf16[256,512]{1,0:T(8,128)(2,1)S(1)} %get-tuple-element.26), channel_id=1, source_target_pairs={{0,2},{2,4},{4,6},{6,8},{8,10},{10,12},{12,14},{14,16},{16,18},{18... | collective-permute-start | bytes 786440 | tf_op jit(solution)/shard_map/ppermute | solution.py:187
  12.6 7.7 %collective-permute-start.2 = (bf16[256,512]{1,0:T(8,128)(2,1)S(1)}, bf16[256,512]{1,0:T(8,128)(2,1)S(1)}, u32[]{:S(2)}, u32[]{:S(2)}) collective-permute-start(bf16[256,512]{1,0:T(8,128)(2,1)S(1)} %get-tuple-element.23), channel_id=1, source_target_pairs={{0,2},{1,31},{2,4},{3,1},{4,6},{5,3},{6,8},{7,5},{8,10},{9,7},{10,... | collective-permute-start | bytes 786440 | tf_op jit(solution)/shard_map/ppermute | solution.py:197
  20.3 1.5 %collective-permute-done.right_ref = bf16[256,512]{1,0:T(8,128)(2,1)S(1)} collective-permute-done((bf16[256,512]{1,0:T(8,128)(2,1)}, bf16[256,512]{1,0:T(8,128)(2,1)S(1)}, u32[]{:S(2)}, u32[]{:S(2)}) %collective-permute-start) | collective-permute-done | bytes 262176 | tf_op jit(solution)/shard_map/ppermute | solution.py:197
  21.8 1.9 %collective-permute-start.1 = (bf16[256,512]{1,0:T(8,128)(2,1)S(1)}, bf16[256,512]{1,0:T(8,128)(2,1)S(1)}, u32[]{:S(2)}, u32[]{:S(2)}) collective-permute-start(bf16[256,512]{1,0:T(8,128)(2,1)S(1)} %get-tuple-element.22), channel_id=1, source_target_pairs={{0,30},{1,3},{2,0},{3,5},{4,2},{5,7},{6,4},{7,9},{8,6},{9,11},{10,... | collective-permute-start | bytes 786440 | tf_op jit(solution)/shard_map/ppermute | solution.py:197
  23.8 1.3 %shard_map.107 = (f32[256,512]{1,0:T(8,128)S(1)}, bf16[256,512]{1,0:T(8,128)(2,1)S(1)}, f32[8,128]{1,0:T(8,128)S(1)}) custom-call(s32[1]{0:T(128)} %bitcast.1.yl_ref, s32[6,1,8]{2,1,0:T(1,128)S(1)} %bitcast.9, s32[6,1,8]{2,1,0:T(1,128)S(1)} %bitcast.13, s32[1,8]{1,0:T(1,128)S(1)} %copy-done.8, bf16[1,8,6,128,128]{4,3,2,1,0:T(8,128)(2,1)S(1)} %copy-done.1, ...), custom_call_target="tpu_custom_call" | custom-call | tf_op jit(solution)/shard_map/pallas_call | solution.py:170
  25.1 2.0 %collective-permute-done.3.right_ref = bf16[256,512]{1,0:T(8,128)(2,1)S(1)} collective-permute-done((bf16[256,512]{1,0:T(8,128)(2,1)S(1)}, bf16[256,512]{1,0:T(8,128)(2,1)S(1)}, u32[]{:S(2)}, u32[]{:S(2)}) %collective-permute-start.3) | collective-permute-done | bytes 262176 | tf_op jit(solution)/shard_map/ppermute | solution.py:187
  27.1 0.1 shard_map.110
  27.2 1.9 %collective-permute-start.4 = (bf16[256,512]{1,0:T(8,128)(2,1)S(1)}, bf16[256,512]{1,0:T(8,128)(2,1)S(1)}, u32[]{:S(2)}, u32[]{:S(2)}) collective-permute-start(bf16[256,512]{1,0:T(8,128)(2,1)S(1)} %shard_map.110), channel_id=1, source_target_pairs={{0,2},{2,4},{4,6},{6,8},{8,10},{10,12},{12,14},{14,16},{16,18},{18... | collective-permute-start | bytes 786440 | tf_op jit(solution)/shard_map/ppermute | solution.py:187
  29.1 5.1 %collective-permute-start.5 = (bf16[256,512]{1,0:T(8,128)(2,1)S(1)}, bf16[256,512]{1,0:T(8,128)(2,1)S(1)}, u32[]{:S(2)}, u32[]{:S(2)}) collective-permute-start(bf16[256,512]{1,0:T(8,128)(2,1)S(1)} %get-tuple-element.27), channel_id=1, source_target_pairs={{0,30},{2,0},{4,2},{6,4},{8,6},{10,8},{12,10},{14,12},{16,14},{18,... | collective-permute-start | bytes 786440 | tf_op jit(solution)/shard_map/ppermute | solution.py:187
  34.2 0.0 copy-start.4
  34.2 1.6 %shard_map.108 = (f32[256,512]{1,0:T(8,128)S(1)}, f32[256,512]{1,0:T(8,128)S(1)}, f32[8,128]{1,0:T(8,128)}) custom-call(s32[1]{0:T(128)} %bitcast.1.yl_ref, s32[6,1,8]{2,1,0:T(1,128)S(1)} %bitcast.10, s32[6,1,8]{2,1,0:T(1,128)S(1)} %bitcast.14, s32[1,8]{1,0:T(1,128)S(1)} %copy-done.8, bf16[1,8,6,128,128]{4,3,2,1,0:T(8,128)(2,1)S(1)} %copy-done.1, ...), custom_call_target="tpu_custom_call" | custom-call | tf_op jit(solution)/shard_map/pallas_call | solution.py:170
  35.8 0.0 collective-permute-done.2.second_ref
  35.8 0.0 collective-permute-done.1.first_ref
  35.8 0.1 shard_map.109.other_ref
  35.9 1.9 %collective-permute-done.4.first_ref = bf16[256,512]{1,0:T(8,128)(2,1)S(1)} collective-permute-done((bf16[256,512]{1,0:T(8,128)(2,1)S(1)}, bf16[256,512]{1,0:T(8,128)(2,1)S(1)}, u32[]{:S(2)}, u32[]{:S(2)}) %collective-permute-start.4) | collective-permute-done | bytes 262176 | tf_op jit(solution)/shard_map/ppermute | solution.py:187
  37.8 0.6 collective-permute-done.5.second_ref
  38.4 0.0 copy-done.4
  38.4 0.7 shard_map.111
  39.1 0.0 copy-start.5
  39.2 13.8 %all_to_all.15.in_ref = bf16[8,256,128]{2,1,0:T(8,128)(2,1)S(1)} all-to-all(bf16[8,256,128]{2,1,0:T(8,128)(2,1)S(1)} %shard_map.111), channel_id=1, replica_groups=mesh['dp'=4,'rep'=4,'zh'=4,'zl'=4,'yl'=2] {'rep','yl'}, dimensions={0} | all-to-all | bytes 1048576 | tf_op jit(solution)/shard_map/all_to_all | solution.py:182
  53.0 0.1 shard_map.112
  53.0 5.5 %collective-permute-start.6 = (bf16[256,128]{1,0:T(8,128)(2,1)S(1)}, bf16[256,128]{1,0:T(8,128)(2,1)S(1)}, u32[]{:S(2)}, u32[]{:S(2)}) collective-permute-start(bf16[256,128]{1,0:T(8,128)(2,1)S(1)} %get-tuple-element.29), channel_id=1, source_target_pairs={{0,24},{2,26},{4,28},{6,30},{8,0},{10,2},{12,4},{14,6},{16,8},{18,... | collective-permute-start | bytes 196616 | tf_op jit(solution)/shard_map/ppermute | solution.py:187
  58.5 4.3 %collective-permute-start.8 = (bf16[256,128]{1,0:T(8,128)(2,1)S(1)}, bf16[256,128]{1,0:T(8,128)(2,1)S(1)}, u32[]{:S(2)}, u32[]{:S(2)}) collective-permute-start(bf16[256,128]{1,0:T(8,128)(2,1)S(1)} %get-tuple-element.31), channel_id=1, source_target_pairs={{0,8},{2,10},{4,12},{6,14},{8,16},{10,18},{12,20},{14,22},{16,24},... | collective-permute-start | bytes 196616 | tf_op jit(solution)/shard_map/ppermute | solution.py:187
  62.8 0.4 collective-permute-done.6.right_ref
  63.2 4.2 %collective-permute-start.7 = (bf16[256,128]{1,0:T(8,128)(2,1)S(1)}, bf16[256,128]{1,0:T(8,128)(2,1)S(1)}, u32[]{:S(2)}, u32[]{:S(2)}) collective-permute-start(bf16[256,128]{1,0:T(8,128)(2,1)S(1)} %shard_map.113), channel_id=1, source_target_pairs={{0,28},{2,30},{4,0},{6,2},{8,4},{10,6},{12,8},{14,10},{16,12},{18,... | collective-permute-start | bytes 196616 | tf_op jit(solution)/shard_map/ppermute | solution.py:187
  67.4 1.2 %collective-permute-done.8.right_ref = bf16[256,128]{1,0:T(8,128)(2,1)S(1)} collective-permute-done((bf16[256,128]{1,0:T(8,128)(2,1)S(1)}, bf16[256,128]{1,0:T(8,128)(2,1)S(1)}, u32[]{:S(2)}, u32[]{:S(2)}) %collective-permute-start.8) | collective-permute-done | bytes 65568 | tf_op jit(solution)/shard_map/ppermute | solution.py:187
  68.6 4.6 %collective-permute-start.9 = (bf16[256,128]{1,0:T(8,128)(2,1)S(1)}, bf16[256,128]{1,0:T(8,128)(2,1)S(1)}, u32[]{:S(2)}, u32[]{:S(2)}) collective-permute-start(bf16[256,128]{1,0:T(8,128)(2,1)S(1)} %shard_map.114), channel_id=1, source_target_pairs={{0,4},{2,6},{4,8},{6,10},{8,12},{10,14},{12,16},{14,18},{16,20},{1... | collective-permute-start | bytes 196616 | tf_op jit(solution)/shard_map/ppermute | solution.py:187
  73.3 0.0 collective-permute-done.7.refs_0_
  73.3 3.7 %collective-permute-done.9.refs_1_ = bf16[256,128]{1,0:T(8,128)(2,1)S(1)} collective-permute-done((bf16[256,128]{1,0:T(8,128)(2,1)S(1)}, bf16[256,128]{1,0:T(8,128)(2,1)S(1)}, u32[]{:S(2)}, u32[]{:S(2)}) %collective-permute-start.9) | collective-permute-done | bytes 65568 | tf_op jit(solution)/shard_map/ppermute | solution.py:187
  77.0 0.0 copy-done.5
  77.0 1.0 shard_map.115
  78.0 10.4 %all-to-all-start.1 = ((bf16[32,16,128]{2,1,0:T(8,128)(2,1)}), bf16[32,16,128]{2,1,0:T(8,128)(2,1)S(1)}, u32[]{:S(2)}, u32[]{:S(2)}) async-start(bf16[32,16,128]{2,1,0:T(8,128)(2,1)} %bitcast.4), calls=%async_computation.1 | async-start | bytes 262144 | tf_op jit(solution)/shard_map/all_to_all | solution.py:182
  88.4 3.3 %collective-permute-start.12 = (bf16[2,256,128]{2,1,0:T(8,128)(2,1)S(1)}, bf16[2,256,128]{2,1,0:T(8,128)(2,1)S(1)}, u32[]{:S(2)}, u32[]{:S(2)}) collective-permute-start(bf16[2,256,128]{2,1,0:T(8,128)(2,1)S(1)} %get-tuple-element.32.refs_0_), channel_id=1, source_target_pairs={{0,96},{32,0},{64,32},{96,64},{1,97},{33,1},{65,33},{97,65},{2,98}... | collective-permute-start | bytes 393224 | tf_op jit(solution)/shard_map/ppermute | solution.py:283
  91.7 3.3 %collective-permute-start.11 = (bf16[2,256,128]{2,1,0:T(8,128)(2,1)S(1)}, bf16[2,256,128]{2,1,0:T(8,128)(2,1)S(1)}, u32[]{:S(2)}, u32[]{:S(2)}) collective-permute-start(bf16[2,256,128]{2,1,0:T(8,128)(2,1)S(1)} %get-tuple-element.32.refs_0_), channel_id=1, source_target_pairs={{0,64},{32,96},{64,0},{96,32},{1,65},{33,97},{65,1},{97,33},{2,66}... | collective-permute-start | bytes 393224 | tf_op jit(solution)/shard_map/ppermute | solution.py:283
  94.9 1.9 %collective-permute-start.10 = (bf16[2,256,128]{2,1,0:T(8,128)(2,1)S(1)}, bf16[2,256,128]{2,1,0:T(8,128)(2,1)S(1)}, u32[]{:S(2)}, u32[]{:S(2)}) collective-permute-start(bf16[2,256,128]{2,1,0:T(8,128)(2,1)S(1)} %get-tuple-element.32.refs_0_), channel_id=1, source_target_pairs={{0,32},{32,64},{64,96},{96,0},{1,33},{33,65},{65,97},{97,1},{2,34}... | collective-permute-start | bytes 393224 | tf_op jit(solution)/shard_map/ppermute | solution.py:283
  96.9 6.1 %all-to-all-done.1.in_ref = bf16[32,16,128]{2,1,0:T(8,128)(2,1)S(1)} async-done(((bf16[32,16,128]{2,1,0:T(8,128)(2,1)}), bf16[32,16,128]{2,1,0:T(8,128)(2,1)S(1)}, u32[]{:S(2)}, u32[]{:S(2)}) %all-to-all-start.1) | async-done | bytes 131104 | tf_op jit(solution)/shard_map/all_to_all | solution.py:182
  103.0 0.7 shard_map.117
  103.6 3.3 %all-to-all-start.2 = ((f32[4,16,128]{2,1,0:T(8,128)}), f32[4,16,128]{2,1,0:T(8,128)S(1)}, u32[]{:S(2)}, u32[]{:S(2)}) async-start(f32[4,16,128]{2,1,0:T(8,128)} %shard_map.117), calls=%async_computation.2 | async-start | bytes 65536 | tf_op jit(solution)/shard_map/all_to_all | solution.py:182
  106.9 0.0 copy-done
  106.9 0.5 convolution_convert_fusion.refs_4_
  107.4 0.0 collective-permute-done.12.refs_3_
  107.4 0.0 collective-permute-done.11.refs_2_
  107.4 0.0 collective-permute-done.10.refs_1_
  107.4 1.4 %shard_map.116 = bf16[256,512]{1,0:T(8,128)(2,1)} custom-call(s32[1]{0:T(128)} %bitcast.lane_ref, bf16[2,256,128]{2,1,0:T(8,128)(2,1)S(1)} %get-tuple-element.32.refs_0_, bf16[2,256,128]{2,1,0:T(8,128)(2,1)S(1)} %collective-permute-done.10.refs_1_, bf16[2,256,128]{2,1,0:T(8,128)(2,1)S(1)} %collective-permute-done.11.refs_2_, ...), custom_call_target="tpu_custom_call" | custom-call | tf_op jit(solution)/shard_map/pallas_call | solution.py:170
  108.8 3.5 %all-to-all-done.2.in_ref = f32[4,16,128]{2,1,0:T(8,128)S(1)} async-done(((f32[4,16,128]{2,1,0:T(8,128)}), f32[4,16,128]{2,1,0:T(8,128)S(1)}, u32[]{:S(2)}, u32[]{:S(2)}) %all-to-all-start.2) | async-done | bytes 32800 | tf_op jit(solution)/shard_map/all_to_all | solution.py:182
  112.3 0.6 shard_map.118
  (3 shorter events, 0.1 us)
Async XLA Ops:
  0.6 106.3 %copy-start = (bf16[512,512]{1,0:T(8,128)(2,1)S(1)}, bf16[512,512]{1,0:T(8,128)(2,1)}, u32[]{:S(2)}) copy-start(bf16[512,512]{1,0:T(8,128)(2,1)} %param.12) | copy-start | bytes 1572868
  0.6 6.2 %copy-start.8 = (s32[1,8]{1,0:T(1,128)S(1)}, s32[1,8]{1,0:T(1,128)}, u32[]{:S(2)}) copy-start(s32[1,8]{1,0:T(1,128)} %count_ref.5) | copy-start | bytes 100
  0.7 6.2 %copy-start.1 = (bf16[1,8,6,128,128]{4,3,2,1,0:T(8,128)(2,1)S(1)}, bf16[1,8,6,128,128]{4,3,2,1,0:T(8,128)(2,1)}, u32[]{:S(2)}) copy-start(bf16[1,8,6,128,128]{4,3,2,1,0:T(8,128)(2,1)} %tiles_ref.5) | copy-start | bytes 4718596
  0.7 6.2 %copy-start.3 = (bf16[256,512]{1,0:T(8,128)(2,1)S(1)}, bf16[256,512]{1,0:T(8,128)(2,1)}, u32[]{:S(2)}) copy-start(bf16[256,512]{1,0:T(8,128)(2,1)} %up_ref.5) | copy-start | bytes 786436
  0.7 6.2 %copy-start.2 = (bf16[256,512]{1,0:T(8,128)(2,1)S(1)}, bf16[256,512]{1,0:T(8,128)(2,1)}, u32[]{:S(2)}) copy-start(bf16[256,512]{1,0:T(8,128)(2,1)} %pre_ref.5) | copy-start | bytes 786436
  0.7 6.2 %copy-start.7 = (s32[1,8,6]{1,0,2:T(1,128)S(1)}, s32[1,8,6]{1,0,2:T(1,128)}, u32[]{:S(2)}) copy-start(s32[1,8,6]{1,0,2:T(1,128)} %param.15) | copy-start | bytes 580
  0.7 6.2 %copy-start.6 = (s32[1,8,6]{1,0,2:T(1,128)S(1)}, s32[1,8,6]{1,0,2:T(1,128)}, u32[]{:S(2)}) copy-start(s32[1,8,6]{1,0,2:T(1,128)} %param.14) | copy-start | bytes 580
  3.0 18.8 %collective-permute-start = (bf16[256,512]{1,0:T(8,128)(2,1)}, bf16[256,512]{1,0:T(8,128)(2,1)S(1)}, u32[]{:S(2)}, u32[]{:S(2)}) collective-permute-start(bf16[256,512]{1,0:T(8,128)(2,1)} %shard_map.105), channel_id=1, source_target_pairs={{0,30},{1,3},{2,0},{3,5},{4,2},{5,7},{6,4},{7,9},{8,6},{9,11},{10,... | collective-permute-start | bytes 786440 | tf_op jit(solution)/shard_map/ppermute | solution.py:197
  8.9 18.2 %collective-permute-start.3 = (bf16[256,512]{1,0:T(8,128)(2,1)S(1)}, bf16[256,512]{1,0:T(8,128)(2,1)S(1)}, u32[]{:S(2)}, u32[]{:S(2)}) collective-permute-start(bf16[256,512]{1,0:T(8,128)(2,1)S(1)} %get-tuple-element.26), channel_id=1, source_target_pairs={{0,2},{2,4},{4,6},{6,8},{8,10},{10,12},{12,14},{14,16},{16,18},{18... | collective-permute-start | bytes 786440 | tf_op jit(solution)/shard_map/ppermute | solution.py:187
  12.6 23.2 %collective-permute-start.2 = (bf16[256,512]{1,0:T(8,128)(2,1)S(1)}, bf16[256,512]{1,0:T(8,128)(2,1)S(1)}, u32[]{:S(2)}, u32[]{:S(2)}) collective-permute-start(bf16[256,512]{1,0:T(8,128)(2,1)S(1)} %get-tuple-element.23), channel_id=1, source_target_pairs={{0,2},{1,31},{2,4},{3,1},{4,6},{5,3},{6,8},{7,5},{8,10},{9,7},{10,... | collective-permute-start | bytes 786440 | tf_op jit(solution)/shard_map/ppermute | solution.py:197
  21.8 14.0 %collective-permute-start.1 = (bf16[256,512]{1,0:T(8,128)(2,1)S(1)}, bf16[256,512]{1,0:T(8,128)(2,1)S(1)}, u32[]{:S(2)}, u32[]{:S(2)}) collective-permute-start(bf16[256,512]{1,0:T(8,128)(2,1)S(1)} %get-tuple-element.22), channel_id=1, source_target_pairs={{0,30},{1,3},{2,0},{3,5},{4,2},{5,7},{6,4},{7,9},{8,6},{9,11},{10,... | collective-permute-start | bytes 786440 | tf_op jit(solution)/shard_map/ppermute | solution.py:197
  27.2 10.7 %collective-permute-start.4 = (bf16[256,512]{1,0:T(8,128)(2,1)S(1)}, bf16[256,512]{1,0:T(8,128)(2,1)S(1)}, u32[]{:S(2)}, u32[]{:S(2)}) collective-permute-start(bf16[256,512]{1,0:T(8,128)(2,1)S(1)} %shard_map.110), channel_id=1, source_target_pairs={{0,2},{2,4},{4,6},{6,8},{8,10},{10,12},{12,14},{14,16},{16,18},{18... | collective-permute-start | bytes 786440 | tf_op jit(solution)/shard_map/ppermute | solution.py:187
  29.1 9.3 %collective-permute-start.5 = (bf16[256,512]{1,0:T(8,128)(2,1)S(1)}, bf16[256,512]{1,0:T(8,128)(2,1)S(1)}, u32[]{:S(2)}, u32[]{:S(2)}) collective-permute-start(bf16[256,512]{1,0:T(8,128)(2,1)S(1)} %get-tuple-element.27), channel_id=1, source_target_pairs={{0,30},{2,0},{4,2},{6,4},{8,6},{10,8},{12,10},{14,12},{16,14},{18,... | collective-permute-start | bytes 786440 | tf_op jit(solution)/shard_map/ppermute | solution.py:187
  34.2 4.2 %copy-start.4 = (bf16[512,512]{1,0:T(8,128)(2,1)S(1)}, bf16[512,512]{1,0:T(8,128)(2,1)}, u32[]{:S(2)}) copy-start(bf16[512,512]{1,0:T(8,128)(2,1)} %constant.12.clone.spread_ref) | copy-start | bytes 1572868
  39.1 37.8 %copy-start.5 = (bf16[256,512]{1,0:T(8,128)(2,1)S(1)}, bf16[256,512]{1,0:T(8,128)(2,1)}, u32[]{:S(2)}) copy-start(bf16[256,512]{1,0:T(8,128)(2,1)} %refs_2_.1) | copy-start | bytes 786436
  53.0 10.2 %collective-permute-start.6 = (bf16[256,128]{1,0:T(8,128)(2,1)S(1)}, bf16[256,128]{1,0:T(8,128)(2,1)S(1)}, u32[]{:S(2)}, u32[]{:S(2)}) collective-permute-start(bf16[256,128]{1,0:T(8,128)(2,1)S(1)} %get-tuple-element.29), channel_id=1, source_target_pairs={{0,24},{2,26},{4,28},{6,30},{8,0},{10,2},{12,4},{14,6},{16,8},{18,... | collective-permute-start | bytes 196616 | tf_op jit(solution)/shard_map/ppermute | solution.py:187
  58.5 10.1 %collective-permute-start.8 = (bf16[256,128]{1,0:T(8,128)(2,1)S(1)}, bf16[256,128]{1,0:T(8,128)(2,1)S(1)}, u32[]{:S(2)}, u32[]{:S(2)}) collective-permute-start(bf16[256,128]{1,0:T(8,128)(2,1)S(1)} %get-tuple-element.31), channel_id=1, source_target_pairs={{0,8},{2,10},{4,12},{6,14},{8,16},{10,18},{12,20},{14,22},{16,24},... | collective-permute-start | bytes 196616 | tf_op jit(solution)/shard_map/ppermute | solution.py:187
  63.2 10.1 %collective-permute-start.7 = (bf16[256,128]{1,0:T(8,128)(2,1)S(1)}, bf16[256,128]{1,0:T(8,128)(2,1)S(1)}, u32[]{:S(2)}, u32[]{:S(2)}) collective-permute-start(bf16[256,128]{1,0:T(8,128)(2,1)S(1)} %shard_map.113), channel_id=1, source_target_pairs={{0,28},{2,30},{4,0},{6,2},{8,4},{10,6},{12,8},{14,10},{16,12},{18,... | collective-permute-start | bytes 196616 | tf_op jit(solution)/shard_map/ppermute | solution.py:187
  68.6 8.3 %collective-permute-start.9 = (bf16[256,128]{1,0:T(8,128)(2,1)S(1)}, bf16[256,128]{1,0:T(8,128)(2,1)S(1)}, u32[]{:S(2)}, u32[]{:S(2)}) collective-permute-start(bf16[256,128]{1,0:T(8,128)(2,1)S(1)} %shard_map.114), channel_id=1, source_target_pairs={{0,4},{2,6},{4,8},{6,10},{8,12},{10,14},{12,16},{14,18},{16,20},{1... | collective-permute-start | bytes 196616 | tf_op jit(solution)/shard_map/ppermute | solution.py:187
  78.0 25.0 %all-to-all-start.1 = ((bf16[32,16,128]{2,1,0:T(8,128)(2,1)}), bf16[32,16,128]{2,1,0:T(8,128)(2,1)S(1)}, u32[]{:S(2)}, u32[]{:S(2)}) async-start(bf16[32,16,128]{2,1,0:T(8,128)(2,1)} %bitcast.4), calls=%async_computation.1 | async-start | bytes 262144 | tf_op jit(solution)/shard_map/all_to_all | solution.py:182
  88.4 19.0 %collective-permute-start.12 = (bf16[2,256,128]{2,1,0:T(8,128)(2,1)S(1)}, bf16[2,256,128]{2,1,0:T(8,128)(2,1)S(1)}, u32[]{:S(2)}, u32[]{:S(2)}) collective-permute-start(bf16[2,256,128]{2,1,0:T(8,128)(2,1)S(1)} %get-tuple-element.32.refs_0_), channel_id=1, source_target_pairs={{0,96},{32,0},{64,32},{96,64},{1,97},{33,1},{65,33},{97,65},{2,98}... | collective-permute-start | bytes 393224 | tf_op jit(solution)/shard_map/ppermute | solution.py:283
  91.7 15.7 %collective-permute-start.11 = (bf16[2,256,128]{2,1,0:T(8,128)(2,1)S(1)}, bf16[2,256,128]{2,1,0:T(8,128)(2,1)S(1)}, u32[]{:S(2)}, u32[]{:S(2)}) collective-permute-start(bf16[2,256,128]{2,1,0:T(8,128)(2,1)S(1)} %get-tuple-element.32.refs_0_), channel_id=1, source_target_pairs={{0,64},{32,96},{64,0},{96,32},{1,65},{33,97},{65,1},{97,33},{2,66}... | collective-permute-start | bytes 393224 | tf_op jit(solution)/shard_map/ppermute | solution.py:283
  94.9 12.5 %collective-permute-start.10 = (bf16[2,256,128]{2,1,0:T(8,128)(2,1)S(1)}, bf16[2,256,128]{2,1,0:T(8,128)(2,1)S(1)}, u32[]{:S(2)}, u32[]{:S(2)}) collective-permute-start(bf16[2,256,128]{2,1,0:T(8,128)(2,1)S(1)} %get-tuple-element.32.refs_0_), channel_id=1, source_target_pairs={{0,32},{32,64},{64,96},{96,0},{1,33},{33,65},{65,97},{97,1},{2,34}... | collective-permute-start | bytes 393224 | tf_op jit(solution)/shard_map/ppermute | solution.py:283
  103.6 8.7 %all-to-all-start.2 = ((f32[4,16,128]{2,1,0:T(8,128)}), f32[4,16,128]{2,1,0:T(8,128)S(1)}, u32[]{:S(2)}, u32[]{:S(2)}) async-start(f32[4,16,128]{2,1,0:T(8,128)} %shard_map.117), calls=%async_computation.2 | async-start | bytes 65536 | tf_op jit(solution)/shard_map/all_to_all | solution.py:182

commit v9 on v8

--- a/solution.py
+++ b/solution.py
@@ -84,20 +84,25 @@
         )
 
 
-def gather_kernel(keep_ref, first_ref, second_ref, out_ref):
+def by_quarters(total, spread_ref):
+    low = total.astype(BF16)
+    quarter = low.shape[1] // REP
+    for q in range(REP):
+        span = slice(q * quarter, (q + 1) * quarter)
+        yield q, jnp.dot(low, spread_ref[:, span], preferred_element_type=F32).astype(BF16)
+
+
+def gather_kernel(keep_ref, first_ref, second_ref, spread_ref, out_ref):
     total = keep_ref[...] + first_ref[...].astype(F32) + second_ref[...].astype(F32)
-    out_ref[...] = total.astype(BF16)
+    for q, piece in by_quarters(total, spread_ref):
+        out_ref[q] = piece
 
 
 def near_kernel(yl_ref, other_ref, keep_ref, first_ref, second_ref, spread_ref, out_ref):
-    quarter = out_ref.shape[2]
     total = keep_ref[...] + first_ref[...].astype(F32) + second_ref[...].astype(F32)
-    for low, lane in ((total.astype(BF16), yl_ref[0]), (other_ref[...], 1 - yl_ref[0])):
-        for q in range(REP):
-            span = slice(q * quarter, (q + 1) * quarter)
-            out_ref[YL * q + lane] = jnp.dot(
-                low, spread_ref[:, span], preferred_element_type=F32
-            ).astype(BF16)
+    for q, piece in by_quarters(total, spread_ref):
+        out_ref[YL * q + yl_ref[0]] = piece
+        out_ref[YL * q + 1 - yl_ref[0]] = other_ref[q]
 
 
 def sides_kernel(in_ref, *out_refs):
@@ -249,11 +254,16 @@
     back_other = turned_along_z(back_other, -1)
     mid_same = along_z(mid_same, 1)
     back_same = along_z(back_same, -1)
-    other = whole(gather_kernel, (block,), (), (keep_other, mid_other, back_other))[0]
 
     spread = np.zeros((hidden, hidden), np.float32)
     spread[hidden_order(hidden), np.arange(hidden)] = 1.0
     spread = jnp.asarray(spread, BF16)
+    other = whole(
+        gather_kernel,
+        (shape((REP, nodes, quarter), BF16),),
+        (),
+        (keep_other, mid_other, back_other, spread),
+    )[0]
     weight = contract_rows(spread, weight).astype(BF16)
     parts = whole(
         near_kernel,

time: 114 us -> 113 us (level)
  transfers between devices with their start and end apart: 15 -> 15, of which waited for: 9 -> 9; matrix products, arithmetic and copies ran while one was open for 0% -> 0% of each run, Pallas kernels for 6% -> 7%
where the time goes in v9:
time: 113 us
  starting transfers between devices  65.1 us (58%)
  waiting for transfers between devices  20.7 us (18%)
  blocking collectives  13.8 us (12%)
  Pallas kernels  11.8 us (10%)
    ppermute x7, starting transfers between devices, along_z(): lax.ppermute(value, ('zh', 'zl'), [(z, (z + shift) % count) for z in rang...  29.6 us
    all_to_all x1, blocking collectives, exchange(): return lax.all_to_all(value, axes, 0, 0)  13.8 us
    all_to_all x2, starting transfers between devices, exchange(): return lax.all_to_all(value, axes, 0, 0)  13.7 us
    ppermute x3, starting transfers between devices, turned_along_z(): return lax.ppermute(value, BLK, pairs)  13.3 us
    pallas_call x15, Pallas kernels, whole(): pl.pallas_call(kernel, in_specs=[pl.BlockSpec(memory_space=pltpu.SMEM)] *...  11.8 us
    all_to_all x2, waiting for transfers between devices, exchange(): return lax.all_to_all(value, axes, 0, 0)  9.69 us
    ppermute x7, waiting for transfers between devices, along_z(): lax.ppermute(value, ('zh', 'zl'), [(z, (z + shift) % count) for z in rang...  9.42 us
    ppermute x3, starting transfers between devices, shards(): lax.ppermute(p_quarter, 'rep', [(r, (r + back) % REP) for r in range(REP)])  8.37 us
  transfers between devices with their start and end apart: 15, of which 9 were waited for; matrix products, arithmetic and copies ran while one was open for 0% of the time, Pallas kernels for 7%

profile of v9, /device:TPU:24, one launch (start us, length us, event | category | flops | bytes accessed | tf_op | source)
XLA Modules:
  0.0 112.8 jit_solution(11328079975060255763)
XLA Ops:
  0.6 0.0 copy-start
  0.6 0.0 copy-start.8
  0.7 0.0 copy-start.1
  0.7 0.0 copy-start.3
  0.7 0.0 copy-start.2
  0.7 0.0 copy-start.7
  0.7 0.0 copy-start.6
  0.7 2.3 %shard_map.105 = bf16[256,512]{1,0:T(8,128)(2,1)} custom-call(s32[1]{0:T(128)} %bitcast.1.yl_ref, bf16[1,8,6,128,128]{4,3,2,1,0:T(8,128)(2,1)} %tiles_ref.5, s32[6,1,8]{2,1,0:T(1,128)} %bitcast.7, s32[6,1,8]{2,1,0:T(1,128)} %bitcast.11, s32[1,8]{1,0:T(1,128)} %count_ref.5, bf16[256,512]{1,0:T(8,128)(2,1)} %pre_ref.5, bf16[256,512]{1,0:T(8,128)(2,1)} %up_ref.5), custom_call_target="tpu_custom_call" | custom-call | tf_op jit(solution)/shard_map/pallas_call | solution.py:175
  3.0 3.8 %collective-permute-start = (bf16[256,512]{1,0:T(8,128)(2,1)}, bf16[256,512]{1,0:T(8,128)(2,1)S(1)}, u32[]{:S(2)}, u32[]{:S(2)}) collective-permute-start(bf16[256,512]{1,0:T(8,128)(2,1)} %shard_map.105), channel_id=1, source_target_pairs={{0,30},{1,3},{2,0},{3,5},{4,2},{5,7},{6,4},{7,9},{8,6},{9,11},{10,... | collective-permute-start | bytes 786440 | tf_op jit(solution)/shard_map/ppermute | solution.py:202
  6.9 0.0 copy-done.8
  6.9 0.0 copy-done.1
  6.9 0.0 copy-done.3
  6.9 0.0 copy-done.2
  6.9 0.0 copy-done.7
  6.9 0.0 copy-done.6
  6.9 1.9 %shard_map.104 = (bf16[256,512]{1,0:T(8,128)(2,1)S(1)}, bf16[256,512]{1,0:T(8,128)(2,1)S(1)}, f32[256,512]{1,0:T(8,128)S(1)}, f32[8,128]{1,0:T(8,128)}) custom-call(s32[1]{0:T(128)} %bitcast.1.yl_ref, s32[6,1,8]{2,1,0:T(1,128)S(1)} %bitcast.8, s32[6,1,8]{2,1,0:T(1,128)S(1)} %bitcast.12, s32[1,8]{1,0:T(1,128)S(1)} %copy-done.8, ...), custom_call_target="tpu_custom_call" | custom-call | tf_op jit(solution)/shard_map/pallas_call | solution.py:175
  8.9 3.8 %collective-permute-start.3 = (bf16[256,512]{1,0:T(8,128)(2,1)S(1)}, bf16[256,512]{1,0:T(8,128)(2,1)S(1)}, u32[]{:S(2)}, u32[]{:S(2)}) collective-permute-start(bf16[256,512]{1,0:T(8,128)(2,1)S(1)} %get-tuple-element.26), channel_id=1, source_target_pairs={{0,2},{2,4},{4,6},{6,8},{8,10},{10,12},{12,14},{14,16},{16,18},{18... | collective-permute-start | bytes 786440 | tf_op jit(solution)/shard_map/ppermute | solution.py:192
  12.6 7.6 %collective-permute-start.2 = (bf16[256,512]{1,0:T(8,128)(2,1)S(1)}, bf16[256,512]{1,0:T(8,128)(2,1)S(1)}, u32[]{:S(2)}, u32[]{:S(2)}) collective-permute-start(bf16[256,512]{1,0:T(8,128)(2,1)S(1)} %get-tuple-element.23), channel_id=1, source_target_pairs={{0,2},{1,31},{2,4},{3,1},{4,6},{5,3},{6,8},{7,5},{8,10},{9,7},{10,... | collective-permute-start | bytes 786440 | tf_op jit(solution)/shard_map/ppermute | solution.py:202
  20.2 1.5 %collective-permute-done.right_ref = bf16[256,512]{1,0:T(8,128)(2,1)S(1)} collective-permute-done((bf16[256,512]{1,0:T(8,128)(2,1)}, bf16[256,512]{1,0:T(8,128)(2,1)S(1)}, u32[]{:S(2)}, u32[]{:S(2)}) %collective-permute-start) | collective-permute-done | bytes 262176 | tf_op jit(solution)/shard_map/ppermute | solution.py:202
  21.8 1.9 %collective-permute-start.1 = (bf16[256,512]{1,0:T(8,128)(2,1)S(1)}, bf16[256,512]{1,0:T(8,128)(2,1)S(1)}, u32[]{:S(2)}, u32[]{:S(2)}) collective-permute-start(bf16[256,512]{1,0:T(8,128)(2,1)S(1)} %get-tuple-element.22), channel_id=1, source_target_pairs={{0,30},{1,3},{2,0},{3,5},{4,2},{5,7},{6,4},{7,9},{8,6},{9,11},{10,... | collective-permute-start | bytes 786440 | tf_op jit(solution)/shard_map/ppermute | solution.py:202
  23.8 1.2 %shard_map.107 = (f32[256,512]{1,0:T(8,128)S(1)}, bf16[256,512]{1,0:T(8,128)(2,1)S(1)}, f32[8,128]{1,0:T(8,128)S(1)}) custom-call(s32[1]{0:T(128)} %bitcast.1.yl_ref, s32[6,1,8]{2,1,0:T(1,128)S(1)} %bitcast.9, s32[6,1,8]{2,1,0:T(1,128)S(1)} %bitcast.13, s32[1,8]{1,0:T(1,128)S(1)} %copy-done.8, bf16[1,8,6,128,128]{4,3,2,1,0:T(8,128)(2,1)S(1)} %copy-done.1, ...), custom_call_target="tpu_custom_call" | custom-call | tf_op jit(solution)/shard_map/pallas_call | solution.py:175
  25.0 2.1 %collective-permute-done.3.right_ref = bf16[256,512]{1,0:T(8,128)(2,1)S(1)} collective-permute-done((bf16[256,512]{1,0:T(8,128)(2,1)S(1)}, bf16[256,512]{1,0:T(8,128)(2,1)S(1)}, u32[]{:S(2)}, u32[]{:S(2)}) %collective-permute-start.3) | collective-permute-done | bytes 262176 | tf_op jit(solution)/shard_map/ppermute | solution.py:192
  27.1 0.0 copy-start.4
  27.1 2.1 %collective-permute-start.4 = (bf16[256,512]{1,0:T(8,128)(2,1)S(1)}, bf16[256,512]{1,0:T(8,128)(2,1)S(1)}, u32[]{:S(2)}, u32[]{:S(2)}) collective-permute-start(bf16[256,512]{1,0:T(8,128)(2,1)S(1)} %shard_map.110), channel_id=1, source_target_pairs={{0,2},{2,4},{4,6},{6,8},{8,10},{10,12},{12,14},{14,16},{16,18},{18... | collective-permute-start | bytes 786440 | tf_op jit(solution)/shard_map/ppermute | solution.py:192
  29.2 5.1 %collective-permute-start.5 = (bf16[256,512]{1,0:T(8,128)(2,1)S(1)}, bf16[256,512]{1,0:T(8,128)(2,1)S(1)}, u32[]{:S(2)}, u32[]{:S(2)}) collective-permute-start(bf16[256,512]{1,0:T(8,128)(2,1)S(1)} %get-tuple-element.27), channel_id=1, source_target_pairs={{0,30},{2,0},{4,2},{6,4},{8,6},{10,8},{12,10},{14,12},{16,14},{18,... | collective-permute-start | bytes 786440 | tf_op jit(solution)/shard_map/ppermute | solution.py:192
  34.3 1.6 %shard_map.108 = (f32[256,512]{1,0:T(8,128)S(1)}, f32[256,512]{1,0:T(8,128)S(1)}, f32[8,128]{1,0:T(8,128)}) custom-call(s32[1]{0:T(128)} %bitcast.1.yl_ref, s32[6,1,8]{2,1,0:T(1,128)S(1)} %bitcast.10, s32[6,1,8]{2,1,0:T(1,128)S(1)} %bitcast.14, s32[1,8]{1,0:T(1,128)S(1)} %copy-done.8, bf16[1,8,6,128,128]{4,3,2,1,0:T(8,128)(2,1)S(1)} %copy-done.1, ...), custom_call_target="tpu_custom_call" | custom-call | tf_op jit(solution)/shard_map/pallas_call | solution.py:175
  35.9 0.0 collective-permute-done.2.second_ref
  35.9 0.0 collective-permute-done.1.first_ref
  35.9 0.0 copy-done.4
  35.9 0.4 shard_map.109.other_ref
  36.4 1.4 %collective-permute-done.4.first_ref = bf16[256,512]{1,0:T(8,128)(2,1)S(1)} collective-permute-done((bf16[256,512]{1,0:T(8,128)(2,1)S(1)}, bf16[256,512]{1,0:T(8,128)(2,1)S(1)}, u32[]{:S(2)}, u32[]{:S(2)}) %collective-permute-start.4) | collective-permute-done | bytes 262176 | tf_op jit(solution)/shard_map/ppermute | solution.py:192
  37.8 0.7 collective-permute-done.5.second_ref
  38.5 0.4 shard_map.111
  38.9 0.0 copy-start.5
  39.0 13.8 %all_to_all.15.in_ref = bf16[8,256,128]{2,1,0:T(8,128)(2,1)S(1)} all-to-all(bf16[8,256,128]{2,1,0:T(8,128)(2,1)S(1)} %shard_map.111), channel_id=1, replica_groups=mesh['dp'=4,'rep'=4,'zh'=4,'zl'=4,'yl'=2] {'rep','yl'}, dimensions={0} | all-to-all | bytes 1048576 | tf_op jit(solution)/shard_map/all_to_all | solution.py:187
  52.8 0.1 shard_map.112
  52.8 5.5 %collective-permute-start.6 = (bf16[256,128]{1,0:T(8,128)(2,1)S(1)}, bf16[256,128]{1,0:T(8,128)(2,1)S(1)}, u32[]{:S(2)}, u32[]{:S(2)}) collective-permute-start(bf16[256,128]{1,0:T(8,128)(2,1)S(1)} %get-tuple-element.29), channel_id=1, source_target_pairs={{0,24},{2,26},{4,28},{6,30},{8,0},{10,2},{12,4},{14,6},{16,8},{18,... | collective-permute-start | bytes 196616 | tf_op jit(solution)/shard_map/ppermute | solution.py:192
  58.3 4.2 %collective-permute-start.8 = (bf16[256,128]{1,0:T(8,128)(2,1)S(1)}, bf16[256,128]{1,0:T(8,128)(2,1)S(1)}, u32[]{:S(2)}, u32[]{:S(2)}) collective-permute-start(bf16[256,128]{1,0:T(8,128)(2,1)S(1)} %get-tuple-element.31), channel_id=1, source_target_pairs={{0,8},{2,10},{4,12},{6,14},{8,16},{10,18},{12,20},{14,22},{16,24},... | collective-permute-start | bytes 196616 | tf_op jit(solution)/shard_map/ppermute | solution.py:192
  62.6 0.5 collective-permute-done.6.right_ref
  63.1 4.3 %collective-permute-start.7 = (bf16[256,128]{1,0:T(8,128)(2,1)S(1)}, bf16[256,128]{1,0:T(8,128)(2,1)S(1)}, u32[]{:S(2)}, u32[]{:S(2)}) collective-permute-start(bf16[256,128]{1,0:T(8,128)(2,1)S(1)} %shard_map.113), channel_id=1, source_target_pairs={{0,28},{2,30},{4,0},{6,2},{8,4},{10,6},{12,8},{14,10},{16,12},{18,... | collective-permute-start | bytes 196616 | tf_op jit(solution)/shard_map/ppermute | solution.py:192
  67.4 1.1 collective-permute-done.8.right_ref
  68.5 4.6 %collective-permute-start.9 = (bf16[256,128]{1,0:T(8,128)(2,1)S(1)}, bf16[256,128]{1,0:T(8,128)(2,1)S(1)}, u32[]{:S(2)}, u32[]{:S(2)}) collective-permute-start(bf16[256,128]{1,0:T(8,128)(2,1)S(1)} %shard_map.114), channel_id=1, source_target_pairs={{0,4},{2,6},{4,8},{6,10},{8,12},{10,14},{12,16},{14,18},{16,20},{1... | collective-permute-start | bytes 196616 | tf_op jit(solution)/shard_map/ppermute | solution.py:192
  73.1 0.0 collective-permute-done.7.refs_0_
  73.1 3.7 %collective-permute-done.9.refs_1_ = bf16[256,128]{1,0:T(8,128)(2,1)S(1)} collective-permute-done((bf16[256,128]{1,0:T(8,128)(2,1)S(1)}, bf16[256,128]{1,0:T(8,128)(2,1)S(1)}, u32[]{:S(2)}, u32[]{:S(2)}) %collective-permute-start.9) | collective-permute-done | bytes 65568 | tf_op jit(solution)/shard_map/ppermute | solution.py:192
  76.8 0.0 copy-done.5
  76.8 1.0 shard_map.115
  77.8 10.4 %all-to-all-start.1 = ((bf16[32,16,128]{2,1,0:T(8,128)(2,1)}), bf16[32,16,128]{2,1,0:T(8,128)(2,1)S(1)}, u32[]{:S(2)}, u32[]{:S(2)}) async-start(bf16[32,16,128]{2,1,0:T(8,128)(2,1)} %bitcast.4), calls=%async_computation.1 | async-start | bytes 262144 | tf_op jit(solution)/shard_map/all_to_all | solution.py:187
  88.3 3.1 %collective-permute-start.12 = (bf16[2,256,128]{2,1,0:T(8,128)(2,1)S(1)}, bf16[2,256,128]{2,1,0:T(8,128)(2,1)S(1)}, u32[]{:S(2)}, u32[]{:S(2)}) collective-permute-start(bf16[2,256,128]{2,1,0:T(8,128)(2,1)S(1)} %get-tuple-element.32.refs_0_), channel_id=1, source_target_pairs={{0,96},{32,0},{64,32},{96,64},{1,97},{33,1},{65,33},{97,65},{2,98}... | collective-permute-start | bytes 393224 | tf_op jit(solution)/shard_map/ppermute | solution.py:293
  91.4 3.3 %collective-permute-start.11 = (bf16[2,256,128]{2,1,0:T(8,128)(2,1)S(1)}, bf16[2,256,128]{2,1,0:T(8,128)(2,1)S(1)}, u32[]{:S(2)}, u32[]{:S(2)}) collective-permute-start(bf16[2,256,128]{2,1,0:T(8,128)(2,1)S(1)} %get-tuple-element.32.refs_0_), channel_id=1, source_target_pairs={{0,64},{32,96},{64,0},{96,32},{1,65},{33,97},{65,1},{97,33},{2,66}... | collective-permute-start | bytes 393224 | tf_op jit(solution)/shard_map/ppermute | solution.py:293
  94.7 1.9 %collective-permute-start.10 = (bf16[2,256,128]{2,1,0:T(8,128)(2,1)S(1)}, bf16[2,256,128]{2,1,0:T(8,128)(2,1)S(1)}, u32[]{:S(2)}, u32[]{:S(2)}) collective-permute-start(bf16[2,256,128]{2,1,0:T(8,128)(2,1)S(1)} %get-tuple-element.32.refs_0_), channel_id=1, source_target_pairs={{0,32},{32,64},{64,96},{96,0},{1,33},{33,65},{65,97},{97,1},{2,34}... | collective-permute-start | bytes 393224 | tf_op jit(solution)/shard_map/ppermute | solution.py:293
  96.7 6.2 %all-to-all-done.1.in_ref = bf16[32,16,128]{2,1,0:T(8,128)(2,1)S(1)} async-done(((bf16[32,16,128]{2,1,0:T(8,128)(2,1)}), bf16[32,16,128]{2,1,0:T(8,128)(2,1)S(1)}, u32[]{:S(2)}, u32[]{:S(2)}) %all-to-all-start.1) | async-done | bytes 131104 | tf_op jit(solution)/shard_map/all_to_all | solution.py:187
  102.8 0.7 shard_map.117
  103.5 3.3 %all-to-all-start.2 = ((f32[4,16,128]{2,1,0:T(8,128)}), f32[4,16,128]{2,1,0:T(8,128)S(1)}, u32[]{:S(2)}, u32[]{:S(2)}) async-start(f32[4,16,128]{2,1,0:T(8,128)} %shard_map.117), calls=%async_computation.2 | async-start | bytes 65536 | tf_op jit(solution)/shard_map/all_to_all | solution.py:187
  106.8 0.0 copy-done
  106.8 0.5 convolution_convert_fusion.refs_4_
  107.2 0.0 collective-permute-done.12.refs_3_
  107.3 0.0 collective-permute-done.11.refs_2_
  107.3 0.0 collective-permute-done.10.refs_1_
  107.3 1.4 %shard_map.116 = bf16[256,512]{1,0:T(8,128)(2,1)} custom-call(s32[1]{0:T(128)} %bitcast.lane_ref, bf16[2,256,128]{2,1,0:T(8,128)(2,1)S(1)} %get-tuple-element.32.refs_0_, bf16[2,256,128]{2,1,0:T(8,128)(2,1)S(1)} %collective-permute-done.10.refs_1_, bf16[2,256,128]{2,1,0:T(8,128)(2,1)S(1)} %collective-permute-done.11.refs_2_, ...), custom_call_target="tpu_custom_call" | custom-call | tf_op jit(solution)/shard_map/pallas_call | solution.py:175
  108.7 3.5 %all-to-all-done.2.in_ref = f32[4,16,128]{2,1,0:T(8,128)S(1)} async-done(((f32[4,16,128]{2,1,0:T(8,128)}), f32[4,16,128]{2,1,0:T(8,128)S(1)}, u32[]{:S(2)}, u32[]{:S(2)}) %all-to-all-start.2) | async-done | bytes 32800 | tf_op jit(solution)/shard_map/all_to_all | solution.py:187
  112.2 0.6 shard_map.118
  (4 shorter events, 0.1 us)
Async XLA Ops:
  0.6 106.1 %copy-start = (bf16[512,512]{1,0:T(8,128)(2,1)S(1)}, bf16[512,512]{1,0:T(8,128)(2,1)}, u32[]{:S(2)}) copy-start(bf16[512,512]{1,0:T(8,128)(2,1)} %param.12) | copy-start | bytes 1572868
  0.6 6.2 %copy-start.8 = (s32[1,8]{1,0:T(1,128)S(1)}, s32[1,8]{1,0:T(1,128)}, u32[]{:S(2)}) copy-start(s32[1,8]{1,0:T(1,128)} %count_ref.5) | copy-start | bytes 100
  0.7 6.2 %copy-start.1 = (bf16[1,8,6,128,128]{4,3,2,1,0:T(8,128)(2,1)S(1)}, bf16[1,8,6,128,128]{4,3,2,1,0:T(8,128)(2,1)}, u32[]{:S(2)}) copy-start(bf16[1,8,6,128,128]{4,3,2,1,0:T(8,128)(2,1)} %tiles_ref.5) | copy-start | bytes 4718596
  0.7 6.2 %copy-start.3 = (bf16[256,512]{1,0:T(8,128)(2,1)S(1)}, bf16[256,512]{1,0:T(8,128)(2,1)}, u32[]{:S(2)}) copy-start(bf16[256,512]{1,0:T(8,128)(2,1)} %up_ref.5) | copy-start | bytes 786436
  0.7 6.2 %copy-start.2 = (bf16[256,512]{1,0:T(8,128)(2,1)S(1)}, bf16[256,512]{1,0:T(8,128)(2,1)}, u32[]{:S(2)}) copy-start(bf16[256,512]{1,0:T(8,128)(2,1)} %pre_ref.5) | copy-start | bytes 786436
  0.7 6.2 %copy-start.7 = (s32[1,8,6]{1,0,2:T(1,128)S(1)}, s32[1,8,6]{1,0,2:T(1,128)}, u32[]{:S(2)}) copy-start(s32[1,8,6]{1,0,2:T(1,128)} %param.15) | copy-start | bytes 580
  0.7 6.2 %copy-start.6 = (s32[1,8,6]{1,0,2:T(1,128)S(1)}, s32[1,8,6]{1,0,2:T(1,128)}, u32[]{:S(2)}) copy-start(s32[1,8,6]{1,0,2:T(1,128)} %param.14) | copy-start | bytes 580
  3.0 18.7 %collective-permute-start = (bf16[256,512]{1,0:T(8,128)(2,1)}, bf16[256,512]{1,0:T(8,128)(2,1)S(1)}, u32[]{:S(2)}, u32[]{:S(2)}) collective-permute-start(bf16[256,512]{1,0:T(8,128)(2,1)} %shard_map.105), channel_id=1, source_target_pairs={{0,30},{1,3},{2,0},{3,5},{4,2},{5,7},{6,4},{7,9},{8,6},{9,11},{10,... | collective-permute-start | bytes 786440 | tf_op jit(solution)/shard_map/ppermute | solution.py:202
  8.9 18.2 %collective-permute-start.3 = (bf16[256,512]{1,0:T(8,128)(2,1)S(1)}, bf16[256,512]{1,0:T(8,128)(2,1)S(1)}, u32[]{:S(2)}, u32[]{:S(2)}) collective-permute-start(bf16[256,512]{1,0:T(8,128)(2,1)S(1)} %get-tuple-element.26), channel_id=1, source_target_pairs={{0,2},{2,4},{4,6},{6,8},{8,10},{10,12},{12,14},{14,16},{16,18},{18... | collective-permute-start | bytes 786440 | tf_op jit(solution)/shard_map/ppermute | solution.py:192
  12.6 23.3 %collective-permute-start.2 = (bf16[256,512]{1,0:T(8,128)(2,1)S(1)}, bf16[256,512]{1,0:T(8,128)(2,1)S(1)}, u32[]{:S(2)}, u32[]{:S(2)}) collective-permute-start(bf16[256,512]{1,0:T(8,128)(2,1)S(1)} %get-tuple-element.23), channel_id=1, source_target_pairs={{0,2},{1,31},{2,4},{3,1},{4,6},{5,3},{6,8},{7,5},{8,10},{9,7},{10,... | collective-permute-start | bytes 786440 | tf_op jit(solution)/shard_map/ppermute | solution.py:202
  21.8 14.1 %collective-permute-start.1 = (bf16[256,512]{1,0:T(8,128)(2,1)S(1)}, bf16[256,512]{1,0:T(8,128)(2,1)S(1)}, u32[]{:S(2)}, u32[]{:S(2)}) collective-permute-start(bf16[256,512]{1,0:T(8,128)(2,1)S(1)} %get-tuple-element.22), channel_id=1, source_target_pairs={{0,30},{1,3},{2,0},{3,5},{4,2},{5,7},{6,4},{7,9},{8,6},{9,11},{10,... | collective-permute-start | bytes 786440 | tf_op jit(solution)/shard_map/ppermute | solution.py:202
  27.1 8.8 %copy-start.4 = (bf16[512,512]{1,0:T(8,128)(2,1)S(1)}, bf16[512,512]{1,0:T(8,128)(2,1)}, u32[]{:S(2)}) copy-start(bf16[512,512]{1,0:T(8,128)(2,1)} %constant.12.clone.spread_ref) | copy-start | bytes 1572868
  27.1 10.6 %collective-permute-start.4 = (bf16[256,512]{1,0:T(8,128)(2,1)S(1)}, bf16[256,512]{1,0:T(8,128)(2,1)S(1)}, u32[]{:S(2)}, u32[]{:S(2)}) collective-permute-start(bf16[256,512]{1,0:T(8,128)(2,1)S(1)} %shard_map.110), channel_id=1, source_target_pairs={{0,2},{2,4},{4,6},{6,8},{8,10},{10,12},{12,14},{14,16},{16,18},{18... | collective-permute-start | bytes 786440 | tf_op jit(solution)/shard_map/ppermute | solution.py:192
  29.2 9.3 %collective-permute-start.5 = (bf16[256,512]{1,0:T(8,128)(2,1)S(1)}, bf16[256,512]{1,0:T(8,128)(2,1)S(1)}, u32[]{:S(2)}, u32[]{:S(2)}) collective-permute-start(bf16[256,512]{1,0:T(8,128)(2,1)S(1)} %get-tuple-element.27), channel_id=1, source_target_pairs={{0,30},{2,0},{4,2},{6,4},{8,6},{10,8},{12,10},{14,12},{16,14},{18,... | collective-permute-start | bytes 786440 | tf_op jit(solution)/shard_map/ppermute | solution.py:192
  38.9 37.9 %copy-start.5 = (bf16[256,512]{1,0:T(8,128)(2,1)S(1)}, bf16[256,512]{1,0:T(8,128)(2,1)}, u32[]{:S(2)}) copy-start(bf16[256,512]{1,0:T(8,128)(2,1)} %refs_2_.1) | copy-start | bytes 786436
  52.8 10.3 %collective-permute-start.6 = (bf16[256,128]{1,0:T(8,128)(2,1)S(1)}, bf16[256,128]{1,0:T(8,128)(2,1)S(1)}, u32[]{:S(2)}, u32[]{:S(2)}) collective-permute-start(bf16[256,128]{1,0:T(8,128)(2,1)S(1)} %get-tuple-element.29), channel_id=1, source_target_pairs={{0,24},{2,26},{4,28},{6,30},{8,0},{10,2},{12,4},{14,6},{16,8},{18,... | collective-permute-start | bytes 196616 | tf_op jit(solution)/shard_map/ppermute | solution.py:192
  58.3 10.1 %collective-permute-start.8 = (bf16[256,128]{1,0:T(8,128)(2,1)S(1)}, bf16[256,128]{1,0:T(8,128)(2,1)S(1)}, u32[]{:S(2)}, u32[]{:S(2)}) collective-permute-start(bf16[256,128]{1,0:T(8,128)(2,1)S(1)} %get-tuple-element.31), channel_id=1, source_target_pairs={{0,8},{2,10},{4,12},{6,14},{8,16},{10,18},{12,20},{14,22},{16,24},... | collective-permute-start | bytes 196616 | tf_op jit(solution)/shard_map/ppermute | solution.py:192
  63.1 10.0 %collective-permute-start.7 = (bf16[256,128]{1,0:T(8,128)(2,1)S(1)}, bf16[256,128]{1,0:T(8,128)(2,1)S(1)}, u32[]{:S(2)}, u32[]{:S(2)}) collective-permute-start(bf16[256,128]{1,0:T(8,128)(2,1)S(1)} %shard_map.113), channel_id=1, source_target_pairs={{0,28},{2,30},{4,0},{6,2},{8,4},{10,6},{12,8},{14,10},{16,12},{18,... | collective-permute-start | bytes 196616 | tf_op jit(solution)/shard_map/ppermute | solution.py:192
  68.5 8.3 %collective-permute-start.9 = (bf16[256,128]{1,0:T(8,128)(2,1)S(1)}, bf16[256,128]{1,0:T(8,128)(2,1)S(1)}, u32[]{:S(2)}, u32[]{:S(2)}) collective-permute-start(bf16[256,128]{1,0:T(8,128)(2,1)S(1)} %shard_map.114), channel_id=1, source_target_pairs={{0,4},{2,6},{4,8},{6,10},{8,12},{10,14},{12,16},{14,18},{16,20},{1... | collective-permute-start | bytes 196616 | tf_op jit(solution)/shard_map/ppermute | solution.py:192
  77.8 25.0 %all-to-all-start.1 = ((bf16[32,16,128]{2,1,0:T(8,128)(2,1)}), bf16[32,16,128]{2,1,0:T(8,128)(2,1)S(1)}, u32[]{:S(2)}, u32[]{:S(2)}) async-start(bf16[32,16,128]{2,1,0:T(8,128)(2,1)} %bitcast.4), calls=%async_computation.1 | async-start | bytes 262144 | tf_op jit(solution)/shard_map/all_to_all | solution.py:187
  88.3 19.0 %collective-permute-start.12 = (bf16[2,256,128]{2,1,0:T(8,128)(2,1)S(1)}, bf16[2,256,128]{2,1,0:T(8,128)(2,1)S(1)}, u32[]{:S(2)}, u32[]{:S(2)}) collective-permute-start(bf16[2,256,128]{2,1,0:T(8,128)(2,1)S(1)} %get-tuple-element.32.refs_0_), channel_id=1, source_target_pairs={{0,96},{32,0},{64,32},{96,64},{1,97},{33,1},{65,33},{97,65},{2,98}... | collective-permute-start | bytes 393224 | tf_op jit(solution)/shard_map/ppermute | solution.py:293
  91.4 15.9 %collective-permute-start.11 = (bf16[2,256,128]{2,1,0:T(8,128)(2,1)S(1)}, bf16[2,256,128]{2,1,0:T(8,128)(2,1)S(1)}, u32[]{:S(2)}, u32[]{:S(2)}) collective-permute-start(bf16[2,256,128]{2,1,0:T(8,128)(2,1)S(1)} %get-tuple-element.32.refs_0_), channel_id=1, source_target_pairs={{0,64},{32,96},{64,0},{96,32},{1,65},{33,97},{65,1},{97,33},{2,66}... | collective-permute-start | bytes 393224 | tf_op jit(solution)/shard_map/ppermute | solution.py:293
  94.7 12.5 %collective-permute-start.10 = (bf16[2,256,128]{2,1,0:T(8,128)(2,1)S(1)}, bf16[2,256,128]{2,1,0:T(8,128)(2,1)S(1)}, u32[]{:S(2)}, u32[]{:S(2)}) collective-permute-start(bf16[2,256,128]{2,1,0:T(8,128)(2,1)S(1)} %get-tuple-element.32.refs_0_), channel_id=1, source_target_pairs={{0,32},{32,64},{64,96},{96,0},{1,33},{33,65},{65,97},{97,1},{2,34}... | collective-permute-start | bytes 393224 | tf_op jit(solution)/shard_map/ppermute | solution.py:293
  103.5 8.7 %all-to-all-start.2 = ((f32[4,16,128]{2,1,0:T(8,128)}), f32[4,16,128]{2,1,0:T(8,128)S(1)}, u32[]{:S(2)}, u32[]{:S(2)}) async-start(f32[4,16,128]{2,1,0:T(8,128)} %shard_map.117), calls=%async_computation.2 | async-start | bytes 65536 | tf_op jit(solution)/shard_map/all_to_all | solution.py:187
